TPU v7x, 32 devices: a whole 2x2x4 slice. The times are simulated.
32 devices in a mesh: dp: 16 (over z, y, x), mp: 2 (over core).
Axes of the slice: x: 2, y: 2, z: 4, core: 2. Of those that a mesh axis runs over, the one named last changes fastest.
Arguments:
- items: int32 [2, 8, 1024], P(None, None, 'dp'), may hold values from 0 to 18815
- targets: int32 [2, 8, 1024], P(None, None, 'dp'), may hold values from 0 to 18815
- masks: int32 [2, 8, 1024], P(None, None, 'dp'), may hold values from 0 to 2, as said below
- plan: int32 [1, 1024], P(None, 'dp'), may hold values from 0 to 1023, as said below
- negatives: int32 [2, 2048], replicated, may hold values from 0 to 18815, as said below
- h_init: float32 [1024, 1000], P('dp', 'mp'), may hold values from -0.9 to 0.9
- emb: bfloat16 [18816, 1000], P('dp', 'mp'), may hold values from -6 to 6
- w_in: bfloat16 [1000, 3, 1000], P(None, None, 'mp'), may hold values from -0.1875 to 0.1875
- w_rec: bfloat16 [1000, 3, 1000], P(None, None, 'mp'), may hold values from -0.1875 to 0.1875
- b_in: float32 [3, 1000], P(None, 'mp'), may hold values from -4 to 7
- b_rec_n: float32 [1000], P('mp'), may hold values from -2.5 to 2.5
- out_table: bfloat16 [18816, 1000], P('dp', 'mp'), may hold values from -0.59765625 to 0.59765625
- out_bias: float32 [18816], P('dp'), may hold values from -3 to 3
Outputs:
- loss: float32 [], replicated
- rms_inputs: float32 [], replicated
- rms_hidden: float32 [], replicated
- rms_scores: float32 [], replicated
- final_state: float32 [1024, 1000], P('dp', 'mp')
- grad_init: float32 [1024, 1000], P('dp', 'mp')
- grad_emb: float32 [18816, 1000], P('dp', 'mp')
- grad_w_in: float32 [1000, 3, 1000], P(None, None, 'mp')
- grad_w_rec: float32 [1000, 3, 1000], P(None, None, 'mp')
- grad_b_in: float32 [3, 1000], P(None, 'mp')
- grad_b_rec_n: float32 [1000], P('mp')
- grad_out_table: float32 [18816, 1000], P('dp', 'mp')
- grad_out_bias: float32 [18816], P('dp')
Inputs may be any that keep to these rules, and one draw needn't show every extreme that they name: `masks`: code 2 marks a session's first event, 1 an event continuing the slot's state, 0 an empty step; the last slot is never empty, and slots with higher numbers are empty less often. Each row plan[b] is a bijection of the 1024 slots. Slot k of every device goes to the device a common offset ahead (offsets of slots k and k + 16 agree), and into a local slot given by one permutation of the 64 local slots that all devices share, so one device hands at most 4 slots to any one device, and exactly 4 to some. The offsets 1 and 8 are always among those used. `negatives`: the ids of one row are distinct.
All inputs are finite; a program needn't handle non-finite values.
Results may differ from a plain program's by a relative error of at most 0.017.
Values may be sent and summed in bfloat16 or wider, within the bound.
No kernel may reach another device: no remote copies, remote signals or barrier semaphores. Data moves between devices by JAX's collectives and lax.ppermute only.
A program may use at most 320 MiB of HBM per device.

v0:
```python
import math

import jax
import jax.numpy as jnp
from jax import lax
from jax.sharding import PartitionSpec as P

REGULAR = 1.0
NEGATIVE_FLOOR = -1e30


def bpr_rows(scores, wanted, chosen, usable):
    session_events = scores.shape[0]
    allowed = usable[None, :] & (chosen[None, :] != wanted[:, None])
    positive = jnp.diagonal(scores[:, :session_events])
    top_score = jnp.max(jnp.where(allowed, scores, NEGATIVE_FLOOR), axis=1, keepdims=True)
    weights = jnp.exp(jnp.where(allowed, scores - top_score, NEGATIVE_FLOOR))
    normal = jnp.sum(weights, axis=1, keepdims=True)
    joined = scores + jax.nn.log_sigmoid(positive[:, None] - scores)
    top_joined = jnp.max(jnp.where(allowed, joined, NEGATIVE_FLOOR), axis=1, keepdims=True)
    joined_sum = jnp.sum(
        jnp.exp(jnp.where(allowed, joined - top_joined, NEGATIVE_FLOOR)), axis=1, keepdims=True
    )
    ranking = top_score + jnp.log(normal) - top_joined - jnp.log(joined_sum)
    penalty = jnp.sum(weights / normal * scores * scores, axis=1)
    return ranking[:, 0] + REGULAR * penalty


def gru_cell(gates_in, recurrent, prior, bias_cand, active_sessions):
    update = jax.nn.sigmoid(gates_in[:, 0] + recurrent[:, 0])
    reset = jax.nn.sigmoid(gates_in[:, 1] + recurrent[:, 1])
    candidate = jnp.tanh(gates_in[:, 2] + reset * (recurrent[:, 2] + bias_cand))
    return active_sessions * ((1.0 - update) * candidate + update * prior)


def block_rows(total, row_count):
    return math.gcd(total, 2 ** max(8, 22 - row_count.bit_length()))


def lookup_rows(index, table, row_count):
    total = index.shape[0]
    size = block_rows(total, row_count)

    def one_block(index_block):
        indicator = index_block[:, None] == jnp.arange(row_count, dtype=jnp.int32)[None, :]
        return jnp.dot(indicator.astype(jnp.bfloat16), table, preferred_element_type=jnp.float32)

    picked = lax.map(one_block, index.reshape(total // size, size))
    return picked.reshape(total, table.shape[1])


def sum_rows(index, values, row_count):
    total = index.shape[0]
    breadth = values.shape[1]
    size = block_rows(total, row_count)

    def add_block(accum, pair):
        index_block, value_block = pair
        indicator = index_block[:, None] == jnp.arange(row_count, dtype=jnp.int32)[None, :]
        term = lax.dot_general(
            indicator.astype(jnp.bfloat16),
            value_block,
            (((0,), (0,)), ((), ())),
            preferred_element_type=jnp.float32,
        )
        return (accum + term, None)

    accum, _ = lax.scan(
        add_block,
        jnp.zeros((row_count, breadth), jnp.float32),
        (index.reshape(total // size, size), values.reshape(total // size, size, breadth)),
    )
    return accum


def spread(own_low):
    return lax.all_gather(own_low, "mp", axis=1, tiled=True)


def move_state(state, destination, devices, slots):
    capacity = (slots + devices - 1) // devices
    target_device = destination // slots
    target_slot = destination % slots
    order = jnp.arange(slots)
    earlier = (target_device[:, None] == target_device[None, :]) & (order[:, None] > order[None, :])
    position = target_device * capacity + jnp.sum(earlier.astype(jnp.int32), axis=1)
    outgoing = jnp.zeros((devices * capacity, state.shape[1]), jnp.float32).at[position].set(state)
    labels = jnp.full((devices * capacity,), slots, jnp.int32).at[position].set(target_slot)
    arrived, arrived_labels = (
        lax.all_to_all(
            outgoing.astype(jnp.bfloat16), "dp", split_axis=0, concat_axis=0, tiled=True
        ).astype(outgoing.dtype),
        lax.all_to_all(labels, "dp", split_axis=0, concat_axis=0, tiled=True),
    )
    moved = jnp.zeros_like(state).at[arrived_labels].set(arrived, mode="drop")
    return (moved, arrived_labels, position)


def return_state(grad_start, labels, position, slots):
    inside = labels < slots
    spot = jnp.where(inside, labels, 0)
    returning = jnp.where(inside[:, None], jnp.take(grad_start, spot, axis=0), 0.0)
    back = lax.all_to_all(
        returning.astype(jnp.bfloat16), "dp", split_axis=0, concat_axis=0, tiled=True
    ).astype(returning.dtype)
    return jnp.take(back, position, axis=0)


def shards(
    items,
    targets,
    masks,
    plan,
    negatives,
    h_init,
    emb,
    w_in,
    w_rec,
    b_in,
    b_rec_n,
    out_table,
    out_bias,
):
    blocks, steps, slots = items.shape
    halfwidth = h_init.shape[1]
    breadth = w_in.shape[0]
    vocab_rows = emb.shape[0]
    devices = lax.axis_size("dp")
    negs = negatives.shape[1]
    session_events = steps * slots
    columns = session_events + negs
    token_ids = blocks * session_events
    item_ids = items.reshape(token_ids)
    cand_ids = jnp.concatenate([targets.reshape(blocks, session_events), negatives], axis=1)
    flat_cands = cand_ids.reshape(blocks * columns)
    alive_flags = (masks > 0).astype(jnp.float32)
    w_in_flat = w_in.reshape(breadth, 3 * halfwidth)
    w_rec_flat = w_rec.reshape(breadth, 3 * halfwidth)
    cand_rows = jnp.zeros((blocks * columns, halfwidth), jnp.bfloat16)
    cand_bias = jnp.zeros((blocks * columns,), jnp.float32)
    emb_piece = lax.all_gather(emb, "dp", axis=0, tiled=True)
    out_piece = lax.all_gather(out_table, "dp", axis=0, tiled=True)
    bias_piece = lax.all_gather(out_bias.astype(jnp.bfloat16), "dp", axis=0, tiled=True).astype(
        jnp.float32
    )
    row_count = emb_piece.shape[0]
    embedded = lookup_rows(item_ids, emb_piece, row_count)
    shifted = flat_cands
    inside = (shifted >= 0) & (shifted < row_count)
    take_position = jnp.clip(shifted, 0, row_count - 1)
    cand_rows = jnp.where(inside[:, None], jnp.take(out_piece, take_position, axis=0), cand_rows)
    cand_bias = jnp.where(inside, jnp.take(bias_piece, take_position), cand_bias)
    embedded, cand_rows, cand_bias = (embedded, cand_rows, cand_bias)
    inputs_full, cand_full = (
        lax.all_gather(embedded.astype(jnp.bfloat16), "mp", axis=1, tiled=True),
        lax.all_gather(cand_rows, "mp", axis=1, tiled=True),
    )
    preacts = jnp.dot(inputs_full, w_in_flat, preferred_element_type=jnp.float32)
    preacts = preacts.reshape(blocks, steps, slots, 3, halfwidth) + b_in

    def advance(carry_pair, step_inputs):
        prior, prior_low = carry_pair
        gates_in, codes = step_inputs
        keeping = (codes == 1).astype(jnp.float32)[:, None]
        active_sessions = (codes > 0).astype(jnp.float32)[:, None]
        entering = prior_low * keeping.astype(jnp.bfloat16)
        recurrent = jnp.dot(entering, w_rec_flat, preferred_element_type=jnp.float32).reshape(
            slots, 3, halfwidth
        )
        fresh = gru_cell(gates_in, recurrent, prior * keeping, b_rec_n, active_sessions)
        fresh_own = fresh.astype(jnp.bfloat16)
        fresh_low = spread(fresh_own)
        return ((fresh, fresh_low), (prior, prior_low, recurrent, fresh_low, fresh_own))

    state = h_init
    state_low = spread(h_init.astype(jnp.bfloat16))
    records = []
    routes = []
    for event_block in range(blocks):
        (state, state_low), record = lax.scan(
            advance, (state, state_low), (preacts[event_block], masks[event_block])
        )
        records.append(record)
        if event_block + 1 < blocks:
            state, labels, position = move_state(state, plan[event_block], devices, slots)
            routes.append((labels, position))
            state_low = spread(state.astype(jnp.bfloat16))
    loss_total_sum = jnp.zeros((), jnp.float32)
    score_squared = jnp.zeros((), jnp.float32)
    hidden_squared = jnp.zeros((), jnp.float32)
    score_list = []
    for event_block in range(blocks):
        outputs = records[event_block][3].reshape(session_events, breadth)
        candidates = cand_full[event_block * columns : (event_block + 1) * columns]
        scores = lax.dot_general(
            outputs, candidates, (((1,), (1,)), ((), ())), preferred_element_type=jnp.float32
        )
        scores = scores + cand_bias[event_block * columns : (event_block + 1) * columns]
        active_sessions = alive_flags[event_block].reshape(session_events)
        usable = jnp.concatenate([active_sessions > 0, jnp.ones((negs,), dtype=bool)])
        losses = bpr_rows(
            scores, targets[event_block].reshape(session_events), cand_ids[event_block], usable
        )
        loss_total_sum = loss_total_sum + jnp.sum(active_sessions * losses)
        score_squared = score_squared + jnp.sum(active_sessions * jnp.sum(scores * scores, axis=1))
        output_values = outputs.astype(jnp.float32)
        hidden_squared = hidden_squared + jnp.sum(
            active_sessions[:, None] * output_values * output_values
        )
        score_list.append(scores)
    input_entries = inputs_full.astype(jnp.float32)
    input_squared = jnp.sum(alive_flags.reshape(token_ids)[:, None] * input_entries * input_entries)
    count_all, loss_all, input_all, hidden_all, score_all = lax.psum(
        (jnp.sum(alive_flags), loss_total_sum, input_squared, hidden_squared, score_squared), "dp"
    )
    loss = loss_all / count_all
    rms_inputs = jnp.sqrt(input_all / (count_all * breadth))
    rms_hidden = jnp.sqrt(hidden_all / (count_all * breadth))
    rms_scores = jnp.sqrt(score_all / (count_all * columns))
    from_scores = []
    row_grads = []
    bias_grads = []
    for event_block in range(blocks):
        active_sessions = alive_flags[event_block].reshape(session_events)
        usable = jnp.concatenate([active_sessions > 0, jnp.ones((negs,), dtype=bool)])
        wanted = targets[event_block].reshape(session_events)
        chosen = cand_ids[event_block]

        def block_loss(scores_arg):
            return jnp.sum(active_sessions * bpr_rows(scores_arg, wanted, chosen, usable))

        _, pullback = jax.vjp(block_loss, score_list[event_block])
        (grad_scores,) = pullback(jnp.ones((), jnp.float32) / count_all)
        bias_grads.append(jnp.sum(grad_scores, axis=0))
        scores_low = grad_scores.astype(jnp.bfloat16)
        own_rows = cand_rows[event_block * columns : (event_block + 1) * columns]
        to_outputs = jnp.dot(scores_low, own_rows, preferred_element_type=jnp.float32)
        from_scores.append(to_outputs.reshape(steps, slots, halfwidth))
        own_outputs = records[event_block][4].reshape(session_events, halfwidth)
        row_grads.append(
            lax.dot_general(
                scores_low,
                own_outputs,
                (((0,), (0,)), ((), ())),
                preferred_element_type=jnp.float32,
            )
        )
    cand_row_grads = jnp.concatenate(row_grads, axis=0)
    cand_bias_grads = jnp.concatenate(bias_grads, axis=0)

    def retreat(carry_triple, saved):
        grad_state, grad_rec_w, grad_bias_cand = carry_triple
        prior, prior_low, recurrent, gates_in, codes, from_output = saved
        grad_state = grad_state + from_output
        keeping = (codes == 1).astype(jnp.float32)[:, None]
        active_sessions = (codes > 0).astype(jnp.float32)[:, None]
        _, cell_pull = jax.vjp(
            lambda gate_arg, rec_arg, prior_arg, bias_arg: gru_cell(
                gate_arg, rec_arg, prior_arg, bias_arg, active_sessions
            ),
            gates_in,
            recurrent,
            prior * keeping,
            b_rec_n,
        )
        grad_gates, grad_rec, grad_prior, grad_bias = cell_pull(grad_state)
        rec_low = grad_rec.reshape(slots, 3 * halfwidth).astype(jnp.bfloat16)
        partial_sum = lax.dot_general(
            rec_low, w_rec_flat, (((1,), (1,)), ((), ())), preferred_element_type=jnp.float32
        )
        through_rec = lax.psum_scatter(
            partial_sum.astype(jnp.bfloat16), "mp", scatter_dimension=1, tiled=True
        ).astype(jnp.float32)
        entering = prior_low * keeping.astype(jnp.bfloat16)
        grad_rec_w = grad_rec_w + lax.dot_general(
            entering, rec_low, (((0,), (0,)), ((), ())), preferred_element_type=jnp.float32
        )
        previous = keeping * (grad_prior + through_rec)
        return ((previous, grad_rec_w, grad_bias_cand + grad_bias), grad_gates)

    grad_state = jnp.zeros((slots, halfwidth), jnp.float32)
    grad_rec_w = jnp.zeros((breadth, 3 * halfwidth), jnp.float32)
    grad_bias_cand = jnp.zeros((halfwidth,), jnp.float32)
    pre_grads = [None] * blocks
    for event_block in reversed(range(blocks)):
        prior_all, prior_low_all, recurrent_all, _, _ = records[event_block]
        (grad_state, grad_rec_w, grad_bias_cand), grad_pre = lax.scan(
            retreat,
            (grad_state, grad_rec_w, grad_bias_cand),
            (
                prior_all,
                prior_low_all,
                recurrent_all,
                preacts[event_block],
                masks[event_block],
                from_scores[event_block],
            ),
            reverse=True,
        )
        pre_grads[event_block] = grad_pre
        if event_block > 0:
            grad_state = return_state(
                grad_state, routes[event_block - 1][0], routes[event_block - 1][1], slots
            )
    pre_all = jnp.stack(pre_grads)
    grad_bias_in = jnp.sum(pre_all, axis=(0, 1, 2))
    pre_low = pre_all.reshape(token_ids, 3 * halfwidth).astype(jnp.bfloat16)
    grad_w_in = lax.dot_general(
        inputs_full, pre_low, (((0,), (0,)), ((), ())), preferred_element_type=jnp.float32
    )
    input_part = lax.dot_general(
        pre_low, w_in_flat, (((1,), (1,)), ((), ())), preferred_element_type=jnp.float32
    )
    grad_inputs = lax.psum_scatter(
        input_part.astype(jnp.bfloat16), "mp", scatter_dimension=1, tiled=True
    )
    bias_term = jnp.zeros((vocab_rows * devices,), jnp.float32).at[flat_cands].add(cand_bias_grads)
    weight_count = breadth * 3 * halfwidth
    packed_grads = jnp.concatenate(
        [
            grad_w_in.reshape(weight_count),
            grad_rec_w.reshape(weight_count),
            grad_bias_in.reshape(3 * halfwidth),
            grad_bias_cand,
        ]
    )
    packed_length = packed_grads.shape[0]
    padded_length = -(-packed_length // devices) * devices
    packed_grads = jnp.pad(packed_grads, (0, padded_length - packed_length))
    own_share, grad_out_bias = (
        lax.psum_scatter(packed_grads, "dp", scatter_dimension=0, tiled=True),
        lax.psum_scatter(bias_term, "dp", scatter_dimension=0, tiled=True),
    )
    summed_all = lax.all_gather(own_share.astype(jnp.bfloat16), "dp", axis=0, tiled=True).astype(
        own_share.dtype
    )
    summed_w_in = summed_all[:weight_count]
    summed_w_rec = summed_all[weight_count : 2 * weight_count]
    summed_b_in = summed_all[2 * weight_count : 2 * weight_count + 3 * halfwidth].reshape(
        3, halfwidth
    )
    summed_b_cand = summed_all[2 * weight_count + 3 * halfwidth : 2 * weight_count + 4 * halfwidth]
    shifted = flat_cands
    inside = (shifted >= 0) & (shifted < lax.axis_size("dp") * vocab_rows)
    position = jnp.where(inside, shifted, lax.axis_size("dp") * vocab_rows)
    both = lax.psum_scatter(
        jnp.concatenate(
            [
                sum_rows(item_ids, grad_inputs, lax.axis_size("dp") * vocab_rows),
                jnp.zeros((lax.axis_size("dp") * vocab_rows, halfwidth), jnp.float32)
                .at[position]
                .add(cand_row_grads, mode="drop"),
            ],
            axis=1,
        ),
        "dp",
        scatter_dimension=0,
        tiled=True,
    )
    grad_emb = both[:, :halfwidth]
    grad_out_table = both[:, halfwidth:]
    return (
        loss,
        rms_inputs,
        rms_hidden,
        rms_scores,
        state,
        grad_state,
        grad_emb,
        summed_w_in.reshape(breadth, 3, halfwidth),
        summed_w_rec.reshape(breadth, 3, halfwidth),
        summed_b_in,
        summed_b_cand,
        grad_out_table,
        grad_out_bias,
    )


def solution(mesh):
    return jax.shard_map(
        shards,
        mesh=mesh,
        in_specs=(
            P(None, None, "dp"),
            P(None, None, "dp"),
            P(None, None, "dp"),
            P(None, "dp"),
            P(),
            P("dp", "mp"),
            P("dp", "mp"),
            P(None, None, "mp"),
            P(None, None, "mp"),
            P(None, "mp"),
            P("mp"),
            P("dp", "mp"),
            P("dp"),
        ),
        out_specs=(
            P(),
            P(),
            P(),
            P(),
            P("dp", "mp"),
            P("dp", "mp"),
            P("dp", "mp"),
            P(None, None, "mp"),
            P(None, None, "mp"),
            P(None, "mp"),
            P("mp"),
            P("dp", "mp"),
            P("dp"),
        ),
        check_vma=False,
    )
```

profile of v0, /device:TPU:1, one launch (start us, length us, event | category | flops | bytes accessed | tf_op | source)
XLA Modules:
  0.0 4678.8 jit_solution(15017027040682932980)
XLA Ops:
  22.0 36.2 psum.36
  96.4 60.2 %all-reduce.12 = bf16[18816]{0:T(1024)(128)(2,1)S(1)} all-reduce(bf16[18816]{0:T(1024)(128)(2,1)S(1)} %dynamic-update-slice), channel_id=1, replica_groups=mesh['dp'=16,'mp'=2] {'dp'}, use_global_device_ids=true, to_apply=%add.12 | all-reduce | flops 18816 | bytes 75264
  162.7 28.7 gather_fusion.1
  199.6 30.5 all-gather.15.cloned.1.call-done
  230.1 52.2 %while.106 = (s32[]{:T(128)}, bf16[4,256,500]{1,2,0:T(8,128)(2,1)}, s32[4,256]{1,0:T(4,128)S(1)}, bf16[18816,500]{1,0:T(8,128)(2,1)}, s32[]{:T(128)}) while((s32[]{:T(128)}, bf16[4,256,500]{1,2,0:T(8,128)(2,1)}, s32[4,256]{1,0:T(4,128)S(1)}, bf16[18816,500]{1,0:T(8,128)(2,1)}, s32[]{:T(128)}) %tuple.284), condition=%wide.region_1.2_spmd, body=%wide.region_0.1_spmd.sunk | while | flops 4821712896 | bytes 19786828 | solution.py:48
  286.9 159.7 %all-gather.17.cloned.1.call-done = bf16[18816,500]{1,0:T(8,128)(2,1)} async-done(((bf16[1176,500]{1,0:T(8,128)(2,1)}), bf16[18816,500]{1,0:T(8,128)(2,1)}) %all-gather.17.cloned.1.call-update) | async-done | bytes 18816016 | tf_op jit(solution)/shard_map/all_gather | solution.py:142
  446.6 31.1 gather_fusion
  524.4 165.6 %while.107 = (s32[]{:T(128)}, f32[64,500]{1,0:T(8,128)}, bf16[64,1000]{1,0:T(8,128)(2,1)}, f32[8,64,500]{2,1,0:T(8,128)}, bf16[8,64,1000]{2,1,0:T(8,128)(2,1)}, ...) while((s32[]{:T(128)}, f32[64,500]{1,0:T(8,128)}, ...), condition=%wide.region_3.4_spmd, body=%wide.region_2.3_spmd.sunk | while | flops 192672320 | bytes 10283313 | solution.py:180
  715.5 165.2 %while.108 = (s32[]{:T(128)}, f32[64,500]{1,0:T(8,128)}, bf16[64,1000]{1,0:T(8,128)(2,1)}, f32[8,64,500]{2,1,0:T(8,128)}, bf16[8,64,1000]{2,1,0:T(8,128)(2,1)}, ...) while((s32[]{:T(128)}, f32[64,500]{1,0:T(8,128)}, ...), condition=%wide.region_15.16_spmd, body=%wide.region_14.15_spmd.sunk | while | flops 192672320 | bytes 10283313 | solution.py:180
  946.0 68.6 %scatter_fusion = f32[512,512]{1,0:T(8,128)} fusion(f32[512,512]{1,0:T(8,128)} %transpose_jvp_jit_diagonal___.4.clone, s32[512]{0:T(512)S(1)} %bitcast.470, f32[512]{0:T(512)S(1)} %neg.175), kind=kCustom, calls=%fused_computation.11 | custom fusion | flops 512 | bytes 10240 | tf_op jit(solution)/shard_map/transpose(jvp(jit(diagonal)))/cond/branch_0_fun/scatter-add | solution.py:15
  1035.3 241.1 %while.110 = (s32[]{:T(128)}, f32[64,500]{1,0:T(8,128)}, f32[1000,1500]{1,0:T(8,128)}, f32[500]{0:T(512)S(1)}, f32[8,64,3,500]{3,1,2,0:T(8,128)}, /*index=5*/s32...) while((s32[]{:T(128)}, f32[64,500]{1,0:T(8,128)}, ...), condition=%wide.region_47.50_spmd.clone, body=%wide.region_44.49_spmd.clone.sunk | while | flops 389208800 | bytes 27350500 | solution.py:287
  1328.8 68.5 %scatter_fusion.1 = f32[512,512]{1,0:T(8,128)} fusion(f32[512,512]{1,0:T(8,128)} %transpose_jvp_jit_diagonal___.4.clone.1, s32[512]{0:T(512)S(1)} %bitcast.471, f32[512]{0:T(512)S(1)} %neg.181), kind=kCustom, calls=%fused_computation.12 | custom fusion | flops 512 | bytes 10240 | tf_op jit(solution)/shard_map/transpose(jvp(jit(diagonal)))/cond/branch_0_fun/scatter-add | solution.py:15
  1457.5 46.5 scatter_custom_fusion.5
  1504.0 27.9 scatter_custom_fusion.6
  1535.5 251.0 %while.109 = (s32[]{:T(128)}, f32[64,500]{1,0:T(8,128)}, f32[1000,1500]{1,0:T(8,128)}, f32[500]{0:T(512)S(1)}, f32[8,64,3,500]{3,1,2,0:T(8,128)}, /*index=5*/s32...) while((s32[]{:T(128)}, f32[64,500]{1,0:T(8,128)}, ...), condition=%wide.region_60.64_spmd, body=%wide.region_57.63_spmd.sunk | while | flops 387676352 | bytes 27350480 | solution.py:287
  1834.9 97.3 %concatenate.37 = f32[3002000]{0:T(1024)} concatenate(f32[1500000]{0:T(1024)} %reshape.859, f32[1500000]{0:T(1024)} %reshape.860, f32[1500]{0:T(1024)S(1)} %reduce_sum.452, f32[500]{0:T(512)S(1)} %get-tuple-element.755), dimensions={0} | concatenate | bytes 24016000 | tf_op jit(solution)/shard_map/concatenate | solution.py:319
  1938.6 520.4 %all-reduce.40 = (bf16[3002000]{0:T(1024)(128)(2,1)}, f32[]{:T(128)}, f32[]{:T(128)}, f32[]{:T(128)}, f32[]{:T(128)}) all-reduce(f32[3002000]{0:T(1024)} %concatenate.37, f32[]{:T(128)S(6)} %add.631, f32[]{:T(128)} %fusion.147, f32[]{:T(128)S(6)} %add.632, f32[]{:T(128)S(6)} %add.633), channel_id=6, replica_groups=mesh['dp'=16,'mp'=2] {'dp'}, use_global_device_ids=true, to_apply=%region_68.72.clone | all-reduce | flops 3002004 | bytes 18012032
  2472.6 102.0 %while.111 = (s32[]{:T(128)}, f32[18816,500]{0,1:T(8,128)}, s32[4,256]{1,0:T(4,128)}, bf16[4,256,500]{2,1,0:T(8,128)(2,1)S(1)}, s32[]{:T(128)}, /*index=5*/s32[]{:T(128)}) while((s32[]{:T(128)}, f32[18816,500]{0,1:T(8,128)}, s32[4,256]{1,0:T(4,128)}, bf16[4,256,500]{2,1,0:T(8,128)(2,1)S(1)}, s32[]{:T(128)}, ...), condition=%wide.region_63.67_spmd.clone, body=%wide.region_62.66_spmd.clone.sunk | while | flops 4840528896 | bytes 75529312 | solution.py:68
  2488.7 28.7 select_add_fusion.10
  2518.1 28.0 select_add_fusion.10
  2546.7 27.9 select_add_fusion.10
  2574.7 38.5 copy.173
  2613.1 52.7 %pad_maximum_fusion = f32[18816,1000]{1,0:T(8,128)} fusion(f32[18816,500]{1,0:T(8,128)} %scatter_custom_fusion.5, f32[18816,500]{1,0:T(8,128)} %copy.173), kind=kLoop, calls=%fused_computation.201 | loop fusion | flops 18816000 | bytes 150528000 | tf_op jit(solution)/shard_map/concatenate | solution.py:347
  2718.4 1941.9 %all-reduce.35.cloned.1.call-done = (f32[18816,1000]{1,0:T(8,128)}, f32[18816]{0:T(1024)}) async-done(((f32[18816,1000]{1,0:T(8,128)}, f32[18816]{0:T(1024)}), (f32[18816,1000]{1,0:T(8,128)}, f32[18816]{0:T(1024)})) %all-reduce.35.cloned.1.call-update) | async-done | bytes 75339280
  (978 shorter events, 1340.9 us)
Async XLA Ops:
  7.2 222.9 %all-gather.15.cloned.1.call-start = ((), (), s32[]{:S(2)}) async-start(), calls=%async_computation.3 | async-start | bytes 20471808 | tf_op jit(solution)/shard_map/all_gather | solution.py:141
  8.8 437.8 %all-gather.17.cloned.1.call-start = ((), (), s32[]{:S(2)}) async-start(), calls=%async_computation.4 | async-start | bytes 20471808 | tf_op jit(solution)/shard_map/all_gather | solution.py:142
  14.5 182.5 %all-to-all-start = ((s32[16,4,1]{1,2,0:T(1,128)}), s32[16,4,1]{1,2,0:T(1,128)S(1)}, u32[]{:S(2)}, u32[]{:S(2)}) async-start(s32[16,4,1]{1,2,0:T(1,128)} %bitcast.70), calls=%async_computation | async-start | bytes 16384 | tf_op jit(solution)/shard_map/all_to_all | solution.py:93
  22.0 478.2 %all-gather.19.cloned.1.call-start = ((), (), s32[]{:S(2)}) async-start(), calls=%async_computation.6 | async-start | bytes 3096576 | tf_op jit(solution)/shard_map/all_gather | solution.py:155
  286.9 593.8 %all-gather.21.cloned.1.call-start = ((), (), s32[]{:S(2)}) async-start(), calls=%async_computation.7 | async-start | bytes 15482880 | tf_op jit(solution)/shard_map/all_gather | solution.py:156
  1061.8 28.9 all-reduce.39.cloned.1.call-start
  1092.4 28.9 all-reduce.39.cloned.1.call-start
  1123.1 28.9 all-reduce.39.cloned.1.call-start
  1153.7 28.9 all-reduce.39.cloned.1.call-start
  1184.4 28.9 all-reduce.39.cloned.1.call-start
  1215.0 28.9 all-reduce.39.cloned.1.call-start
  1245.7 28.9 all-reduce.39.cloned.1.call-start
  1278.8 253.1 %all-to-all-start.2 = ((bf16[16,4,500]{2,1,0:T(4,128)(2,1)}), bf16[16,4,500]{2,1,0:T(4,128)(2,1)S(1)}, u32[]{:S(2)}, u32[]{:S(2)}) async-start(bf16[16,4,500]{2,1,0:T(4,128)(2,1)} %all_to_all.28), calls=%async_computation.2 | async-start | bytes 131072 | tf_op jit(solution)/shard_map/all_to_all | solution.py:103
  1535.5 30.0 all-reduce.37.cloned.1.call-start
  1567.3 29.6 all-reduce.37.cloned.1.call-start
  1598.6 29.6 all-reduce.37.cloned.1.call-start
  1629.9 29.6 all-reduce.37.cloned.1.call-start
  1661.3 29.6 all-reduce.37.cloned.1.call-start
  1692.6 29.6 all-reduce.37.cloned.1.call-start
  1723.9 29.6 all-reduce.37.cloned.1.call-start
  1755.2 29.6 all-reduce.37.cloned.1.call-start
  1786.5 884.7 %all-reduce.33.cloned.1.call-start = ((), (), s32[]{:S(2)}) async-start(), calls=%async_computation.5 | async-start | bytes 12009472
  1937.3 532.6 %collective-permute-start = (bf16[1024,4]{0,1:T(4,128)(2,1)S(1)}, bf16[1024,4]{0,1:T(4,128)(2,1)S(1)}, u32[]{:S(2)}, u32[]{:S(2)}) collective-permute-start(bf16[1024,4]{0,1:T(4,128)(2,1)S(1)} %slice.331), channel_id=1, source_target_pairs={{0,1},{2,3},{4,5},{6,7},{8,9},{10,11},{12,13},{14,15},{16,17},{18,... | collective-permute-start | bytes 24584
  2469.9 2190.4 %all-reduce.35.cloned.1.call-start = ((), (), s32[]{:S(2)}) async-start(), calls=%async_computation.8 | async-start | bytes 154296320
  (135 other events, 1900.4 us)
Sparse Core Ops, SparseCore 0:
  10.8 219.2 all-gather.14
  232.9 213.6 all-gather.16
  448.8 9.4 all-gather.18
  500.3 21.6 all-gather.20
  1045.1 14.9 all-reduce.38
  1071.6 19.0 all-reduce.38
  1102.2 19.0 all-reduce.38
  1132.9 19.0 all-reduce.38
  1163.5 19.0 all-reduce.38
  1194.2 19.0 all-reduce.38
  1224.8 19.0 all-reduce.38
  1255.5 19.0 all-reduce.38
  1546.0 19.5 all-reduce.36
  1577.7 19.0 all-reduce.36
  1609.1 19.0 all-reduce.36
  1640.4 19.0 all-reduce.36
  1671.7 19.0 all-reduce.36
  1703.0 19.0 all-reduce.36
  1734.3 19.0 all-reduce.36
  1765.6 19.0 all-reduce.36
  2470.0 201.1 all-reduce.32
  2677.6 1982.5 all-reduce.34
where the time goes:
time: 4710 us; the launch traced here: 4680 us
  waiting for transfers between devices  2280 us (48%)
  local copies, waits for them, and re-layouts  746 us (16%)
  blocking collectives  666 us (14%)
  other arithmetic  550 us (12%)
  matrix products  370 us (8%)
    unnamed x9, waiting for transfers between devices  1940 us
    unnamed x3, blocking collectives  586 us
    all_gather x1, waiting for transfers between devices, shards(): out_piece = lax.all_gather(out_table, 'dp', axis=0, tiled=True)  160 us
    while x32, waiting for transfers between devices  145 us
    scatter-add x2, other arithmetic, bpr_rows(): positive = jnp.diagonal(scores[:, :session_events])  137 us
    dynamic_update_slice x64, local copies, waits for them, and re-layouts, shards(): lax.scan(advance, (state, state_low), (preacts[event_block], masks[event_...  106 us
    dot_general x16, matrix products, retreat(): lax.dot_general(entering, rec_low, (((0,), (0,)), ((), ())), preferred_el...  105 us
    dot_general x4, matrix products, add_block(): lax.dot_general(indicator.astype(jnp.bfloat16), value_block, (((0,), (0,)...  99.3 us
  transfers between devices with their start and end apart: 26, of which 21 were waited for; matrix products, arithmetic and copies ran while one was open for 25% of the time, Pallas kernels for 0%

commit v1 on v0

--- a/solution.py
+++ b/solution.py
@@ -1,12 +1,16 @@
+import functools
 import math
 
 import jax
 import jax.numpy as jnp
 from jax import lax
+from jax.experimental import pallas as pl
+from jax.experimental.pallas import tpu as pltpu
 from jax.sharding import PartitionSpec as P
 
 REGULAR = 1.0
 NEGATIVE_FLOOR = -1e30
+VMEM_LIMIT = 56 * 1024 * 1024
 
 
 def bpr_rows(scores, wanted, chosen, usable):
@@ -106,7 +110,7 @@
     return jnp.take(back, position, axis=0)
 
 
-def shards(
+def general(
     items,
     targets,
     masks,
@@ -376,6 +380,759 @@
     )
 
 
+def roundup(value, unit):
+    return -(-value // unit) * unit
+
+
+def bf16_parts(values):
+    first = lax.reduce_precision(values, 8, 7)
+    second = lax.reduce_precision(values - first, 8, 7)
+    third = lax.reduce_precision(values - first - second, 8, 7)
+    return first, second, third
+
+
+def one_hot(index, size):
+    return (index[:, None] == jnp.arange(size, dtype=index.dtype)[None, :]).astype(jnp.bfloat16)
+
+
+def dot_f32(left, right):
+    return jnp.dot(left, right, preferred_element_type=jnp.float32)
+
+
+def dot_first(left, right):
+    return lax.dot_general(
+        left, right, (((0,), (0,)), ((), ())), preferred_element_type=jnp.float32
+    )
+
+
+def dot_last(left, right):
+    return lax.dot_general(
+        left, right, (((1,), (1,)), ((), ())), preferred_element_type=jnp.float32
+    )
+
+
+def swap_cores(values):
+    return lax.ppermute(values, "mp", [(0, 1), (1, 0)])
+
+
+def exchange(values):
+    return lax.all_to_all(values, "dp", split_axis=0, concat_axis=0, tiled=True)
+
+
+def plan_requests(ids, devices, rows, capacity):
+    owner = ids // rows
+    owners = one_hot(owner, devices)
+    local = one_hot(ids % rows, rows)
+    wanted = dot_first(owners, local) > 0.5
+    order = jnp.arange(rows)
+    before = (order[:, None] < order[None, :]).astype(jnp.bfloat16)
+    position = dot_f32(wanted.astype(jnp.bfloat16), before)
+    longest = jnp.max(jnp.sum(wanted.astype(jnp.float32), axis=1))
+    spots = jnp.sum(
+        owners.astype(jnp.float32) * dot_last(local, position.astype(jnp.bfloat16)), axis=1
+    )
+    slot = owner * capacity + spots.astype(jnp.int32)
+    keyed = jnp.where(wanted, position, -1.0)
+    match = keyed[:, None, :] == jnp.arange(capacity, dtype=jnp.float32)[None, :, None]
+    listed = jnp.sum(jnp.where(match, order.astype(jnp.float32) + 1.0, 0.0), axis=2) - 1.0
+    return listed.astype(jnp.int32), slot, longest
+
+
+def plan_negatives(negatives, devices, rows, capacity, device):
+    blocks, negs = negatives.shape
+    chunk = math.gcd(negs, 128)
+    owner = negatives // rows
+    counts = jnp.sum(
+        (owner[:, None, :] == jnp.arange(devices)[None, :, None]).astype(jnp.float32), axis=2
+    )
+    mine = (owner == device).astype(jnp.float32)
+    grouped = mine.reshape(blocks * (negs // chunk), chunk)
+    order = jnp.arange(chunk)
+    before = (order[:, None] < order[None, :]).astype(jnp.bfloat16)
+    inner = dot_f32(grouped.astype(jnp.bfloat16), before).reshape(blocks, negs // chunk, chunk)
+    totals = jnp.sum(grouped, axis=1).reshape(blocks, negs // chunk)
+    group = jnp.arange(negs // chunk)
+    outer = jnp.sum(
+        jnp.where(group[None, :, None] > group[None, None, :], totals[:, None, :], 0.0), axis=2
+    )
+    position = (inner + outer[:, :, None]).reshape(blocks, negs)
+    keyed = jnp.where(mine > 0.5, position, -1.0)
+    match = keyed[:, None, :] == jnp.arange(capacity, dtype=jnp.float32)[None, :, None]
+    local = (negatives % rows).astype(jnp.float32) + 1.0
+    listed = jnp.sum(jnp.where(match, local[:, None, :], 0.0), axis=2) - 1.0
+    return listed.astype(jnp.int32), jnp.max(counts)
+
+
+def widen(code, width):
+    return jnp.concatenate([code] * (width // code.shape[1]), axis=1)
+
+
+def forward_kernel(half, mp_ref, own_ref, oth_ref, code_ref, start_ref, wi_own, wi_oth, wr_own,
+                   wr_oth, out_ref, ent_ref, upd_ref, rst_ref, cand_ref, rec_ref, pri_ref, end_ref,
+                   sq_ref, wi, wr, pre, state, sems):
+    me = mp_ref[0]
+    other = 1 - me
+    copies = [
+        pltpu.make_async_copy(wi_own, wi.at[me], sems.at[0]),
+        pltpu.make_async_copy(wi_oth, wi.at[other], sems.at[1]),
+        pltpu.make_async_copy(wr_own, wr.at[me], sems.at[2]),
+        pltpu.make_async_copy(wr_oth, wr.at[other], sems.at[3]),
+    ]
+    for copy in copies:
+        copy.start()
+    steps, slots, _ = code_ref.shape
+    width = own_ref.shape[1]
+    lane = lax.broadcasted_iota(jnp.int32, (slots, width), 1)
+    real = lane < half
+    ones = (lane >= half) & (lane < half + 3)
+    own = own_ref[...]
+    oth = oth_ref[...]
+    state[...] = start_ref[...]
+    copies[0].wait()
+    copies[1].wait()
+    for side in range(2):
+        for gate in range(3):
+            value = dot_f32(own, wi[side, gate, me]) + dot_f32(oth, wi[side, gate, other])
+            pre[side, gate] = value.reshape(steps, slots, width)
+    copies[2].wait()
+    copies[3].wait()
+
+    def step(t, sums):
+        in_sum, out_sum = sums
+        code = code_ref[t]
+        keep = widen((code == 1.0).astype(jnp.float32), width)
+        live = widen((code > 0.0).astype(jnp.float32), width)
+        rows = pl.ds(pl.multiple_of(t * slots, slots), slots)
+        for ref in (own_ref, oth_ref):
+            entry = jnp.where(real, ref[rows, :].astype(jnp.float32), 0.0)
+            in_sum = in_sum + live * entry * entry
+        entering = []
+        for side in range(2):
+            value = keep * state[side].astype(jnp.bfloat16).astype(jnp.float32)
+            if side == 0:
+                value = jnp.where(ones, 1.0, value)
+            value = value.astype(jnp.bfloat16)
+            ent_ref[side, t] = value
+            entering.append(value)
+        for side in range(2):
+            recurrent = [
+                dot_f32(entering[0], wr[side, gate, 0]) + dot_f32(entering[1], wr[side, gate, 1])
+                for gate in range(3)
+            ]
+            update = jax.nn.sigmoid(pre[side, 0, t] + recurrent[0])
+            reset = jax.nn.sigmoid(pre[side, 1, t] + recurrent[1])
+            candidate = jnp.tanh(pre[side, 2, t] + reset * recurrent[2])
+            prior = keep * state[side]
+            fresh = live * ((1.0 - update) * candidate + update * prior)
+            fresh = jnp.where(real, fresh, 0.0)
+            upd_ref[side, t] = update
+            rst_ref[side, t] = reset
+            cand_ref[side, t] = candidate
+            rec_ref[side, t] = recurrent[2]
+            pri_ref[side, t] = prior
+            state[side] = fresh
+            low = fresh.astype(jnp.bfloat16)
+            out_sum = out_sum + low.astype(jnp.float32) * low.astype(jnp.float32)
+            if side == 0:
+                low = jnp.where(ones, 1.0, low.astype(jnp.float32)).astype(jnp.bfloat16)
+            out_ref[side, t] = low
+        return in_sum, out_sum
+
+    zero = jnp.zeros((slots, width), jnp.float32)
+    in_sum, out_sum = lax.fori_loop(0, steps, step, (zero, zero))
+    end_ref[...] = state[...]
+    sq_ref[0] = in_sum
+    sq_ref[1] = out_sum
+
+
+def run_forward(half, block, me, own, oth, codes, start, weights):
+    _, blocks, events, width = own.shape
+    _, steps, slots, lanes = codes.shape
+    f32, low = jnp.float32, jnp.bfloat16
+    whole = lambda shape: pl.BlockSpec(shape, lambda i, s: (0,) * len(shape))
+    saved = (2, steps, slots, width)
+    hidden = (2, slots, width)
+    return pl.pallas_call(
+        functools.partial(forward_kernel, half),
+        grid_spec=pltpu.PrefetchScalarGridSpec(
+            num_scalar_prefetch=1,
+            grid=(1,),
+            in_specs=[
+                pl.BlockSpec((None, None, events, width), lambda i, s: (s[0], block, 0, 0)),
+                pl.BlockSpec((None, None, events, width), lambda i, s: (s[0], block, 0, 0)),
+                pl.BlockSpec((None, steps, slots, lanes), lambda i, s: (block, 0, 0, 0)),
+                whole(hidden),
+            ]
+            + [pl.BlockSpec(memory_space=pl.ANY)] * 4,
+            out_specs=[whole(saved)] * 7 + [whole(hidden)] * 2,
+            scratch_shapes=[
+                pltpu.VMEM((2, 3, 2, width, width), low),
+                pltpu.VMEM((2, 3, 2, width, width), low),
+                pltpu.VMEM((2, 3, steps, slots, width), f32),
+                pltpu.VMEM(hidden, f32),
+                pltpu.SemaphoreType.DMA((4,)),
+            ],
+        ),
+        out_shape=[jax.ShapeDtypeStruct(saved, low)] * 2
+        + [jax.ShapeDtypeStruct(saved, f32)] * 5
+        + [jax.ShapeDtypeStruct(hidden, f32)] * 2,
+        compiler_params=pltpu.CompilerParams(vmem_limit_bytes=VMEM_LIMIT),
+        name="forward",
+    )(me, own, oth, codes, start, *weights)
+
+
+def backward_kernel(half, mp_ref, code_ref, from_ref, upd_ref, rst_ref, cand_ref, rec_ref, pri_ref,
+                    last_ref, wi_own, wi_oth, wr_own, wr_oth, gate_ref, emb_ref, first_ref, wi, wr,
+                    state, sems):
+    me = mp_ref[0]
+    other = 1 - me
+    copies = [
+        pltpu.make_async_copy(wr_own, wr.at[me], sems.at[0]),
+        pltpu.make_async_copy(wr_oth, wr.at[other], sems.at[1]),
+        pltpu.make_async_copy(wi_own, wi.at[me], sems.at[2]),
+        pltpu.make_async_copy(wi_oth, wi.at[other], sems.at[3]),
+    ]
+    for copy in copies:
+        copy.start()
+    steps, slots, _ = code_ref.shape
+    width = from_ref.shape[-1]
+    real = lax.broadcasted_iota(jnp.int32, (slots, width), 1) < half
+    state[...] = last_ref[...]
+    copies[0].wait()
+    copies[1].wait()
+
+    def step(i, carry):
+        t = steps - 1 - i
+        code = code_ref[t]
+        keep = widen((code == 1.0).astype(jnp.float32), width)
+        live = widen((code > 0.0).astype(jnp.float32), width)
+        gates = []
+        direct = []
+        for side in range(2):
+            grad = live * (state[side] + from_ref[side, t])
+            update, reset = upd_ref[side, t], rst_ref[side, t]
+            candidate = cand_ref[side, t]
+            grad_update = grad * (pri_ref[side, t] - candidate)
+            grad_cand = grad * (1.0 - update) * (1.0 - candidate * candidate)
+            grad_reset = grad_cand * rec_ref[side, t]
+            values = [
+                grad_update * update * (1.0 - update),
+                grad_reset * reset * (1.0 - reset),
+                grad_cand * reset,
+                grad_cand,
+            ]
+            values = [value.astype(jnp.bfloat16) for value in values]
+            for gate in range(4):
+                gate_ref[gate, side, t] = values[gate]
+            gates.append(values)
+            direct.append(grad * update)
+        for into in range(2):
+            total = direct[into]
+            for side in range(2):
+                for gate in range(3):
+                    total = total + dot_last(gates[side][gate], wr[side, gate, into])
+            state[into] = jnp.where(real, keep * total, 0.0)
+        return carry
+
+    lax.fori_loop(0, steps, step, 0)
+    first_ref[...] = state[...]
+    copies[2].wait()
+    copies[3].wait()
+    events = steps * slots
+    for into in range(2):
+        total = jnp.zeros((events, width), jnp.float32)
+        for side in range(2):
+            for gate in range(3):
+                grads = gate_ref[3 if gate == 2 else gate, side].reshape(events, width)
+                total = total + dot_last(grads, wi[side, gate, into])
+        emb_ref[into] = total.astype(jnp.bfloat16)
+
+
+def run_backward(half, block, me, codes, from_scores, saved_values, last, weights):
+    _, steps, slots, lanes = codes.shape
+    width = last.shape[-1]
+    f32, low = jnp.float32, jnp.bfloat16
+    whole = lambda shape: pl.BlockSpec(shape, lambda i, s: (0,) * len(shape))
+    saved = (2, steps, slots, width)
+    hidden = (2, slots, width)
+    return pl.pallas_call(
+        functools.partial(backward_kernel, half),
+        grid_spec=pltpu.PrefetchScalarGridSpec(
+            num_scalar_prefetch=1,
+            grid=(1,),
+            in_specs=[pl.BlockSpec((None, steps, slots, lanes), lambda i, s: (block, 0, 0, 0))]
+            + [whole(saved)] * 6
+            + [whole(hidden)]
+            + [pl.BlockSpec(memory_space=pl.ANY)] * 4,
+            out_specs=[
+                whole((4,) + saved),
+                whole((2, steps * slots, width)),
+                whole(hidden),
+            ],
+            scratch_shapes=[
+                pltpu.VMEM((2, 3, 2, width, width), low),
+                pltpu.VMEM((2, 3, 2, width, width), low),
+                pltpu.VMEM(hidden, f32),
+                pltpu.SemaphoreType.DMA((4,)),
+            ],
+        ),
+        out_shape=[
+            jax.ShapeDtypeStruct((4,) + saved, low),
+            jax.ShapeDtypeStruct((2, steps * slots, width), low),
+            jax.ShapeDtypeStruct(hidden, f32),
+        ],
+        compiler_params=pltpu.CompilerParams(vmem_limit_bytes=VMEM_LIMIT),
+        name="backward",
+    )(me, codes, from_scores, *saved_values, last, *weights)
+
+
+def score_kernel(half, mp_ref, inv_ref, out_ref, want_ref, live_ref, use_ref, tgt_own, tgt_oth,
+                 neg_own, neg_oth, grad_ref, to_ref, stat_ref, scores):
+    me = mp_ref[0]
+    other = 1 - me
+    _, events, width = out_ref.shape
+    batch = tgt_own.shape[0]
+    devices, capacity, _ = neg_own.shape
+    negs = devices * capacity
+    cols = batch + negs
+    lane = lax.broadcasted_iota(jnp.int32, (16, width), 1)
+    row = lax.broadcasted_iota(jnp.int32, (16, width), 0)
+    pick = jnp.where(
+        row == 0,
+        jnp.where(lane == half + 3, 256.0, jnp.where(lane == half + 4, 1.0, 0.0)),
+        jnp.where((row == 1) & (lane == half + 5), 1.0, 0.0),
+    ).astype(jnp.bfloat16)
+    left_own = jnp.concatenate([out_ref[me], pick], axis=0)
+    left_oth = jnp.concatenate([out_ref[other], pick], axis=0)
+    nown = neg_own[...].reshape(negs, width)
+    noth = neg_oth[...].reshape(negs, width)
+    scores[:, :batch] = dot_last(left_own, tgt_own[...]) + dot_last(left_oth, tgt_oth[...])
+    scores[:, batch:] = dot_last(left_own, nown) + dot_last(left_oth, noth)
+    ids = scores[events : events + 1, :]
+    usable = jnp.concatenate([use_ref[:1, :], scores[events + 1 : events + 2, batch:]], axis=1)
+    ids = jnp.where(usable > 0.5, ids, -1.0)
+    group = 16
+    inv = inv_ref[0]
+    base = me * events
+
+    def rows_step(i, stats):
+        loss_sum, square_sum = stats
+        rows = pl.ds(pl.multiple_of(i * group, group), group)
+        s = scores[rows, :]
+        want = want_ref[rows, :1]
+        live = live_ref[rows, :1]
+        allowed = (ids != want) & (usable > 0.5)
+        head = s[:, :batch]
+        column = lax.broadcasted_iota(jnp.int32, (group, batch), 1)
+        place = lax.broadcasted_iota(jnp.int32, (group, batch), 0) + (base + i * group)
+        diagonal = column == place
+        positive = jnp.sum(jnp.where(diagonal, head, 0.0), axis=1, keepdims=True)
+        masked = jnp.where(allowed, s, NEGATIVE_FLOOR)
+        top = jnp.max(masked, axis=1, keepdims=True)
+        weight = jnp.exp(masked - top)
+        normal = jnp.sum(weight, axis=1, keepdims=True)
+        gap = positive - s
+        tail = jnp.exp(-jnp.abs(gap))
+        lift = 1.0 + tail
+        joined = jnp.where(allowed, jnp.minimum(s, positive) - jnp.log(lift), NEGATIVE_FLOOR)
+        top_joined = jnp.max(joined, axis=1, keepdims=True)
+        mass = jnp.exp(joined - top_joined)
+        joined_sum = jnp.sum(mass, axis=1, keepdims=True)
+        shared = mass / lift
+        below = gap >= 0.0
+        to_score = shared * jnp.where(below, 1.0, tail)
+        to_positive = jnp.sum(shared * jnp.where(below, tail, 1.0), axis=1, keepdims=True)
+        square = s * s
+        penalty = jnp.sum(weight * square, axis=1, keepdims=True) / normal
+        loss = top + jnp.log(normal) - top_joined - jnp.log(joined_sum) + REGULAR * penalty
+        scale = live * inv
+        grad = (scale / normal) * weight * (
+            1.0 + REGULAR * (square + 2.0 * s - penalty)
+        ) - (scale / joined_sum) * to_score
+        drop = jnp.where(diagonal, scale * to_positive / joined_sum, 0.0)
+        grad_ref[rows, :batch] = (grad[:, :batch] - drop).astype(jnp.bfloat16)
+        grad_ref[rows, batch:] = grad[:, batch:].astype(jnp.bfloat16)
+        loss_sum = loss_sum + live * loss
+        square_sum = square_sum + live * jnp.sum(square, axis=1, keepdims=True)
+        return loss_sum, square_sum
+
+    zero = jnp.zeros((group, 1), jnp.float32)
+    loss_sum, square_sum = lax.fori_loop(0, events // group, rows_step, (zero, zero))
+    stat_ref[0] = jnp.broadcast_to(loss_sum[:8] + loss_sum[8:], (8, 128))
+    stat_ref[1] = jnp.broadcast_to(square_sum[:8] + square_sum[8:], (8, 128))
+    grad_tgt = grad_ref[:, :batch]
+    grad_neg = grad_ref[:, batch:]
+    real = lax.broadcasted_iota(jnp.int32, (events, width), 1) < half
+    to_own = dot_f32(grad_tgt, tgt_own[...]) + dot_f32(grad_neg, nown)
+    to_oth = dot_f32(grad_tgt, tgt_oth[...]) + dot_f32(grad_neg, noth)
+    to_ref[me] = jnp.where(real, to_own, 0.0)
+    to_ref[other] = jnp.where(real, to_oth, 0.0)
+
+
+def run_scores(half, block, me, inv, outputs, want, live, use, tgt_own, tgt_oth, neg_own, neg_oth):
+    _, events, width = outputs.shape
+    batch = tgt_own.shape[1]
+    devices, _, capacity, _ = neg_own.shape
+    cols = batch + devices * capacity
+    low, f32 = jnp.bfloat16, jnp.float32
+    whole = lambda shape: pl.BlockSpec(shape, lambda i, s: (0,) * len(shape))
+    ofblock = lambda shape: pl.BlockSpec((None,) + shape, lambda i, s: (block,) + (0,) * len(shape))
+    once = pl.Buffered(1)
+    neg = pl.BlockSpec(
+        (devices, None, capacity, width), lambda i, s: (0, block, 0, 0), pipeline_mode=once
+    )
+    return pl.pallas_call(
+        functools.partial(score_kernel, half),
+        grid_spec=pltpu.PrefetchScalarGridSpec(
+            num_scalar_prefetch=1,
+            grid=(1,),
+            in_specs=[
+                pl.BlockSpec(memory_space=pltpu.SMEM),
+                whole((2, events, width)),
+                ofblock((events, 128)),
+                ofblock((events, 128)),
+                ofblock((8, batch)),
+                ofblock((batch, width)),
+                ofblock((batch, width)),
+                neg,
+                neg,
+            ],
+            out_specs=[whole((events, cols)), whole((2, events, width)), whole((2, 8, 128))],
+            scratch_shapes=[pltpu.VMEM((events + 16, cols), f32)],
+        ),
+        out_shape=[
+            jax.ShapeDtypeStruct((events, cols), low),
+            jax.ShapeDtypeStruct((2, events, width), f32),
+            jax.ShapeDtypeStruct((2, 8, 128), f32),
+        ],
+        compiler_params=pltpu.CompilerParams(vmem_limit_bytes=VMEM_LIMIT),
+        name="scores",
+    )(me, inv, outputs, want, live, use, tgt_own, tgt_oth, neg_own, neg_oth)
+
+
+def weight_grads_kernel(count, *refs):
+    lefts, rights, out_ref = refs[:count], refs[count : 2 * count], refs[2 * count]
+    for side in range(2):
+        total = dot_first(lefts[0][side], rights[0][...])
+        for left, right in zip(lefts[1:], rights[1:]):
+            total = total + dot_first(left[side], right[...])
+        out_ref[side] = total.astype(jnp.bfloat16)
+
+
+def weight_grads(lefts, rights):
+    _, _, width = lefts[0].shape
+    return pl.pallas_call(
+        functools.partial(weight_grads_kernel, len(lefts)),
+        out_shape=jax.ShapeDtypeStruct((2, width, width), jnp.bfloat16),
+        compiler_params=pltpu.CompilerParams(vmem_limit_bytes=VMEM_LIMIT),
+        name="weights",
+    )(*lefts, *rights)
+
+
+def pair(index, own, oth):
+    return jnp.where(index == 0, jnp.stack([own, oth]), jnp.stack([oth, own]))
+
+
+def sum_devices(chunk):
+    return lax.psum(chunk, "dp")
+
+
+def routed(items, targets, masks, plan, negatives, h_init, emb, w_in, w_rec, b_in, b_rec_n,
+           out_table, out_bias, wanted_rows, item_slot, target_slot, own_negatives, count):
+    f32, low = jnp.float32, jnp.bfloat16
+    blocks, steps, all_slots = items.shape
+    slots = all_slots // 2
+    events = steps * slots
+    batch = 2 * events
+    half = h_init.shape[1]
+    width = roundup(half + 6, 128)
+    rows = emb.shape[0]
+    devices = lax.axis_size("dp")
+    device = lax.axis_index("dp")
+    core = lax.axis_index("mp")
+    me = core.astype(jnp.int32).reshape(1)
+    first_half = (core == 0).astype(f32)
+    capacity = wanted_rows.shape[1] // 2
+    neg_capacity = own_negatives.shape[1]
+    breadth = 2 * half
+    spare = width - half
+
+    def mine(values):
+        return lax.dynamic_index_in_dim(values, core, 0, keepdims=False)
+
+    def core_major(values):
+        return values.reshape(blocks, steps, 2, slots).transpose(2, 0, 1, 3)
+
+    row_lanes = jnp.concatenate(
+        [jnp.ones((rows, 3), f32), jnp.zeros((rows, spare - 3), f32)], axis=1
+    )
+    emb_wide = jnp.concatenate([emb, (row_lanes * first_half).astype(low)], axis=1)
+    ids = device * rows + jnp.arange(rows)
+    parts = bf16_parts(out_bias)
+    out_lanes = jnp.stack(
+        [*parts, (ids // 256).astype(f32), (ids % 256).astype(f32), jnp.ones((rows,), f32)]
+        + [jnp.zeros((rows,), f32)] * (spare - 6),
+        axis=1,
+    )
+    out_wide = jnp.concatenate([out_table, (out_lanes * first_half).astype(low)], axis=1)
+
+    item_pick = one_hot(wanted_rows[:, :capacity].reshape(devices * capacity), rows)
+    target_pick = one_hot(wanted_rows[:, capacity:].reshape(devices * capacity), rows)
+    negative_pick = one_hot(own_negatives.reshape(blocks * neg_capacity), rows)
+    item_rows = exchange(
+        dot_f32(item_pick, emb_wide).astype(low).reshape(devices, capacity, width)
+    ).reshape(devices * capacity, width)
+    neg_own = lax.all_gather(
+        dot_f32(negative_pick, out_wide).astype(low), "dp", axis=0, tiled=True
+    )
+    target_rows = exchange(
+        dot_f32(target_pick, out_wide).astype(low).reshape(devices, capacity, width)
+    ).reshape(devices * capacity, width)
+
+    def widened(weight, bias, gate):
+        matrix = weight[:, gate, :].reshape(2, half, half)
+        matrix = jnp.pad(matrix, ((0, 0), (0, 0), (0, spare)))
+        if bias is None:
+            extra = jnp.zeros((2, spare, width), low)
+        else:
+            line = jnp.stack([*bf16_parts(bias)]).astype(low)
+            extra = jnp.pad(line[None], ((0, 1), (0, spare - 3), (0, spare)))
+        return jnp.concatenate([matrix, extra], axis=1)
+
+    wi_own = jnp.stack([widened(w_in, b_in[gate], gate) for gate in range(3)])
+    wr_own = jnp.stack([widened(w_rec, b_rec_n if gate == 2 else None, gate) for gate in range(3)])
+    weights = (wi_own, swap_cores(wi_own), wr_own, swap_cores(wr_own))
+
+    start_all = jnp.pad(h_init, ((0, 0), (0, spare))).reshape(2, slots, width)
+    start_own = mine(start_all)
+    start_oth = swap_cores(lax.dynamic_index_in_dim(start_all, 1 - core, 0, keepdims=False))
+    state = pair(core, start_own, start_oth)
+
+    codes_all = core_major(masks)
+    codes = mine(codes_all).astype(f32)
+    codes_wide = jnp.broadcast_to(codes[..., None], (blocks, steps, slots, 128))
+    target_all = core_major(targets).reshape(2, blocks, events)
+    want = jnp.broadcast_to(mine(target_all).astype(f32)[..., None], (blocks, events, 128))
+    live = (codes_wide > 0.0).astype(f32).reshape(blocks, events, 128)
+    use = (codes_all > 0).astype(f32).reshape(2, blocks, events).transpose(1, 0, 2)
+    use = jnp.broadcast_to(use.reshape(blocks, 1, batch), (blocks, 8, batch))
+
+    emb_own = dot_f32(one_hot(item_slot, devices * capacity), item_rows).astype(low)
+    emb_oth = swap_cores(emb_own).reshape(2, blocks, events, width)
+    emb_own = emb_own.reshape(2, blocks, events, width)
+
+    hop = -(-slots // devices)
+    saves = []
+    outs = []
+    entries = []
+    routes = []
+    in_square = jnp.zeros((), f32)
+    out_square = jnp.zeros((), f32)
+    lane_real = (jnp.arange(2 * width) % width < half).astype(f32)
+    for block in range(blocks):
+        result = run_forward(half, block, me, emb_own, emb_oth, codes_wide, state, weights)
+        outs.append(result[0].reshape(2, events, width))
+        entries.append(result[1].reshape(2, events, width))
+        saves.append(result[2:7])
+        state = result[7]
+        in_square = in_square + jnp.sum(result[8][0])
+        out_square = out_square + jnp.sum(result[8][1])
+        if block + 1 < blocks:
+            going = lax.dynamic_slice_in_dim(plan[block], core * slots, slots, 0)
+            aim = going // all_slots
+            place = going % all_slots
+            order = jnp.arange(slots)
+            earlier = (aim[:, None] == aim[None, :]) & (order[:, None] > order[None, :])
+            position = aim * hop + jnp.sum(earlier.astype(jnp.int32), axis=1)
+            lanes = jnp.arange(2 * width)[None, :]
+            flat = state.transpose(1, 0, 2).reshape(slots, 2 * width)
+            flat = jnp.where(lanes == half, place.astype(f32)[:, None], flat)
+            flat = jnp.where(lanes == half + 1, 1.0, flat).astype(low)
+            put = (jnp.arange(devices * hop)[:, None] == position[None, :]).astype(low)
+            sent = dot_f32(put, flat).astype(low).reshape(devices, hop, 2 * width)
+            came = exchange(sent).reshape(devices * hop, 2 * width)
+            both = jnp.concatenate([came, swap_cores(came)], axis=0)
+            label = jnp.where(both[:, half + 1] > 0.5, both[:, half].astype(f32), -1.0)
+            here = (core * slots + order).astype(f32)
+            take = (here[:, None] == label[None, :]).astype(low)
+            moved = dot_f32(take, both) * lane_real
+            state = moved.reshape(slots, 2, width).transpose(1, 0, 2)
+            routes.append((label[: devices * hop], put))
+
+    neg_oth = swap_cores(neg_own).reshape(devices, blocks, neg_capacity, width)
+    neg_own = neg_own.reshape(devices, blocks, neg_capacity, width)
+    target_slot_blocks = target_slot.reshape(2, blocks, events).transpose(1, 0, 2)
+    target_hot = one_hot(target_slot_blocks.reshape(blocks * batch), devices * capacity)
+    tgt_own = dot_f32(target_hot, target_rows).astype(low)
+    tgt_oth = swap_cores(tgt_own).reshape(blocks, batch, width)
+    tgt_own = tgt_own.reshape(blocks, batch, width)
+    inv = (1.0 / count).reshape(1)
+    from_scores = [None] * blocks
+    loss_sum = jnp.zeros((), f32)
+    score_square = jnp.zeros((), f32)
+    row_grads = [None] * blocks
+    for block in reversed(range(blocks)):
+        grad_own, toward, stat = run_scores(
+            half, block, me, inv, outs[block], want, live, use, tgt_own, tgt_oth, neg_own, neg_oth
+        )
+        from_scores[block] = toward.reshape(2, steps, slots, width)
+        loss_sum = loss_sum + jnp.sum(stat[0, :, 0])
+        score_square = score_square + jnp.sum(stat[1, :, 0])
+        grad_oth = swap_cores(grad_own)
+        outs_oth = swap_cores(
+            lax.dynamic_index_in_dim(outs[block], 1 - core, 0, keepdims=False)
+        )
+        row_grads[block] = (
+            dot_first(grad_own, mine(outs[block])) + dot_first(grad_oth, outs_oth)
+        ).astype(low)
+    target_grads = jnp.concatenate([value[:batch] for value in row_grads], axis=0)
+    negative_grads = jnp.stack(
+        [value[batch:].reshape(devices, neg_capacity, width) for value in row_grads], axis=1
+    ).reshape(devices, blocks * neg_capacity, width)
+    negative_came = exchange(negative_grads)
+    target_came = exchange(
+        dot_first(target_hot, target_grads).astype(low).reshape(devices, capacity, width)
+    )
+
+    own_stats = jnp.stack([loss_sum, in_square, out_square, score_square])
+    own_stats = jnp.pad(own_stats, (0, 124)).reshape(1, 1, 128)
+    own_stats = own_stats + swap_cores(own_stats)
+    all_stats = jnp.sum(exchange(jnp.broadcast_to(own_stats, (devices, 1, 128))), axis=(0, 1))
+
+    grad_state = jnp.zeros((2, slots, width), f32)
+    gate_own = [None] * blocks
+    gate_oth = [None] * blocks
+    emb_grads = [None] * blocks
+    for block in reversed(range(blocks)):
+        gates, grad_emb_rows, grad_state = run_backward(
+            half, block, me, codes_wide, from_scores[block], saves[block], grad_state, weights
+        )
+        gates = gates.reshape(4, 2, events, width).transpose(1, 0, 2, 3)
+        gate_own[block] = mine(gates)
+        gate_oth[block] = swap_cores(
+            lax.dynamic_index_in_dim(gates, 1 - core, 0, keepdims=False)
+        )
+        emb_own_grad = mine(grad_emb_rows)
+        emb_oth_grad = swap_cores(
+            lax.dynamic_index_in_dim(grad_emb_rows, 1 - core, 0, keepdims=False)
+        )
+        emb_grads[block] = pair(core, emb_own_grad, emb_oth_grad)
+        if block > 0:
+            label, put = routes[block - 1]
+            flat = grad_state.transpose(1, 0, 2).reshape(slots, 2 * width).astype(low)
+            both = jnp.concatenate([flat, swap_cores(flat)], axis=0)
+            order = jnp.arange(slots)
+            names = jnp.concatenate([core * slots + order, (1 - core) * slots + order]).astype(f32)
+            fetch = (label[:, None] == names[None, :]).astype(low)
+            back = exchange(dot_f32(fetch, both).astype(low).reshape(devices, hop, 2 * width))
+            flat = dot_first(put, back.reshape(devices * hop, 2 * width)) * lane_real
+            grad_state = flat.reshape(slots, 2, width).transpose(1, 0, 2)
+
+    entry_oth = [swap_cores(value) for value in entries]
+    emb_full = [
+        [pair(core, mine(emb_own)[block], mine(emb_oth)[block]) for block in range(blocks)],
+        [
+            pair(
+                core,
+                lax.dynamic_index_in_dim(emb_own, 1 - core, 0, keepdims=False)[block],
+                lax.dynamic_index_in_dim(emb_oth, 1 - core, 0, keepdims=False)[block],
+            )
+            for block in range(blocks)
+        ],
+    ]
+    summed = []
+    for lefts, last in (
+        ([*entries, *entry_oth], 2),
+        ([*emb_full[0], *emb_full[1]], 3),
+    ):
+        for gate in (0, 1, last):
+            rights = [value[gate] for value in gate_own] + [value[gate] for value in gate_oth]
+            summed.append(weight_grads(lefts, rights))
+    summed = sum_devices(jnp.stack(summed)).astype(f32)
+    rec_sum, in_sum = summed[:3], summed[3:]
+
+    def unpadded(values):
+        return values[:, :, :half, :half].reshape(3, breadth, half).transpose(1, 0, 2)
+
+    grad_b_in = in_sum[:, 0, half, :half]
+    grad_b_rec = rec_sum[2, 0, half, :half]
+
+    item_slot_blocks = item_slot.reshape(2, blocks, events).transpose(1, 0, 2)
+    item_hot = one_hot(item_slot_blocks.reshape(blocks * batch), devices * capacity)
+    item_grads = jnp.stack(emb_grads).reshape(blocks * batch, width)
+    item_came = exchange(
+        dot_first(item_hot, item_grads).astype(low).reshape(devices, capacity, width)
+    )
+    grad_emb = dot_first(item_pick, item_came.reshape(devices * capacity, width))[:, :half]
+    negative_sum = jnp.sum(negative_came.astype(f32), axis=0).astype(low)
+    grad_out = dot_first(
+        target_pick, target_came.reshape(devices * capacity, width)
+    ) + dot_first(negative_pick, negative_sum)
+    bias_own = grad_out[:, half]
+    grad_out_bias = jnp.where(core == 0, bias_own, swap_cores(bias_own))
+
+    def slots_of(values):
+        own = mine(values)
+        oth = swap_cores(lax.dynamic_index_in_dim(values, 1 - core, 0, keepdims=False))
+        return pair(core, own, oth).reshape(all_slots, width)[:, :half]
+
+    columns = batch + negatives.shape[1]
+    return (
+        all_stats[0] / count,
+        jnp.sqrt(all_stats[1] / (count * breadth)),
+        jnp.sqrt(all_stats[2] / (count * breadth)),
+        jnp.sqrt(all_stats[3] / (count * columns)),
+        slots_of(state),
+        slots_of(grad_state),
+        grad_emb,
+        unpadded(in_sum),
+        unpadded(rec_sum),
+        grad_b_in,
+        grad_b_rec,
+        grad_out[:, :half],
+        grad_out_bias,
+    )
+
+
+def shards(items, targets, masks, plan, negatives, h_init, emb, w_in, w_rec, b_in, b_rec_n,
+           out_table, out_bias):
+    blocks, steps, all_slots = items.shape
+    devices = lax.axis_size("dp")
+    rows = emb.shape[0]
+    requests = blocks * steps * all_slots
+    capacity = max(32, roundup(-(-requests // devices), 16))
+    mean = -(-negatives.shape[1] // devices)
+    neg_capacity = min(roundup(mean + 4 * math.isqrt(mean), 16), roundup(rows, 16))
+
+    def core_major(values):
+        split = values.reshape(blocks, steps, 2, all_slots // 2)
+        return split.transpose(2, 0, 1, 3).reshape(requests)
+
+    item_rows, item_slot, item_most = plan_requests(core_major(items), devices, rows, capacity)
+    target_rows, target_slot, target_most = plan_requests(
+        core_major(targets), devices, rows, capacity
+    )
+    own_negatives, negative_most = plan_negatives(
+        negatives, devices, rows, neg_capacity, lax.axis_index("dp")
+    )
+    wanted_rows = exchange(jnp.concatenate([item_rows, target_rows], axis=1))
+    over = (
+        (item_most > capacity) | (target_most > capacity) | (negative_most > neg_capacity)
+    ).astype(jnp.int32)
+    alive = jnp.sum((masks > 0).astype(jnp.int32))
+    lane = jnp.arange(128)[None, :]
+    tally = jnp.where(lane == 0, alive, jnp.where(lane == 1, over, 0))
+    tally = lax.psum(jnp.broadcast_to(tally, (8, 128)), "dp")
+    count = tally[0, 0].astype(jnp.float32)
+    given = (items, targets, masks, plan, negatives, h_init, emb, w_in, w_rec, b_in, b_rec_n,
+             out_table, out_bias)
+    return lax.cond(
+        tally[0, 1] == 0,
+        lambda: routed(*given, wanted_rows, item_slot, target_slot, own_negatives, count),
+        lambda: general(*given),
+    )
+
+
 def solution(mesh):
     return jax.shard_map(
         shards,

time: 4710 us -> 824 us (0.17)
  waiting for transfers between devices: 2280 us -> 363 us
  local copies, waits for them, and re-layouts: 746 us -> 86.6 us
  blocking collectives: 666 us -> 10.8 us
  other arithmetic: 550 us -> 39.1 us
  matrix products: 370 us -> 49.4 us
  Pallas kernels: 0 us -> 143 us
  starting transfers between devices: 20 us -> 88 us
    unnamed x9 -> x0, waiting for transfers between devices: 1940 us -> none
    unnamed x3 -> x0, blocking collectives: 586 us -> none
    dot_general x65 -> x25, matrix products: 370 us -> 49.4 us  [the longest x12 29.1 us: dot_first(): lax.dot_general(left, right, (((0,), (0,)), ((), ())), preferred_element_...]
    scatter-add x4 -> x0, other arithmetic: 212 us -> none  [the longest x2 137 us: bpr_rows(): positive = jnp.diagonal(scores[:, :session_events])]
    psum x0 -> x1, waiting for transfers between devices: none -> 159 us  [sum_devices(): return lax.psum(chunk, 'dp')]
    while x32 -> x0, waiting for transfers between devices: 145 us -> none
    pallas_call x0 -> x12, Pallas kernels: none -> 143 us  [the longest x2 48.2 us: run_backward(): pl.pallas_call(functools.partial(backward_kernel, half), grid_spec=pltpu....]
    all_to_all x3 -> x9, waiting for transfers between devices: 3.28 us -> 133 us  [exchange(): return lax.all_to_all(values, 'dp', split_axis=0, concat_axis=0, tiled=True)]
  transfers between devices with their start and end apart: 26 -> 33, of which waited for: 21 -> 11; matrix products, arithmetic and copies ran while one was open for 25% -> 19% of each run, Pallas kernels for 0% -> 17%
where the time goes in v1:
time: 824 us; the launch traced here: 819 us
  waiting for transfers between devices  363 us (44%)
  Pallas kernels  143 us (17%)
  starting transfers between devices  88 us (11%)
  local copies, waits for them, and re-layouts  86.6 us (11%)
  matrix products  49.4 us (6%)
  other arithmetic  39.1 us (5%)
  between operations  22.3 us (3%)
  loops' own time  16.4 us (2%)
  blocking collectives  10.8 us (1%)
    psum x1, waiting for transfers between devices, sum_devices(): return lax.psum(chunk, 'dp')  159 us
    all_to_all x9, waiting for transfers between devices, exchange(): return lax.all_to_all(values, 'dp', split_axis=0, concat_axis=0, tiled=True)  133 us
    all_gather x1, waiting for transfers between devices, routed(): lax.all_gather(dot_f32(negative_pick, out_wide).astype(low), 'dp', axis=0...  69.3 us
    all_to_all x9, starting transfers between devices, exchange(): return lax.all_to_all(values, 'dp', split_axis=0, concat_axis=0, tiled=True)  61.3 us
    pallas_call x2, Pallas kernels, run_backward(): pl.pallas_call(functools.partial(backward_kernel, half), grid_spec=pltpu....  48.2 us
    pallas_call x2, Pallas kernels, run_forward(): pl.pallas_call(functools.partial(forward_kernel, half), grid_spec=pltpu.P...  35.6 us
    pallas_call x2, Pallas kernels, run_scores(): pl.pallas_call(functools.partial(score_kernel, half), grid_spec=pltpu.Pre...  34.3 us
    dot_general x12, matrix products, dot_first(): lax.dot_general(left, right, (((0,), (0,)), ((), ())), preferred_element_...  29.1 us
  transfers between devices with their start and end apart: 33, of which 11 were waited for; matrix products, arithmetic and copies ran while one was open for 19% of the time, Pallas kernels for 17%

profile of v1, /device:TPU:1, one launch (start us, length us, event | category | flops | bytes accessed | tf_op | source)
XLA Modules:
  0.0 818.8 jit_solution(5794772922807398762)
XLA Ops:
  17.5 7.4 all-to-all-start.11
  30.2 10.8 %psum.49 = s32[8,128]{1,0:T(8,128)S(1)} all-reduce(s32[8,128]{1,0:T(8,128)S(1)} %broadcast_in_dim.496), channel_id=1, replica_groups=mesh['dp'=16,'mp'=2] {'dp'}, use_global_device_ids=true, to_apply=%region_7.8 | all-reduce | flops 1024 | bytes 8192 | tf_op jit(solution)/shard_map/psum | solution.py:1125
  47.9 758.7 %conditional.1 = (f32[64,500]{1,0:T(8,128)}, f32[64,500]{1,0:T(8,128)}, f32[]{:T(128)}, f32[]{:T(128)}, f32[]{:T(128)}, /*index=5*/f32[]{:T(128)}, f32[1176,500]...) conditional(s32[]{:T(128)} %bitcast.230, ...), branch_computations={%region_15.92_spmd, %region_89.105_spmd} | conditional | flops 30975397888 | bytes 1936932864 | solution.py:1129
  91.8 69.3 %all-gather.24.cloned.1.call-done = bf16[5632,512]{1,0:T(8,128)(2,1)} async-done(((bf16[352,512]{1,0:T(8,128)(2,1)}), bf16[5632,512]{1,0:T(8,128)(2,1)}) %all-gather.24.cloned.1.call-update) | async-done | bytes 5767184 | tf_op jit(solution)/shard_map/cond/branch_1_fun/all_gather | solution.py:885
  178.8 15.7 %all-to-all-start.2 = ((bf16[16,64,512]{2,1,0:T(8,128)(2,1)}), bf16[16,64,512]{2,1,0:T(8,128)(2,1)}, u32[]{:S(2)}, u32[]{:S(2)}) async-start(bf16[16,64,512]{2,1,0:T(8,128)(2,1)} %bitcast.137), calls=%async_computation.2 | async-start | bytes 2097152 | tf_op jit(solution)/shard_map/cond/branch_1_fun/all_to_all | solution.py:419
  198.9 17.3 %all-to-all-done.2 = bf16[16,64,512]{2,1,0:T(8,128)(2,1)} async-done(((bf16[16,64,512]{2,1,0:T(8,128)(2,1)}), bf16[16,64,512]{2,1,0:T(8,128)(2,1)}, u32[]{:S(2)}, u32[]{:S(2)}) %all-to-all-start.2) | async-done | bytes 1048608 | tf_op jit(solution)/shard_map/cond/branch_1_fun/all_to_all | solution.py:419
  224.0 17.8 %forward.2 = (bf16[2,8,32,512]{3,2,1,0:T(8,128)(2,1)}, bf16[2,8,32,512]{3,2,1,0:T(8,128)(2,1)}, f32[2,8,32,512]{3,2,1,0:T(8,128)}, f32[2,8,32,512]{3,2,1,0:T(8,1...) custom-call(s32[1]{0:T(128)} %bitcast.94.mp_ref, ...), custom_call_target="tpu_custom_call" | custom-call | tf_op jit(solution)/shard_map/cond/branch_1_fun/forward/pallas_call | solution.py:555
  243.6 6.1 all-to-all-start.1
  259.6 17.8 %forward.3 = (bf16[2,8,32,512]{3,2,1,0:T(8,128)(2,1)}, bf16[2,8,32,512]{3,2,1,0:T(8,128)(2,1)}, f32[2,8,32,512]{3,2,1,0:T(8,128)}, f32[2,8,32,512]{3,2,1,0:T(8,1...) custom-call(s32[1]{0:T(128)} %bitcast.94.mp_ref, ...), custom_call_target="tpu_custom_call" | custom-call | tf_op jit(solution)/shard_map/cond/branch_1_fun/forward/pallas_call | solution.py:555
  285.5 17.2 %scores.3 = (bf16[256,3328]{1,0:T(8,128)(2,1)}, f32[2,256,512]{2,1,0:T(8,128)}, f32[2,8,128]{2,1,0:T(8,128)}) custom-call(s32[1]{0:T(128)} %bitcast.94.mp_ref, f32[1]{0:T(128)} %bitcast.129.inv_ref, bf16[2,256,512]{2,1,0:T(8,128)(2,1)} %bitcast.850, f32[2,256,128]{2,1,0:T(8,128)} %broadcast_in_dim.473.want_ref, f32[2,256,128]{2,1,0:T(8,128)} %broadcast_in_dim.474.live_ref, ...), custom_call_target="tpu_custom_call" | custom-call | tf_op jit(solution)/shard_map/cond/branch_1_fun/scores/pallas_call | solution.py:784
  302.7 17.2 %scores.2 = (bf16[256,3328]{1,0:T(8,128)(2,1)}, f32[2,256,512]{2,1,0:T(8,128)}, f32[2,8,128]{2,1,0:T(8,128)}) custom-call(s32[1]{0:T(128)} %bitcast.94.mp_ref, f32[1]{0:T(128)} %bitcast.129.inv_ref, bf16[2,256,512]{2,1,0:T(8,128)(2,1)} %bitcast.853, f32[2,256,128]{2,1,0:T(8,128)} %broadcast_in_dim.473.want_ref, f32[2,256,128]{2,1,0:T(8,128)} %broadcast_in_dim.474.live_ref, ...), custom_call_target="tpu_custom_call" | custom-call | tf_op jit(solution)/shard_map/cond/branch_1_fun/scores/pallas_call | solution.py:784
  320.6 24.3 %backward.2 = (bf16[4,2,8,32,512]{4,3,2,1,0:T(8,128)(2,1)}, bf16[2,256,512]{2,1,0:T(8,128)(2,1)}, f32[2,32,512]{2,1,0:T(8,128)}) custom-call(s32[1]{0:T(128)} %bitcast.94.mp_ref, f32[2,8,32,128]{3,2,1,0:T(8,128)} %broadcast_in_dim.467.code_ref, f32[2,8,32,512]{3,2,1,0:T(8,128)} %bitcast.856, f32[2,8,32,512]{3,2,1,0:T(8,128)} %get-tuple-element.815.upd_ref, ...), custom_call_target="tpu_custom_call" | custom-call | tf_op jit(solution)/shard_map/cond/branch_1_fun/backward/pallas_call | solution.py:658
  361.9 23.9 %backward.3 = (bf16[4,2,8,32,512]{4,3,2,1,0:T(8,128)(2,1)}, bf16[2,256,512]{2,1,0:T(8,128)(2,1)}, f32[2,32,512]{2,1,0:T(8,128)}) custom-call(s32[1]{0:T(128)} %bitcast.94.mp_ref, f32[2,8,32,128]{3,2,1,0:T(8,128)} %broadcast_in_dim.467.code_ref, f32[2,8,32,512]{3,2,1,0:T(8,128)} %bitcast.855, f32[2,8,32,512]{3,2,1,0:T(8,128)} %get-tuple-element.809.upd_ref, ...), custom_call_target="tpu_custom_call" | custom-call | tf_op jit(solution)/shard_map/cond/branch_1_fun/backward/pallas_call | solution.py:658
  399.2 6.0 all-to-all-start.5
  419.3 7.7 all-to-all-done.5
  426.9 8.0 all-to-all-start.6
  440.6 16.5 %all-to-all-done.6 = bf16[16,64,512]{2,1,0:T(8,128)(2,1)} async-done(((bf16[16,64,512]{2,1,0:T(8,128)(2,1)}), bf16[16,64,512]{2,1,0:T(8,128)(2,1)}, u32[]{:S(2)}, u32[]{:S(2)}) %all-to-all-start.6) | async-done | bytes 1048608 | tf_op jit(solution)/shard_map/cond/branch_1_fun/all_to_all | solution.py:419
  457.2 6.8 all-to-all-start.7
  525.7 84.3 %all-to-all-done.7 = bf16[16,352,512]{2,1,0:T(8,128)(2,1)} async-done(((bf16[16,352,512]{2,1,0:T(8,128)(2,1)}), bf16[16,352,512]{2,1,0:T(8,128)(2,1)}, u32[]{:S(2)}, u32[]{:S(2)}) %all-to-all-start.7) | async-done | bytes 5767200 | tf_op jit(solution)/shard_map/cond/branch_1_fun/all_to_all | solution.py:419
  617.0 7.0 collective-permute-start.21
  624.0 158.8 %all-reduce.52.cloned.1.call-done = bf16[6,2,512,512]{3,2,1,0:T(8,128)(2,1)} async-done(((bf16[6,2,512,512]{3,2,1,0:T(8,128)(2,1)}), bf16[6,2,512,512]{3,2,1,0:T(8,128)(2,1)}) %all-reduce.52.cloned.1.call-update) | async-done | bytes 6291472 | tf_op jit(solution)/shard_map/cond/branch_1_fun/psum | solution.py:837
  782.8 9.1 %fusion.396 = (f32[3,2,500,500]{3,2,1,0:T(8,128)}, f32[3,2,500,500]{3,2,1,0:T(8,128)}) fusion(bf16[6,2,512,512]{3,2,1,0:T(8,128)(2,1)} %all-reduce.52.cloned.1.call-done), kind=kLoop, calls=%fused_computation.804 | loop fusion | bytes 24000000 | tf_op jit(solution)/shard_map/cond/branch_1_fun/slice | solution.py:1055
  792.7 6.5 reshape.1674
  799.1 6.5 reshape.1675
  (379 shorter events, 218.2 us)
Async XLA Ops:
  17.5 30.3 %all-to-all-start.11 = ((s32[16,1,128]{2,1,0:T(1,128)}), s32[16,1,128]{2,1,0:T(1,128)S(1)}, u32[]{:S(2)}, u32[]{:S(2)}) async-start(s32[16,1,128]{2,1,0:T(1,128)} %bitcast.232), calls=%async_computation.11 | async-start | bytes 16384 | tf_op jit(solution)/shard_map/all_to_all | solution.py:419
  55.1 106.0 %all-gather.24.cloned.1.call-start = ((), (), s32[]{:S(2)}) async-start(), calls=%async_computation.18 | async-start | bytes 6127616 | tf_op jit(solution)/shard_map/cond/branch_1_fun/all_gather | solution.py:885
  65.6 113.2 %all-to-all-start = ((bf16[16,64,512]{2,1,0:T(8,128)(2,1)}), bf16[16,64,512]{2,1,0:T(8,128)(2,1)}, u32[]{:S(2)}, u32[]{:S(2)}) async-start(bf16[16,64,512]{2,1,0:T(8,128)(2,1)} %bitcast.857), calls=%async_computation | async-start | bytes 2097152 | tf_op jit(solution)/shard_map/cond/branch_1_fun/all_to_all | solution.py:419
  70.9 127.3 %collective-permute-start.1 = (f32[32,512]{1,0:T(8,128)S(1)}, f32[32,512]{1,0:T(8,128)S(1)}, u32[]{:S(2)}, u32[]{:S(2)}) collective-permute-start(f32[32,512]{1,0:T(8,128)S(1)} %get-tuple-element.1862), channel_id=1, source_target_pairs={{0,1},{1,0},{2,3},{3,2},{4,5},{5,4},{6,7},{7,6},{8,9},{9,8},{10,11... | collective-permute-start | bytes 196616 | tf_op jit(solution)/shard_map/cond/branch_1_fun/ppermute | solution.py:415
  91.8 131.1 %collective-permute-start.2 = (bf16[3,2,512,512]{3,2,1,0:T(8,128)(2,1)}, bf16[3,2,512,512]{3,2,1,0:T(8,128)(2,1)}, u32[]{:S(2)}, u32[]{:S(2)}) collective-permute-start(bf16[3,2,512,512]{3,2,1,0:T(8,128)(2,1)} %pad_maximum_fusion.1.wi_own), channel_id=1, source_target_pairs={{0,1},{1,0},{2,3},{3,2},{4,5},{5,4},{6,7},{7,6},{8,9},{9,8},{10,11... | collective-permute-start | bytes 9437192 | tf_op jit(solution)/shard_map/cond/branch_1_fun/ppermute | solution.py:415
  161.1 122.2 %collective-permute-start.6 = (bf16[5632,512]{1,0:T(8,128)(2,1)}, bf16[5632,512]{1,0:T(8,128)(2,1)}, u32[]{:S(2)}, u32[]{:S(2)}) collective-permute-start(bf16[5632,512]{1,0:T(8,128)(2,1)} %all-gather.24.cloned.1.call-done), channel_id=1, source_target_pairs={{0,1},{1,0},{2,3},{3,2},{4,5},{5,4},{6,7},{7,6},{8,9},{9,8},{10,11... | collective-permute-start | bytes 17301512 | tf_op jit(solution)/shard_map/cond/branch_1_fun/ppermute | solution.py:415
  174.2 48.7 %collective-permute-start.3 = (bf16[3,2,512,512]{3,2,1,0:T(8,128)(2,1)}, bf16[3,2,512,512]{3,2,1,0:T(8,128)(2,1)}, u32[]{:S(2)}, u32[]{:S(2)}) collective-permute-start(bf16[3,2,512,512]{3,2,1,0:T(8,128)(2,1)} %pad_maximum_fusion.2.wr_own), channel_id=1, source_target_pairs={{0,1},{1,0},{2,3},{3,2},{4,5},{5,4},{6,7},{7,6},{8,9},{9,8},{10,11... | collective-permute-start | bytes 9437192 | tf_op jit(solution)/shard_map/cond/branch_1_fun/ppermute | solution.py:415
  178.8 37.4 %all-to-all-start.2 = ((bf16[16,64,512]{2,1,0:T(8,128)(2,1)}), bf16[16,64,512]{2,1,0:T(8,128)(2,1)}, u32[]{:S(2)}, u32[]{:S(2)}) async-start(bf16[16,64,512]{2,1,0:T(8,128)(2,1)} %bitcast.137), calls=%async_computation.2 | async-start | bytes 2097152 | tf_op jit(solution)/shard_map/cond/branch_1_fun/all_to_all | solution.py:419
  197.5 25.4 %collective-permute-start = (bf16[1024,512]{1,0:T(8,128)(2,1)S(1)}, bf16[1024,512]{1,0:T(8,128)(2,1)S(1)}, u32[]{:S(2)}, u32[]{:S(2)}) collective-permute-start(bf16[1024,512]{1,0:T(8,128)(2,1)S(1)} %fusion.127), channel_id=1, source_target_pairs={{0,1},{1,0},{2,3},{3,2},{4,5},{5,4},{6,7},{7,6},{8,9},{9,8},{10,11... | collective-permute-start | bytes 3145736 | tf_op jit(solution)/shard_map/cond/branch_1_fun/ppermute | solution.py:415
  219.7 63.6 %collective-permute-start.5 = (bf16[1024,512]{1,0:T(8,128)(2,1)}, bf16[1024,512]{1,0:T(8,128)(2,1)}, u32[]{:S(2)}, u32[]{:S(2)}) collective-permute-start(bf16[1024,512]{1,0:T(8,128)(2,1)} %fusion.128), channel_id=1, source_target_pairs={{0,1},{1,0},{2,3},{3,2},{4,5},{5,4},{6,7},{7,6},{8,9},{9,8},{10,11... | collective-permute-start | bytes 3145736 | tf_op jit(solution)/shard_map/cond/branch_1_fun/ppermute | solution.py:415
  243.6 12.5 %all-to-all-start.1 = ((bf16[16,2,1024]{2,1,0:T(2,128)(2,1)}), bf16[16,2,1024]{2,1,0:T(2,128)(2,1)S(1)}, u32[]{:S(2)}, u32[]{:S(2)}) async-start(bf16[16,2,1024]{2,1,0:T(2,128)(2,1)} %reshape.1645), calls=%async_computation.1 | async-start | bytes 131072 | tf_op jit(solution)/shard_map/cond/branch_1_fun/all_to_all | solution.py:419
  252.9 157.1 %collective-permute-start.18 = (bf16[256,512]{1,0:T(8,128)(2,1)}, bf16[256,512]{1,0:T(8,128)(2,1)S(1)}, u32[]{:S(2)}, u32[]{:S(2)}) collective-permute-start(bf16[256,512]{1,0:T(8,128)(2,1)} %dynamic-slice_bitcast_fusion.19), channel_id=1, source_target_pairs={{0,1},{1,0},{2,3},{3,2},{4,5},{5,4},{6,7},{7,6},{8,9},{9,8},{10,11... | collective-permute-start | bytes 786440 | tf_op jit(solution)/shard_map/cond/branch_1_fun/ppermute | solution.py:415
  346.8 58.4 %collective-permute-start.19 = (bf16[256,3328]{1,0:T(8,128)(2,1)}, bf16[256,3328]{1,0:T(8,128)(2,1)S(1)}, u32[]{:S(2)}, u32[]{:S(2)}) collective-permute-start(bf16[256,3328]{1,0:T(8,128)(2,1)} %get-tuple-element.829), channel_id=1, source_target_pairs={{0,1},{1,0},{2,3},{3,2},{4,5},{5,4},{6,7},{7,6},{8,9},{9,8},{10,11... | collective-permute-start | bytes 5111816 | tf_op jit(solution)/shard_map/cond/branch_1_fun/ppermute | solution.py:415
  354.7 32.9 %collective-permute-start.7 = (f32[1,1,128]{2,1,0:T(1,128)S(1)}, f32[1,1,128]{2,1,0:T(1,128)S(1)}, u32[]{:S(2)}, u32[]{:S(2)}) collective-permute-start(f32[1,1,128]{2,1,0:T(1,128)S(1)} %fusion.247), channel_id=1, source_target_pairs={{0,1},{1,0},{2,3},{3,2},{4,5},{5,4},{6,7},{7,6},{8,9},{9,8},{10,11... | collective-permute-start | bytes 1544 | tf_op jit(solution)/shard_map/cond/branch_1_fun/ppermute | solution.py:415
  356.1 37.1 %collective-permute-start.12 = (bf16[256,512]{1,0:T(8,128)(2,1)S(1)}, bf16[256,512]{1,0:T(8,128)(2,1)S(1)}, u32[]{:S(2)}, u32[]{:S(2)}) collective-permute-start(bf16[256,512]{1,0:T(8,128)(2,1)S(1)} %get-tuple-element.1854), channel_id=1, source_target_pairs={{0,1},{1,0},{2,3},{3,2},{4,5},{5,4},{6,7},{7,6},{8,9},{9,8},{10,11... | collective-permute-start | bytes 786440 | tf_op jit(solution)/shard_map/cond/branch_1_fun/ppermute | solution.py:415
  356.3 53.7 %collective-permute-start.17 = (bf16[256,3328]{1,0:T(8,128)(2,1)}, bf16[256,3328]{1,0:T(8,128)(2,1)}, u32[]{:S(2)}, u32[]{:S(2)}) collective-permute-start(bf16[256,3328]{1,0:T(8,128)(2,1)} %get-tuple-element.828), channel_id=1, source_target_pairs={{0,1},{1,0},{2,3},{3,2},{4,5},{5,4},{6,7},{7,6},{8,9},{9,8},{10,11... | collective-permute-start | bytes 5111816 | tf_op jit(solution)/shard_map/cond/branch_1_fun/ppermute | solution.py:415
  393.2 12.0 %collective-permute-start.20 = (bf16[256,512]{1,0:T(8,128)(2,1)}, bf16[256,512]{1,0:T(8,128)(2,1)}, u32[]{:S(2)}, u32[]{:S(2)}) collective-permute-start(bf16[256,512]{1,0:T(8,128)(2,1)} %dynamic-slice_bitcast_fusion.18), channel_id=1, source_target_pairs={{0,1},{1,0},{2,3},{3,2},{4,5},{5,4},{6,7},{7,6},{8,9},{9,8},{10,11... | collective-permute-start | bytes 786440 | tf_op jit(solution)/shard_map/cond/branch_1_fun/ppermute | solution.py:415
  399.2 27.7 %all-to-all-start.5 = ((bf16[16,64,512]{2,1,0:T(8,128)(2,1)}), bf16[16,64,512]{2,1,0:T(8,128)(2,1)}, u32[]{:S(2)}, u32[]{:S(2)}) async-start(bf16[16,64,512]{2,1,0:T(8,128)(2,1)} %bitcast.170), calls=%async_computation.5 | async-start | bytes 2097152 | tf_op jit(solution)/shard_map/cond/branch_1_fun/all_to_all | solution.py:419
  426.9 30.2 %all-to-all-start.6 = ((bf16[16,64,512]{2,1,0:T(8,128)(2,1)}), bf16[16,64,512]{2,1,0:T(8,128)(2,1)}, u32[]{:S(2)}, u32[]{:S(2)}) async-start(bf16[16,64,512]{2,1,0:T(8,128)(2,1)} %bitcast.217), calls=%async_computation.6 | async-start | bytes 2097152 | tf_op jit(solution)/shard_map/cond/branch_1_fun/all_to_all | solution.py:419
  457.2 152.8 %all-to-all-start.7 = ((bf16[16,352,512]{2,1,0:T(8,128)(2,1)}), bf16[16,352,512]{2,1,0:T(8,128)(2,1)}, u32[]{:S(2)}, u32[]{:S(2)}) async-start(bf16[16,352,512]{2,1,0:T(8,128)(2,1)} %bitcast.813), calls=%async_computation.7 | async-start | bytes 11534336 | tf_op jit(solution)/shard_map/cond/branch_1_fun/all_to_all | solution.py:419
  464.0 318.8 %all-reduce.52.cloned.1.call-start = ((), (), s32[]{:S(2)}) async-start(), calls=%async_computation.19 | async-start | bytes 12582912 | tf_op jit(solution)/shard_map/cond/branch_1_fun/psum | solution.py:837
  471.5 16.8 %collective-permute-start.13 = (bf16[2,256,512]{2,1,0:T(8,128)(2,1)S(1)}, bf16[2,256,512]{2,1,0:T(8,128)(2,1)S(1)}, u32[]{:S(2)}, u32[]{:S(2)}) collective-permute-start(bf16[2,256,512]{2,1,0:T(8,128)(2,1)S(1)} %bitcast.834), channel_id=1, source_target_pairs={{0,1},{1,0},{2,3},{3,2},{4,5},{5,4},{6,7},{7,6},{8,9},{9,8},{10,11... | collective-permute-start | bytes 1572872 | tf_op jit(solution)/shard_map/cond/branch_1_fun/ppermute | solution.py:415
  471.8 16.4 %collective-permute-start.14 = (bf16[2,256,512]{2,1,0:T(8,128)(2,1)S(1)}, bf16[2,256,512]{2,1,0:T(8,128)(2,1)S(1)}, u32[]{:S(2)}, u32[]{:S(2)}) collective-permute-start(bf16[2,256,512]{2,1,0:T(8,128)(2,1)S(1)} %bitcast.838), channel_id=1, source_target_pairs={{0,1},{1,0},{2,3},{3,2},{4,5},{5,4},{6,7},{7,6},{8,9},{9,8},{10,11... | collective-permute-start | bytes 1572872 | tf_op jit(solution)/shard_map/cond/branch_1_fun/ppermute | solution.py:415
  617.0 189.3 %collective-permute-start.21 = (f32[1176]{0:T(1024)S(1)}, f32[1176]{0:T(1024)S(1)}, u32[]{:S(2)}, u32[]{:S(2)}) collective-permute-start(f32[1176]{0:T(1024)S(1)} %slice_reduce_fusion), channel_id=1, source_target_pairs={{0,1},{1,0},{2,3},{3,2},{4,5},{5,4},{6,7},{7,6},{8,9},{9,8},{10,11... | collective-permute-start | bytes 14120 | tf_op jit(solution)/shard_map/cond/branch_1_fun/ppermute | solution.py:415
  (64 other events, 775.8 us)
Sparse Core Ops, SparseCore 0:
  59.8 101.2 all-gather.23
  510.1 272.5 all-reduce.51

commit v2 on v1

--- a/solution.py
+++ b/solution.py
@@ -442,9 +442,6 @@
     blocks, negs = negatives.shape
     chunk = math.gcd(negs, 128)
     owner = negatives // rows
-    counts = jnp.sum(
-        (owner[:, None, :] == jnp.arange(devices)[None, :, None]).astype(jnp.float32), axis=2
-    )
     mine = (owner == device).astype(jnp.float32)
     grouped = mine.reshape(blocks * (negs // chunk), chunk)
     order = jnp.arange(chunk)
@@ -460,7 +457,21 @@
     match = keyed[:, None, :] == jnp.arange(capacity, dtype=jnp.float32)[None, :, None]
     local = (negatives % rows).astype(jnp.float32) + 1.0
     listed = jnp.sum(jnp.where(match, local[:, None, :], 0.0), axis=2) - 1.0
-    return listed.astype(jnp.int32), jnp.max(counts)
+    return listed.astype(jnp.int32)
+
+
+def most_negatives(negatives, devices, rows):
+    owner = negatives // rows
+    counts = jnp.sum(
+        (owner[:, None, :] == jnp.arange(devices)[None, :, None]).astype(jnp.float32), axis=2
+    )
+    return jnp.max(counts)
+
+
+def cost(microseconds):
+    return pl.CostEstimate(
+        flops=0, bytes_accessed=int(microseconds * 3.6e6), transcendentals=0
+    )
 
 
 def widen(code, width):
@@ -468,7 +479,7 @@
 
 
 def forward_kernel(half, mp_ref, own_ref, oth_ref, code_ref, start_ref, wi_own, wi_oth, wr_own,
-                   wr_oth, out_ref, ent_ref, upd_ref, rst_ref, cand_ref, rec_ref, pri_ref, end_ref,
+                   wr_oth, outs_ref, outo_ref, ent_ref, upd_ref, rst_ref, cand_ref, rec_ref, pri_ref, end_ref,
                    sq_ref, wi, wr, pre, state, sems):
     me = mp_ref[0]
     other = 1 - me
@@ -512,8 +523,9 @@
             if side == 0:
                 value = jnp.where(ones, 1.0, value)
             value = value.astype(jnp.bfloat16)
-            ent_ref[side, t] = value
+            ent_ref[t, :, side * width : (side + 1) * width] = value
             entering.append(value)
+        lows = []
         for side in range(2):
             recurrent = [
                 dot_f32(entering[0], wr[side, gate, 0]) + dot_f32(entering[1], wr[side, gate, 1])
@@ -535,7 +547,9 @@
             out_sum = out_sum + low.astype(jnp.float32) * low.astype(jnp.float32)
             if side == 0:
                 low = jnp.where(ones, 1.0, low.astype(jnp.float32)).astype(jnp.bfloat16)
-            out_ref[side, t] = low
+            lows.append(low)
+        outs_ref[t] = jnp.where(me == 0, lows[0], lows[1])
+        outo_ref[t] = jnp.where(me == 0, lows[1], lows[0])
         return in_sum, out_sum
 
     zero = jnp.zeros((slots, width), jnp.float32)
@@ -558,13 +572,16 @@
             num_scalar_prefetch=1,
             grid=(1,),
             in_specs=[
-                pl.BlockSpec((None, None, events, width), lambda i, s: (s[0], block, 0, 0)),
-                pl.BlockSpec((None, None, events, width), lambda i, s: (s[0], block, 0, 0)),
+                pl.BlockSpec((None, None, events, width), lambda i, s: (0, block, 0, 0)),
+                pl.BlockSpec((None, None, events, width), lambda i, s: (1, block, 0, 0)),
                 pl.BlockSpec((None, steps, slots, lanes), lambda i, s: (block, 0, 0, 0)),
                 whole(hidden),
             ]
             + [pl.BlockSpec(memory_space=pl.ANY)] * 4,
-            out_specs=[whole(saved)] * 7 + [whole(hidden)] * 2,
+            out_specs=[whole(saved[1:])] * 2
+            + [whole((steps, slots, 2 * width))]
+            + [whole(saved)] * 5
+            + [whole(hidden)] * 2,
             scratch_shapes=[
                 pltpu.VMEM((2, 3, 2, width, width), low),
                 pltpu.VMEM((2, 3, 2, width, width), low),
@@ -573,17 +590,19 @@
                 pltpu.SemaphoreType.DMA((4,)),
             ],
         ),
-        out_shape=[jax.ShapeDtypeStruct(saved, low)] * 2
+        out_shape=[jax.ShapeDtypeStruct(saved[1:], low)] * 2
+        + [jax.ShapeDtypeStruct((steps, slots, 2 * width), low)]
         + [jax.ShapeDtypeStruct(saved, f32)] * 5
         + [jax.ShapeDtypeStruct(hidden, f32)] * 2,
         compiler_params=pltpu.CompilerParams(vmem_limit_bytes=VMEM_LIMIT),
+        cost_estimate=cost(18),
         name="forward",
     )(me, own, oth, codes, start, *weights)
 
 
-def backward_kernel(half, mp_ref, code_ref, from_ref, upd_ref, rst_ref, cand_ref, rec_ref, pri_ref,
-                    last_ref, wi_own, wi_oth, wr_own, wr_oth, gate_ref, emb_ref, first_ref, wi, wr,
-                    state, sems):
+def backward_kernel(half, mp_ref, code_ref, from_own, from_oth, upd_ref, rst_ref, cand_ref, rec_ref, pri_ref,
+                    last_ref, wi_own, wi_oth, wr_own, wr_oth, gate_own, gate_oth, emb_own, emb_oth,
+                    first_ref, wi, wr, gate_ref, state, sems):
     me = mp_ref[0]
     other = 1 - me
     copies = [
@@ -595,7 +614,7 @@
     for copy in copies:
         copy.start()
     steps, slots, _ = code_ref.shape
-    width = from_ref.shape[-1]
+    width = from_own.shape[-1]
     real = lax.broadcasted_iota(jnp.int32, (slots, width), 1) < half
     state[...] = last_ref[...]
     copies[0].wait()
@@ -609,7 +628,8 @@
         gates = []
         direct = []
         for side in range(2):
-            grad = live * (state[side] + from_ref[side, t])
+            toward = jnp.where(me == side, from_own[t], from_oth[t])
+            grad = live * (state[side] + toward)
             update, reset = upd_ref[side, t], rst_ref[side, t]
             candidate = cand_ref[side, t]
             grad_update = grad * (pri_ref[side, t] - candidate)
@@ -626,6 +646,9 @@
                 gate_ref[gate, side, t] = values[gate]
             gates.append(values)
             direct.append(grad * update)
+        for gate in range(4):
+            gate_own[gate, t] = jnp.where(me == 0, gates[0][gate], gates[1][gate])
+            gate_oth[gate, t] = jnp.where(me == 0, gates[1][gate], gates[0][gate])
         for into in range(2):
             total = direct[into]
             for side in range(2):
@@ -639,16 +662,19 @@
     copies[2].wait()
     copies[3].wait()
     events = steps * slots
+    results = []
     for into in range(2):
         total = jnp.zeros((events, width), jnp.float32)
         for side in range(2):
             for gate in range(3):
                 grads = gate_ref[3 if gate == 2 else gate, side].reshape(events, width)
                 total = total + dot_last(grads, wi[side, gate, into])
-        emb_ref[into] = total.astype(jnp.bfloat16)
-
-
-def run_backward(half, block, me, codes, from_scores, saved_values, last, weights):
+        results.append(total.astype(jnp.bfloat16))
+    emb_own[...] = jnp.where(me == 0, results[0], results[1])
+    emb_oth[...] = jnp.where(me == 0, results[1], results[0])
+
+
+def run_backward(half, block, me, codes, from_own, from_oth, saved_values, last, weights):
     _, steps, slots, lanes = codes.shape
     width = last.shape[-1]
     f32, low = jnp.float32, jnp.bfloat16
@@ -661,36 +687,42 @@
             num_scalar_prefetch=1,
             grid=(1,),
             in_specs=[pl.BlockSpec((None, steps, slots, lanes), lambda i, s: (block, 0, 0, 0))]
-            + [whole(saved)] * 6
+            + [whole(saved[1:])] * 2
+            + [whole(saved)] * 5
             + [whole(hidden)]
             + [pl.BlockSpec(memory_space=pl.ANY)] * 4,
             out_specs=[
-                whole((4,) + saved),
-                whole((2, steps * slots, width)),
+                whole((4,) + saved[1:]),
+                whole((4,) + saved[1:]),
+                whole((steps * slots, width)),
+                whole((steps * slots, width)),
                 whole(hidden),
             ],
             scratch_shapes=[
                 pltpu.VMEM((2, 3, 2, width, width), low),
                 pltpu.VMEM((2, 3, 2, width, width), low),
+                pltpu.VMEM((4,) + saved, low),
                 pltpu.VMEM(hidden, f32),
                 pltpu.SemaphoreType.DMA((4,)),
             ],
         ),
         out_shape=[
-            jax.ShapeDtypeStruct((4,) + saved, low),
-            jax.ShapeDtypeStruct((2, steps * slots, width), low),
+            jax.ShapeDtypeStruct((4,) + saved[1:], low),
+            jax.ShapeDtypeStruct((4,) + saved[1:], low),
+            jax.ShapeDtypeStruct((steps * slots, width), low),
+            jax.ShapeDtypeStruct((steps * slots, width), low),
             jax.ShapeDtypeStruct(hidden, f32),
         ],
         compiler_params=pltpu.CompilerParams(vmem_limit_bytes=VMEM_LIMIT),
+        cost_estimate=cost(23),
         name="backward",
-    )(me, codes, from_scores, *saved_values, last, *weights)
-
-
-def score_kernel(half, mp_ref, inv_ref, out_ref, want_ref, live_ref, use_ref, tgt_own, tgt_oth,
-                 neg_own, neg_oth, grad_ref, to_ref, stat_ref, scores):
+    )(me, codes, from_own, from_oth, *saved_values, last, *weights)
+
+
+def score_kernel(half, mp_ref, inv_ref, out_own, out_oth, want_ref, live_ref, use_ref, tgt_own, tgt_oth,
+                 neg_own, neg_oth, grad_ref, to_own, to_oth, stat_ref, scores):
     me = mp_ref[0]
-    other = 1 - me
-    _, events, width = out_ref.shape
+    events, width = out_own.shape
     batch = tgt_own.shape[0]
     devices, capacity, _ = neg_own.shape
     negs = devices * capacity
@@ -702,8 +734,8 @@
         jnp.where(lane == half + 3, 256.0, jnp.where(lane == half + 4, 1.0, 0.0)),
         jnp.where((row == 1) & (lane == half + 5), 1.0, 0.0),
     ).astype(jnp.bfloat16)
-    left_own = jnp.concatenate([out_ref[me], pick], axis=0)
-    left_oth = jnp.concatenate([out_ref[other], pick], axis=0)
+    left_own = jnp.concatenate([out_own[...], pick], axis=0)
+    left_oth = jnp.concatenate([out_oth[...], pick], axis=0)
     nown = neg_own[...].reshape(negs, width)
     noth = neg_oth[...].reshape(negs, width)
     scores[:, :batch] = dot_last(left_own, tgt_own[...]) + dot_last(left_oth, tgt_oth[...])
@@ -763,14 +795,15 @@
     grad_tgt = grad_ref[:, :batch]
     grad_neg = grad_ref[:, batch:]
     real = lax.broadcasted_iota(jnp.int32, (events, width), 1) < half
-    to_own = dot_f32(grad_tgt, tgt_own[...]) + dot_f32(grad_neg, nown)
-    to_oth = dot_f32(grad_tgt, tgt_oth[...]) + dot_f32(grad_neg, noth)
-    to_ref[me] = jnp.where(real, to_own, 0.0)
-    to_ref[other] = jnp.where(real, to_oth, 0.0)
-
-
-def run_scores(half, block, me, inv, outputs, want, live, use, tgt_own, tgt_oth, neg_own, neg_oth):
-    _, events, width = outputs.shape
+    total = dot_f32(grad_tgt, tgt_own[...]) + dot_f32(grad_neg, nown)
+    to_own[...] = jnp.where(real, total, 0.0)
+    total = dot_f32(grad_tgt, tgt_oth[...]) + dot_f32(grad_neg, noth)
+    to_oth[...] = jnp.where(real, total, 0.0)
+
+
+def run_scores(half, block, me, inv, out_own, out_oth, want, live, use, tgt_own, tgt_oth, neg_own,
+               neg_oth):
+    events, width = out_own.shape
     batch = tgt_own.shape[1]
     devices, _, capacity, _ = neg_own.shape
     cols = batch + devices * capacity
@@ -788,7 +821,8 @@
             grid=(1,),
             in_specs=[
                 pl.BlockSpec(memory_space=pltpu.SMEM),
-                whole((2, events, width)),
+                whole((events, width)),
+                whole((events, width)),
                 ofblock((events, 128)),
                 ofblock((events, 128)),
                 ofblock((8, batch)),
@@ -797,48 +831,167 @@
                 neg,
                 neg,
             ],
-            out_specs=[whole((events, cols)), whole((2, events, width)), whole((2, 8, 128))],
+            out_specs=[
+                whole((events, cols)),
+                whole((events, width)),
+                whole((events, width)),
+                whole((2, 8, 128)),
+            ],
             scratch_shapes=[pltpu.VMEM((events + 16, cols), f32)],
         ),
         out_shape=[
             jax.ShapeDtypeStruct((events, cols), low),
-            jax.ShapeDtypeStruct((2, events, width), f32),
+            jax.ShapeDtypeStruct((events, width), f32),
+            jax.ShapeDtypeStruct((events, width), f32),
             jax.ShapeDtypeStruct((2, 8, 128), f32),
         ],
         compiler_params=pltpu.CompilerParams(vmem_limit_bytes=VMEM_LIMIT),
+        cost_estimate=cost(22),
         name="scores",
-    )(me, inv, outputs, want, live, use, tgt_own, tgt_oth, neg_own, neg_oth)
-
-
-def weight_grads_kernel(count, *refs):
-    lefts, rights, out_ref = refs[:count], refs[count : 2 * count], refs[2 * count]
-    for side in range(2):
-        total = dot_first(lefts[0][side], rights[0][...])
-        for left, right in zip(lefts[1:], rights[1:]):
-            total = total + dot_first(left[side], right[...])
-        out_ref[side] = total.astype(jnp.bfloat16)
-
-
-def weight_grads(lefts, rights):
-    _, _, width = lefts[0].shape
+    )(me, inv, out_own, out_oth, want, live, use, tgt_own, tgt_oth, neg_own, neg_oth)
+
+
+def after(values, *others):
+    return lax.optimization_barrier((values, others))[0]
+
+
+AR_GROUPS = ((0, 2), (1, 3), (4,), (5,))
+
+
+def unpad_kernel(half, sides_ref, *refs):
+    halves, outs = refs[:-2], refs[-2:]
+    width = halves[0].shape[0]
+
+    def one_chunk(i, k, chunk):
+        kept, came = halves[2 * i], halves[2 * i + 1]
+        lanes = slice(k * width, (k + 1) * width)
+        for side in range(2):
+            value = jnp.where(sides_ref[chunk] == side, kept[:, lanes], came[:, lanes])
+            rows = slice(side * half, (side + 1) * half)
+            outs[chunk // 3][rows, :] = value.astype(jnp.float32)[:half, :half]
+
+    for i, group in enumerate(AR_GROUPS):
+        for k, chunk in enumerate(group):
+            pl.when(pl.program_id(0) == chunk % 3)(functools.partial(one_chunk, i, k, chunk))
+
+
+def unpad(half, sides, halves):
+    shape = jax.ShapeDtypeStruct((3, 2 * half, half), jnp.float32)
+    vmem = pl.BlockSpec(memory_space=pltpu.VMEM)
+    out = pl.BlockSpec((None, 2 * half, half), lambda gate: (gate, 0, 0))
     return pl.pallas_call(
-        functools.partial(weight_grads_kernel, len(lefts)),
-        out_shape=jax.ShapeDtypeStruct((2, width, width), jnp.bfloat16),
+        functools.partial(unpad_kernel, half),
+        grid=(3,),
+        in_specs=[pl.BlockSpec(memory_space=pltpu.SMEM)] + [vmem] * len(halves),
+        out_specs=[out, out],
+        out_shape=[shape, shape],
         compiler_params=pltpu.CompilerParams(vmem_limit_bytes=VMEM_LIMIT),
-        name="weights",
-    )(*lefts, *rights)
+        cost_estimate=cost(8),
+        name="unpad",
+    )(sides, *halves)
 
 
 def pair(index, own, oth):
     return jnp.where(index == 0, jnp.stack([own, oth]), jnp.stack([oth, own]))
 
 
-def sum_devices(chunk):
-    return lax.psum(chunk, "dp")
+def reduce_orders(devices):
+    bits = devices.bit_length() - 1
+    if devices != 1 << bits or bits < 3:
+        return None
+    rest = list(range(3, bits))
+    along, across = [0, 1, 2, *rest], [1, 0, 2, *rest]
+    return [along, across] * 3
+
+
+def flip(values, bit):
+    devices = lax.axis_size("dp")
+    return lax.ppermute(values, "dp", [(i, i ^ (1 << bit)) for i in range(devices)])
+
+
+def halve(values, bit):
+    place = (lax.axis_index("dp") >> bit) & 1
+    size = values.shape[0] // 2
+    send = lax.dynamic_slice_in_dim(values, (1 - place) * size, size)
+    keep = lax.dynamic_slice_in_dim(values, place * size, size)
+    return send, keep
+
+
+def add_low(left, right):
+    return (left.astype(jnp.float32) + right.astype(jnp.float32)).astype(left.dtype)
+
+
+def scatter_sum(chunks, orders, owner_sums):
+    parts = list(chunks)
+    for level in range(len(orders[0])):
+        if level >= 2:
+            arrived = [value.came for value in owner_sums]
+            parts = [after(part, arrived) for part in parts]
+        sends = []
+        for i, order in enumerate(orders):
+            send, keep = halve(parts[i], order[level])
+            parts[i] = add_low(keep, flip(send, order[level]))
+            sends.append(send)
+        if level != 1:
+            for value in owner_sums:
+                value.finish(sends)
+                if value.order:
+                    value.start()
+    while owner_sums and owner_sums[0].order:
+        for value in owner_sums:
+            value.start()
+            value.finish()
+    return parts
+
+
+def gather_sum(parts, orders, sent):
+    device = lax.axis_index("dp")
+    parts = [jnp.concatenate([parts[i] for i in group], axis=1) for group in AR_GROUPS]
+    orders = [orders[group[0]] for group in AR_GROUPS]
+    halves = []
+    for level in reversed(range(len(orders[0]))):
+        if level == 1:
+            came_rows = exchange(after(sent, parts))
+        for i, order in enumerate(orders):
+            bit = (device >> order[level]) & 1
+            came = flip(parts[i], order[level])
+            if level == 0:
+                halves += [parts[i], came]
+            else:
+                parts[i] = jnp.where(
+                    bit == 0,
+                    jnp.concatenate([parts[i], came]),
+                    jnp.concatenate([came, parts[i]]),
+                )
+    return halves, came_rows
+
+
+class OwnerSum:
+    def __init__(self, values, order):
+        bits = len(order)
+        self.order = list(order)
+        self.axes = list(reversed(range(bits)))
+        self.values = values.reshape((2,) * bits + values.shape[1:])
+
+    def start(self):
+        bit = self.order.pop(0)
+        axis = self.axes.index(bit)
+        place = (lax.axis_index("dp") >> bit) & 1
+        send = lax.dynamic_index_in_dim(self.values, 1 - place, axis, keepdims=False)
+        self.keep = lax.dynamic_index_in_dim(self.values, place, axis, keepdims=False)
+        self.axes.remove(bit)
+        self.came = flip(send, bit)
+        return send
+
+    def finish(self, *others):
+        self.values = add_low(self.keep, after(self.came, *others) if others else self.came)
+
+    def join(self, other):
+        self.values = jnp.concatenate([self.values, other.values], axis=-2)
 
 
 def routed(items, targets, masks, plan, negatives, h_init, emb, w_in, w_rec, b_in, b_rec_n,
-           out_table, out_bias, wanted_rows, item_slot, target_slot, own_negatives, count):
+           out_table, out_bias, item_list, target_list, item_slot, target_slot, neg_capacity, over):
     f32, low = jnp.float32, jnp.bfloat16
     blocks, steps, all_slots = items.shape
     slots = all_slots // 2
@@ -852,13 +1005,15 @@
     core = lax.axis_index("mp")
     me = core.astype(jnp.int32).reshape(1)
     first_half = (core == 0).astype(f32)
-    capacity = wanted_rows.shape[1] // 2
-    neg_capacity = own_negatives.shape[1]
+    capacity = item_list.shape[1]
     breadth = 2 * half
     spare = width - half
 
     def mine(values):
         return lax.dynamic_index_in_dim(values, core, 0, keepdims=False)
+
+    def theirs(values):
+        return lax.dynamic_index_in_dim(values, 1 - core, 0, keepdims=False)
 
     def core_major(values):
         return values.reshape(blocks, steps, 2, slots).transpose(2, 0, 1, 3)
@@ -876,18 +1031,24 @@
     )
     out_wide = jnp.concatenate([out_table, (out_lanes * first_half).astype(low)], axis=1)
 
+    own_negatives = plan_negatives(negatives, devices, rows, neg_capacity, device)
+    negative_pick = one_hot(own_negatives.reshape(blocks * neg_capacity), rows)
+    neg_own = lax.all_gather(
+        dot_f32(negative_pick, out_wide).astype(low), "dp", axis=0, tiled=True
+    )
+    alive = jnp.sum((masks > 0).astype(jnp.int32))
+    told = jnp.broadcast_to(jnp.stack([alive, over])[None, :], (devices, 2))
+    asking = jnp.concatenate([item_list, target_list, told], axis=1)
+    asked = exchange(asking)
+    wanted_rows = asked[:, : 2 * capacity]
+    count = jnp.sum(asked[:, 2 * capacity]).astype(f32)
+    overs = jnp.sum(asked[:, 2 * capacity + 1])
     item_pick = one_hot(wanted_rows[:, :capacity].reshape(devices * capacity), rows)
     target_pick = one_hot(wanted_rows[:, capacity:].reshape(devices * capacity), rows)
-    negative_pick = one_hot(own_negatives.reshape(blocks * neg_capacity), rows)
-    item_rows = exchange(
-        dot_f32(item_pick, emb_wide).astype(low).reshape(devices, capacity, width)
-    ).reshape(devices * capacity, width)
-    neg_own = lax.all_gather(
-        dot_f32(negative_pick, out_wide).astype(low), "dp", axis=0, tiled=True
-    )
-    target_rows = exchange(
-        dot_f32(target_pick, out_wide).astype(low).reshape(devices, capacity, width)
-    ).reshape(devices * capacity, width)
+    item_send = dot_f32(item_pick, emb_wide).astype(low).reshape(devices, capacity, width)
+    w_in, w_rec = after((w_in, w_rec), item_send)
+    item_rows = exchange(item_send).reshape(devices * capacity, width)
+    target_send = dot_f32(target_pick, out_wide).astype(low).reshape(devices, capacity, width)
 
     def widened(weight, bias, gate):
         matrix = weight[:, gate, :].reshape(2, half, half)
@@ -917,26 +1078,39 @@
     use = (codes_all > 0).astype(f32).reshape(2, blocks, events).transpose(1, 0, 2)
     use = jnp.broadcast_to(use.reshape(blocks, 1, batch), (blocks, 8, batch))
 
-    emb_own = dot_f32(one_hot(item_slot, devices * capacity), item_rows).astype(low)
-    emb_oth = swap_cores(emb_own).reshape(2, blocks, events, width)
+    slots_first = item_slot.reshape(2, blocks * events)
+    slots_first = jnp.concatenate([mine(slots_first), theirs(slots_first)])
+    item_hot = one_hot(slots_first, devices * capacity)
+    emb_own = dot_f32(item_hot, item_rows).astype(low)
+    emb_oth = swap_cores(emb_own)
+    target_rows = exchange(after(target_send, emb_own)).reshape(devices * capacity, width)
     emb_own = emb_own.reshape(2, blocks, events, width)
-
+    emb_oth = emb_oth.reshape(2, blocks, events, width)
+    inputs = jnp.concatenate(
+        [
+            emb_own.reshape(blocks * batch, width),
+            jnp.concatenate([emb_oth[1], emb_oth[0]]).reshape(blocks * batch, width),
+        ],
+        axis=1,
+    )
+
+    target_slot_blocks = target_slot.reshape(2, blocks, events).transpose(1, 0, 2)
+    target_hot = one_hot(target_slot_blocks.reshape(blocks * batch), devices * capacity)
+    tgt_own = dot_f32(target_hot, target_rows).astype(low)
     hop = -(-slots // devices)
     saves = []
     outs = []
     entries = []
     routes = []
-    in_square = jnp.zeros((), f32)
-    out_square = jnp.zeros((), f32)
+    squares = []
     lane_real = (jnp.arange(2 * width) % width < half).astype(f32)
     for block in range(blocks):
         result = run_forward(half, block, me, emb_own, emb_oth, codes_wide, state, weights)
-        outs.append(result[0].reshape(2, events, width))
-        entries.append(result[1].reshape(2, events, width))
-        saves.append(result[2:7])
-        state = result[7]
-        in_square = in_square + jnp.sum(result[8][0])
-        out_square = out_square + jnp.sum(result[8][1])
+        outs.append([value.reshape(events, width) for value in result[:2]])
+        entries.append(result[2].reshape(events, 2 * width))
+        saves.append(result[3:8])
+        state = result[8]
+        squares.append(result[9])
         if block + 1 < blocks:
             going = lax.dynamic_slice_in_dim(plan[block], core * slots, slots, 0)
             aim = going // all_slots
@@ -950,6 +1124,7 @@
             flat = jnp.where(lanes == half + 1, 1.0, flat).astype(low)
             put = (jnp.arange(devices * hop)[:, None] == position[None, :]).astype(low)
             sent = dot_f32(put, flat).astype(low).reshape(devices, hop, 2 * width)
+            sent = after(sent, target_rows)
             came = exchange(sent).reshape(devices * hop, 2 * width)
             both = jnp.concatenate([came, swap_cores(came)], axis=0)
             label = jnp.where(both[:, half + 1] > 0.5, both[:, half].astype(f32), -1.0)
@@ -957,66 +1132,70 @@
             take = (here[:, None] == label[None, :]).astype(low)
             moved = dot_f32(take, both) * lane_real
             state = moved.reshape(slots, 2, width).transpose(1, 0, 2)
+            state = after(state, tgt_own)
+            neg_own = after(neg_own, sent)
+            outs[block] = after(outs[block], state)
             routes.append((label[: devices * hop], put))
 
-    neg_oth = swap_cores(neg_own).reshape(devices, blocks, neg_capacity, width)
+    neg_oth = swap_cores(neg_own)
+    tgt_oth = swap_cores(tgt_own).reshape(blocks, batch, width)
+    outs[-1] = after(outs[-1], neg_oth, tgt_oth)
+    neg_oth = neg_oth.reshape(devices, blocks, neg_capacity, width)
     neg_own = neg_own.reshape(devices, blocks, neg_capacity, width)
-    target_slot_blocks = target_slot.reshape(2, blocks, events).transpose(1, 0, 2)
-    target_hot = one_hot(target_slot_blocks.reshape(blocks * batch), devices * capacity)
-    tgt_own = dot_f32(target_hot, target_rows).astype(low)
-    tgt_oth = swap_cores(tgt_own).reshape(blocks, batch, width)
     tgt_own = tgt_own.reshape(blocks, batch, width)
     inv = (1.0 / count).reshape(1)
     from_scores = [None] * blocks
-    loss_sum = jnp.zeros((), f32)
-    score_square = jnp.zeros((), f32)
+    orders = reduce_orders(devices)
+    stats = []
     row_grads = [None] * blocks
-    for block in reversed(range(blocks)):
-        grad_own, toward, stat = run_scores(
-            half, block, me, inv, outs[block], want, live, use, tgt_own, tgt_oth, neg_own, neg_oth
-        )
-        from_scores[block] = toward.reshape(2, steps, slots, width)
-        loss_sum = loss_sum + jnp.sum(stat[0, :, 0])
-        score_square = score_square + jnp.sum(stat[1, :, 0])
-        grad_oth = swap_cores(grad_own)
-        outs_oth = swap_cores(
-            lax.dynamic_index_in_dim(outs[block], 1 - core, 0, keepdims=False)
-        )
-        row_grads[block] = (
-            dot_first(grad_own, mine(outs[block])) + dot_first(grad_oth, outs_oth)
-        ).astype(low)
-    target_grads = jnp.concatenate([value[:batch] for value in row_grads], axis=0)
-    negative_grads = jnp.stack(
-        [value[batch:].reshape(devices, neg_capacity, width) for value in row_grads], axis=1
-    ).reshape(devices, blocks * neg_capacity, width)
-    negative_came = exchange(negative_grads)
-    target_came = exchange(
-        dot_first(target_hot, target_grads).astype(low).reshape(devices, capacity, width)
-    )
-
-    own_stats = jnp.stack([loss_sum, in_square, out_square, score_square])
-    own_stats = jnp.pad(own_stats, (0, 124)).reshape(1, 1, 128)
-    own_stats = own_stats + swap_cores(own_stats)
-    all_stats = jnp.sum(exchange(jnp.broadcast_to(own_stats, (devices, 1, 128))), axis=(0, 1))
-
-    grad_state = jnp.zeros((2, slots, width), f32)
     gate_own = [None] * blocks
     gate_oth = [None] * blocks
     emb_grads = [None] * blocks
+    emb_grads_oth = [None] * blocks
+    grad_state = jnp.zeros((2, slots, width), f32)
+    grad_pairs = []
     for block in reversed(range(blocks)):
-        gates, grad_emb_rows, grad_state = run_backward(
-            half, block, me, codes_wide, from_scores[block], saves[block], grad_state, weights
+        grad_own, *from_scores[block], stat = run_scores(
+            half, block, me, inv, *outs[block], want, live, use, tgt_own, tgt_oth, neg_own, neg_oth
         )
-        gates = gates.reshape(4, 2, events, width).transpose(1, 0, 2, 3)
-        gate_own[block] = mine(gates)
-        gate_oth[block] = swap_cores(
-            lax.dynamic_index_in_dim(gates, 1 - core, 0, keepdims=False)
+        stats.append(stat)
+        grad_pairs.insert(0, (grad_own, swap_cores(grad_own), swap_cores(outs[block][1])))
+    negative_grads = [None] * blocks
+
+    for block in range(blocks):
+        grad_own, grad_oth, outs_oth = grad_pairs[block]
+        value = dot_first(grad_own, outs[block][0]) + dot_first(grad_oth, outs_oth)
+        row_grads[block] = value.astype(low)
+    negative_grads = jnp.stack(
+        [value[batch:].reshape(devices, neg_capacity, width) for value in row_grads], axis=1
+    )
+    cut = roundup(neg_capacity // 2, 16)
+    owner_sums = []
+    if orders is not None:
+        owner_sums = [
+            OwnerSum(negative_grads[:, :, :cut], orders[0]),
+            OwnerSum(negative_grads[:, :, cut:], orders[1]),
+        ]
+        from_scores[-1] = after(from_scores[-1], [value.start() for value in owner_sums])
+    target_grads = jnp.concatenate([value[:batch] for value in row_grads], axis=0)
+    target_send = dot_first(target_hot, target_grads).astype(low)
+    target_came = exchange(target_send.reshape(devices, capacity, width))
+    entering = jnp.concatenate(entries, axis=0)
+    entering = jnp.concatenate([entering, swap_cores(entering)], axis=0)
+    for block in reversed(range(blocks)):
+        own, oth, emb_grads[block], emb_oth_grad, grad_state = run_backward(
+            half,
+            block,
+            me,
+            codes_wide,
+            *[value.reshape(steps, slots, width) for value in from_scores[block]],
+            saves[block],
+            grad_state,
+            weights,
         )
-        emb_own_grad = mine(grad_emb_rows)
-        emb_oth_grad = swap_cores(
-            lax.dynamic_index_in_dim(grad_emb_rows, 1 - core, 0, keepdims=False)
-        )
-        emb_grads[block] = pair(core, emb_own_grad, emb_oth_grad)
+        gate_own[block] = own.reshape(4, events, width)
+        gate_oth[block] = swap_cores(oth).reshape(4, events, width)
+        emb_grads_oth[block] = swap_cores(emb_oth_grad)
         if block > 0:
             label, put = routes[block - 1]
             flat = grad_state.transpose(1, 0, 2).reshape(slots, 2 * width).astype(low)
@@ -1024,47 +1203,70 @@
             order = jnp.arange(slots)
             names = jnp.concatenate([core * slots + order, (1 - core) * slots + order]).astype(f32)
             fetch = (label[:, None] == names[None, :]).astype(low)
-            back = exchange(dot_f32(fetch, both).astype(low).reshape(devices, hop, 2 * width))
+            home = dot_f32(fetch, both).astype(low).reshape(devices, hop, 2 * width)
+            back = exchange(home)
             flat = dot_first(put, back.reshape(devices * hop, 2 * width)) * lane_real
             grad_state = flat.reshape(slots, 2, width).transpose(1, 0, 2)
-
-    entry_oth = [swap_cores(value) for value in entries]
-    emb_full = [
-        [pair(core, mine(emb_own)[block], mine(emb_oth)[block]) for block in range(blocks)],
-        [
-            pair(
-                core,
-                lax.dynamic_index_in_dim(emb_own, 1 - core, 0, keepdims=False)[block],
-                lax.dynamic_index_in_dim(emb_oth, 1 - core, 0, keepdims=False)[block],
-            )
-            for block in range(blocks)
-        ],
+            if block == 1 and orders is not None:
+                for value in owner_sums:
+                    value.finish(home)
+                grad_state = after(grad_state, [value.start() for value in owner_sums], target_send)
+
+    gates = jnp.concatenate([*gate_own, *gate_oth], axis=1)
+    gates = after(gates, target_came)
+    chunks = [dot_first(entering, gates[gate]).astype(low) for gate in (0, 1, 2)]
+    chunks += [dot_first(inputs, gates[gate]).astype(low) for gate in (0, 1, 3)]
+    marker = chunks[-1]
+    target_came = after(target_came, marker)
+    own_stats = [
+        sum(jnp.sum(value[0, :, 0]) for value in stats),
+        sum(jnp.sum(value[0]) for value in squares),
+        sum(jnp.sum(value[1]) for value in squares),
+        sum(jnp.sum(value[1, :, 0]) for value in stats),
     ]
-    summed = []
-    for lefts, last in (
-        ([*entries, *entry_oth], 2),
-        ([*emb_full[0], *emb_full[1]], 3),
-    ):
-        for gate in (0, 1, last):
-            rights = [value[gate] for value in gate_own] + [value[gate] for value in gate_oth]
-            summed.append(weight_grads(lefts, rights))
-    summed = sum_devices(jnp.stack(summed)).astype(f32)
-    rec_sum, in_sum = summed[:3], summed[3:]
-
-    def unpadded(values):
-        return values[:, :, :half, :half].reshape(3, breadth, half).transpose(1, 0, 2)
-
-    grad_b_in = in_sum[:, 0, half, :half]
-    grad_b_rec = rec_sum[2, 0, half, :half]
-
-    item_slot_blocks = item_slot.reshape(2, blocks, events).transpose(1, 0, 2)
-    item_hot = one_hot(item_slot_blocks.reshape(blocks * batch), devices * capacity)
-    item_grads = jnp.stack(emb_grads).reshape(blocks * batch, width)
-    item_came = exchange(
-        dot_first(item_hot, item_grads).astype(low).reshape(devices, capacity, width)
-    )
+    own_stats = jnp.stack(bf16_parts(jnp.stack(own_stats)))
+    own_stats = jnp.pad(own_stats, ((0, capacity - 3), (width - 4, 0)))
+
+    def row_sums():
+        item_grads = jnp.concatenate([*emb_grads, *emb_grads_oth], axis=0)
+        item_sums = dot_first(item_hot, after(item_grads, marker))
+        item_sums = item_sums.reshape(devices, capacity, width) + own_stats
+        return item_sums.astype(low)
+
+    if orders is None:
+        item_came = exchange(row_sums())
+        sums = [lax.psum(chunk, "dp") for chunk in chunks]
+        sums = [jnp.concatenate([sums[i] for i in group], axis=1) for group in AR_GROUPS]
+        halves = [value for chunk in sums for value in (chunk[:width], chunk[width:])]
+        sides = [jnp.zeros((), jnp.int32)] * 6
+        negative_sum = lax.psum_scatter(
+            negative_grads, "dp", scatter_dimension=0, tiled=True
+        ).reshape(blocks * neg_capacity, width)
+    else:
+
+        parts = scatter_sum(chunks, orders, owner_sums)
+        first, second = [value.values for value in owner_sums]
+        negative_sum = jnp.concatenate(
+            [first.reshape(blocks, cut, width), second.reshape(blocks, neg_capacity - cut, width)],
+            axis=1,
+        ).reshape(blocks * neg_capacity, width)
+        halves, item_came = gather_sum(parts, orders, row_sums())
+        sides = [(device >> order[0]) & 1 for order in orders]
+    all_stats = jnp.sum(item_came[:, :3, width - 4 :].astype(f32), axis=(0, 1))
+    all_stats = all_stats + swap_cores(all_stats)
+    sides = [side.astype(jnp.int32) for side in sides]
+    sides = jnp.stack(sides[:3] + [side ^ core.astype(jnp.int32) for side in sides[3:]])
+
+    def first_row(chunk):
+        for i, group in enumerate(AR_GROUPS):
+            if chunk in group:
+                lanes = slice(group.index(chunk) * width, group.index(chunk) * width + half)
+                kept, came = halves[2 * i][half, lanes], halves[2 * i + 1][half, lanes]
+        return jnp.where(sides[chunk] == 0, kept, came).astype(f32)
+
+    grad_b_in = jnp.stack([first_row(chunk) for chunk in (3, 4, 5)])
+    grad_b_rec = first_row(2)
     grad_emb = dot_first(item_pick, item_came.reshape(devices * capacity, width))[:, :half]
-    negative_sum = jnp.sum(negative_came.astype(f32), axis=0).astype(low)
     grad_out = dot_first(
         target_pick, target_came.reshape(devices * capacity, width)
     ) + dot_first(negative_pick, negative_sum)
@@ -1073,20 +1275,18 @@
 
     def slots_of(values):
         own = mine(values)
-        oth = swap_cores(lax.dynamic_index_in_dim(values, 1 - core, 0, keepdims=False))
+        oth = swap_cores(theirs(values))
         return pair(core, own, oth).reshape(all_slots, width)[:, :half]
 
     columns = batch + negatives.shape[1]
-    return (
+    return overs, halves, sides, (
         all_stats[0] / count,
         jnp.sqrt(all_stats[1] / (count * breadth)),
         jnp.sqrt(all_stats[2] / (count * breadth)),
         jnp.sqrt(all_stats[3] / (count * columns)),
-        slots_of(state),
-        slots_of(grad_state),
+        slots_of(after(state, marker)),
+        slots_of(after(grad_state, marker)),
         grad_emb,
-        unpadded(in_sum),
-        unpadded(rec_sum),
         grad_b_in,
         grad_b_rec,
         grad_out[:, :half],
@@ -1112,25 +1312,28 @@
     target_rows, target_slot, target_most = plan_requests(
         core_major(targets), devices, rows, capacity
     )
-    own_negatives, negative_most = plan_negatives(
-        negatives, devices, rows, neg_capacity, lax.axis_index("dp")
-    )
-    wanted_rows = exchange(jnp.concatenate([item_rows, target_rows], axis=1))
+    negative_most = most_negatives(negatives, devices, rows)
     over = (
         (item_most > capacity) | (target_most > capacity) | (negative_most > neg_capacity)
     ).astype(jnp.int32)
-    alive = jnp.sum((masks > 0).astype(jnp.int32))
-    lane = jnp.arange(128)[None, :]
-    tally = jnp.where(lane == 0, alive, jnp.where(lane == 1, over, 0))
-    tally = lax.psum(jnp.broadcast_to(tally, (8, 128)), "dp")
-    count = tally[0, 0].astype(jnp.float32)
     given = (items, targets, masks, plan, negatives, h_init, emb, w_in, w_rec, b_in, b_rec_n,
              out_table, out_bias)
-    return lax.cond(
-        tally[0, 1] == 0,
-        lambda: routed(*given, wanted_rows, item_slot, target_slot, own_negatives, count),
-        lambda: general(*given),
-    )
+    overs, halves, sides, ready = routed(
+        *given, item_rows, target_rows, item_slot, target_slot, neg_capacity, over
+    )
+
+    halves, sides, ready = lax.optimization_barrier((halves, sides, ready))
+
+    def finish(halves, sides, ready):
+        grad_w_rec, grad_w_in = unpad(h_init.shape[1], sides, halves)
+        return (
+            *ready[:7],
+            grad_w_in.transpose(1, 0, 2),
+            grad_w_rec.transpose(1, 0, 2),
+            *ready[7:],
+        )
+
+    return lax.cond(overs == 0, finish, lambda *unused: general(*given), halves, sides, ready)
 
 
 def solution(mesh):

time: 824 us -> 574 us (0.70)
  waiting for transfers between devices: 363 us -> 128 us
  local copies, waits for them, and re-layouts: 86.6 us -> 47.4 us
  starting transfers between devices: 88 us -> 124 us
  Pallas kernels: 143 us -> 126 us
  loops' own time: 16.4 us -> 1.95 us
  other arithmetic: 39.1 us -> 50.9 us
  blocking collectives: 10.8 us -> 0 us
  between operations: 22.3 us -> 32 us
    psum x1 -> x0, waiting for transfers between devices: 159 us -> none  [sum_devices(): return lax.psum(chunk, 'dp')]
    all_to_all x9 -> x7, waiting for transfers between devices: 133 us -> 24.3 us  [exchange(): return lax.all_to_all(values, 'dp', split_axis=0, concat_axis=0, tiled=True)]
    ppermute x0 -> x48, waiting for transfers between devices: none -> 93.9 us  [flip(): lax.ppermute(values, 'dp', [(i, i ^ 1 << bit) for i in range(devices)])]
    all_gather x1, waiting for transfers between devices: 69.3 us -> 5.17 us  [routed(): lax.all_gather(dot_f32(negative_pick, out_wide).astype(low), 'dp', axis=0...]
    ppermute x0 -> x48, starting transfers between devices: none -> 44.4 us  [flip(): lax.ppermute(values, 'dp', [(i, i ^ 1 << bit) for i in range(devices)])]
    squeeze x14 -> x8, local copies, waits for them, and re-layouts: 22.1 us -> 4.68 us  [start(): lax.dynamic_index_in_dim(self.values, 1 - place, axis, keepdims=False)]
    all_to_all x9 -> x7, starting transfers between devices: 61.3 us -> 44.1 us  [exchange(): return lax.all_to_all(values, 'dp', split_axis=0, concat_axis=0, tiled=True)]
    pallas_call x6 -> x1, Pallas kernels: 24.7 us -> 7.79 us  [unpad(): pl.pallas_call(functools.partial(unpad_kernel, half), grid=(3,), in_specs...]
  transfers between devices with their start and end apart: 33 -> 77, of which waited for: 11 -> 39; matrix products, arithmetic and copies ran while one was open for 19% -> 23% of each run, Pallas kernels for 17% -> 18%
where the time goes in v2:
time: 574 us; the launch traced here: 565 us
  waiting for transfers between devices  128 us (22%)
  Pallas kernels  126 us (22%)
  starting transfers between devices  124 us (22%)
  matrix products  54.5 us (9%)
  other arithmetic  50.9 us (9%)
  local copies, waits for them, and re-layouts  47.4 us (8%)
  between operations  32 us (6%)
    ppermute x48, waiting for transfers between devices, flip(): lax.ppermute(values, 'dp', [(i, i ^ 1 << bit) for i in range(devices)])  93.9 us
    pallas_call x2, Pallas kernels, run_backward(): pl.pallas_call(functools.partial(backward_kernel, half), grid_spec=pltpu....  48 us
    ppermute x48, starting transfers between devices, flip(): lax.ppermute(values, 'dp', [(i, i ^ 1 << bit) for i in range(devices)])  44.4 us
    all_to_all x7, starting transfers between devices, exchange(): return lax.all_to_all(values, 'dp', split_axis=0, concat_axis=0, tiled=True)  44.1 us
    pallas_call x2, Pallas kernels, run_forward(): pl.pallas_call(functools.partial(forward_kernel, half), grid_spec=pltpu.P...  36.3 us
    ppermute x21, starting transfers between devices, swap_cores(): return lax.ppermute(values, 'mp', [(0, 1), (1, 0)])  35.7 us
    pallas_call x2, Pallas kernels, run_scores(): pl.pallas_call(functools.partial(score_kernel, half), grid_spec=pltpu.Pre...  34.1 us
    dot_general x18, matrix products, dot_first(): lax.dot_general(left, right, (((0,), (0,)), ((), ())), preferred_element_...  32.1 us
  transfers between devices with their start and end apart: 77, of which 39 were waited for; matrix products, arithmetic and copies ran while one was open for 23% of the time, Pallas kernels for 18%

profile of v2, /device:TPU:1, one launch (start us, length us, event | category | flops | bytes accessed | tf_op | source)
XLA Modules:
  0.0 565.0 jit_solution(12574670982803689126)
XLA Ops:
  28.5 7.4 %all-to-all-start.3 = ((s32[16,1,130]{2,1,0:T(1,128)}), s32[16,1,130]{2,1,0:T(1,128)S(1)}, u32[]{:S(2)}, u32[]{:S(2)}) async-start(s32[16,1,130]{2,1,0:T(1,128)} %copy.310), calls=%async_computation.3 | async-start | bytes 32768 | tf_op jit(solution)/shard_map/all_to_all | solution.py:419
  46.3 4.6 all-to-all-start.4
  87.5 7.2 %all-to-all-start.5 = ((bf16[16,64,512]{2,1,0:T(8,128)(2,1)}), bf16[16,64,512]{2,1,0:T(8,128)(2,1)}, u32[]{:S(2)}, u32[]{:S(2)}) async-start(bf16[16,64,512]{2,1,0:T(8,128)(2,1)} %bitcast.827), calls=%async_computation.5 | async-start | bytes 2097152 | tf_op jit(solution)/shard_map/all_to_all | solution.py:419
  102.2 18.2 %forward.2 = (bf16[8,32,512]{2,1,0:T(8,128)(2,1)}, bf16[8,32,512]{2,1,0:T(8,128)(2,1)}, bf16[8,32,1024]{2,1,0:T(8,128)(2,1)}, f32[2,8,32,512]{3,2,1,0:T(8,128)},...) custom-call(s32[1]{0:T(128)} %bitcast.103.mp_ref, ...), custom_call_target="tpu_custom_call" | custom-call | bytes 64800000 | tf_op jit(solution)/shard_map/forward/pallas_call | solution.py:569
  122.2 10.9 %all-to-all-done.5 = bf16[16,64,512]{2,1,0:T(8,128)(2,1)} async-done(((bf16[16,64,512]{2,1,0:T(8,128)(2,1)}), bf16[16,64,512]{2,1,0:T(8,128)(2,1)}, u32[]{:S(2)}, u32[]{:S(2)}) %all-to-all-start.5) | async-done | bytes 1048608 | tf_op jit(solution)/shard_map/all_to_all | solution.py:419
  133.2 5.2 all-gather.24.cloned.1.call-done
  144.0 6.4 %all-to-all-start.6 = ((bf16[16,2,1024]{2,1,0:T(2,128)(2,1)}), bf16[16,2,1024]{2,1,0:T(2,128)(2,1)S(1)}, u32[]{:S(2)}, u32[]{:S(2)}) async-start(bf16[16,2,1024]{2,1,0:T(2,128)(2,1)} %reshape.1787), calls=%async_computation.6 | async-start | bytes 131072 | tf_op jit(solution)/shard_map/all_to_all | solution.py:419
  152.0 4.8 all-to-all-done.6
  163.2 17.0 %scores.2 = (bf16[256,3328]{1,0:T(8,128)(2,1)}, f32[256,512]{1,0:T(8,128)}, f32[256,512]{1,0:T(8,128)}, f32[2,8,128]{2,1,0:T(8,128)}) custom-call(s32[1]{0:T(128)} %bitcast.103.mp_ref, f32[1]{0:T(128)} %bitcast.141.inv_ref, bf16[256,512]{1,0:T(8,128)(2,1)} %bitcast.830, bf16[256,512]{1,0:T(8,128)(2,1)} %bitcast.855, ...), custom_call_target="tpu_custom_call" | custom-call | bytes 79200000 | tf_op jit(solution)/shard_map/scores/pallas_call | solution.py:817
  181.2 18.1 %forward.3 = (bf16[8,32,512]{2,1,0:T(8,128)(2,1)}, bf16[8,32,512]{2,1,0:T(8,128)(2,1)}, bf16[8,32,1024]{2,1,0:T(8,128)(2,1)}, f32[2,8,32,512]{3,2,1,0:T(8,128)},...) custom-call(s32[1]{0:T(128)} %bitcast.103.mp_ref, ...), custom_call_target="tpu_custom_call" | custom-call | bytes 64800000 | tf_op jit(solution)/shard_map/forward/pallas_call | solution.py:569
  199.3 17.1 %scores.3 = (bf16[256,3328]{1,0:T(8,128)(2,1)}, f32[256,512]{1,0:T(8,128)}, f32[256,512]{1,0:T(8,128)}, f32[2,8,128]{2,1,0:T(8,128)}) custom-call(s32[1]{0:T(128)} %bitcast.103.mp_ref, f32[1]{0:T(128)} %bitcast.141.inv_ref, bf16[256,512]{1,0:T(8,128)(2,1)} %bitcast.832, bf16[256,512]{1,0:T(8,128)(2,1)} %bitcast.857, ...), custom_call_target="tpu_custom_call" | custom-call | bytes 79200000 | tf_op jit(solution)/shard_map/scores/pallas_call | solution.py:817
  231.4 23.9 %backward.2 = (bf16[4,8,32,512]{3,2,1,0:T(8,128)(2,1)}, bf16[4,8,32,512]{3,2,1,0:T(8,128)(2,1)}, bf16[256,512]{1,0:T(8,128)(2,1)}, bf16[256,512]{1,0:T(8,128)(2,1)}, f32[2,32,512]{2,1,0:T(8,128)}) custom-call(s32[1]{0:T(128)} %bitcast.103.mp_ref, f32[2,8,32,128]{3,2,1,0:T(8,128)} %broadcast_in_dim.484.code_ref, f32[8,32,512]{2,1,0:T(8,128)} %bitcast.838, ...), custom_call_target="tpu_custom_call" | custom-call | bytes 82800000 | tf_op jit(solution)/shard_map/backward/pallas_call | solution.py:684
  281.2 24.0 %backward.3 = (bf16[4,8,32,512]{3,2,1,0:T(8,128)(2,1)}, bf16[4,8,32,512]{3,2,1,0:T(8,128)(2,1)}, bf16[256,512]{1,0:T(8,128)(2,1)}, bf16[256,512]{1,0:T(8,128)(2,1)}, f32[2,32,512]{2,1,0:T(8,128)}) custom-call(s32[1]{0:T(128)} %bitcast.103.mp_ref, f32[2,8,32,128]{3,2,1,0:T(8,128)} %broadcast_in_dim.484.code_ref, f32[8,32,512]{2,1,0:T(8,128)} %bitcast.836, ...), custom_call_target="tpu_custom_call" | custom-call | bytes 82800000 | tf_op jit(solution)/shard_map/backward/pallas_call | solution.py:684
  367.2 5.4 collective-permute-done.33
  373.1 5.1 collective-permute-done.28
  402.6 6.6 %collective-permute-done.58 = bf16[128,512]{1,0:T(8,128)(2,1)S(1)} collective-permute-done((bf16[128,512]{1,0:T(8,128)(2,1)S(1)}, bf16[128,512]{1,0:T(8,128)(2,1)S(1)}, u32[]{:S(2)}, u32[]{:S(2)}) %collective-permute-start.58) | collective-permute-done | bytes 131104 | tf_op jit(solution)/shard_map/ppermute | solution.py:909
  418.7 5.7 %collective-permute-done.39 = bf16[64,512]{1,0:T(8,128)(2,1)S(1)} collective-permute-done((bf16[64,512]{1,0:T(8,128)(2,1)S(1)}, bf16[64,512]{1,0:T(8,128)(2,1)S(1)}, u32[]{:S(2)}, u32[]{:S(2)}) %collective-permute-start.39) | collective-permute-done | bytes 65568 | tf_op jit(solution)/shard_map/ppermute | solution.py:909
  434.0 5.9 %collective-permute-done.48 = bf16[64,1024]{1,0:T(8,128)(2,1)S(1)} collective-permute-done((bf16[64,1024]{1,0:T(8,128)(2,1)S(1)}, bf16[64,1024]{1,0:T(8,128)(2,1)S(1)}, u32[]{:S(2)}, u32[]{:S(2)}) %collective-permute-start.48) | collective-permute-done | bytes 131104 | tf_op jit(solution)/shard_map/ppermute | solution.py:909
  457.1 10.6 %all-to-all-start.9 = ((bf16[16,64,512]{2,1,0:T(8,128)(2,1)}), bf16[16,64,512]{2,1,0:T(8,128)(2,1)}, u32[]{:S(2)}, u32[]{:S(2)}) async-start(bf16[16,64,512]{2,1,0:T(8,128)(2,1)} %add_convert_fusion.2), calls=%async_computation.9 | async-start | bytes 2097152 | tf_op jit(solution)/shard_map/all_to_all | solution.py:419
  468.1 12.9 %collective-permute-start.69 = (f32[1176]{0:T(1024)S(1)}, f32[1176]{0:T(1024)S(1)}, u32[]{:S(2)}, u32[]{:S(2)}) collective-permute-start(f32[1176]{0:T(1024)S(1)} %slice_reduce_fusion.2), channel_id=1, source_target_pairs={{0,1},{1,0},{2,3},{3,2},{4,5},{5,4},{6,7},{7,6},{8,9},{9,8},{10,11... | collective-permute-start | bytes 14120 | tf_op jit(solution)/shard_map/ppermute | solution.py:415
  485.7 6.5 %collective-permute-done.56 = bf16[256,512]{1,0:T(8,128)(2,1)S(1)} collective-permute-done((bf16[256,512]{1,0:T(8,128)(2,1)}, bf16[256,512]{1,0:T(8,128)(2,1)S(1)}, u32[]{:S(2)}, u32[]{:S(2)}) %collective-permute-start.56) | collective-permute-done | bytes 262176 | tf_op jit(solution)/shard_map/ppermute | solution.py:909
  504.9 22.4 %collective-permute-done.51 = bf16[512,1024]{1,0:T(8,128)(2,1)S(1)} collective-permute-done((bf16[512,1024]{1,0:T(8,128)(2,1)S(1)}, bf16[512,1024]{1,0:T(8,128)(2,1)S(1)}, u32[]{:S(2)}, u32[]{:S(2)}) %collective-permute-start.51) | collective-permute-done | bytes 1048608 | tf_op jit(solution)/shard_map/ppermute | solution.py:909
  542.2 9.7 %conditional.1 = (f32[64,500]{1,0:T(8,128)}, f32[64,500]{1,0:T(8,128)}, f32[]{:T(128)}, f32[]{:T(128)}, f32[]{:T(128)}, /*index=5*/f32[]{:T(128)}, f32[1176,500]...) conditional(s32[]{:T(128)} %convert_element_type.991, ...), branch_computations={%region_26.103_spmd, %region_100.104_spmd} | conditional | flops 30975397888 | bytes 1957420800 | solution.py:1336
  544.2 7.8 %unpad.1 = (f32[3,1000,500]{2,1,0:T(8,128)}, f32[3,1000,500]{2,1,0:T(8,128)}) custom-call(s32[6]{0:T(128)} %get-tuple-element.799.sides_ref, bf16[512,1024]{1,0:T(8,128)(2,1)} %get-tuple-element.800.refs_0_, bf16[512,1024]{1,0:T(8,128)(2,1)} %get-tuple-element.801.refs_1_, bf16[512,1024]{1,0:T(8,128)(2,1)} %get-tuple-element.802.refs_2_, ...), custom_call_target="tpu_custom_call" | custom-call | bytes 28800000 | tf_op jit(solution)/shard_map/cond/branch_1_fun/unpad/pallas_call | solution.py:882
  (580 shorter events, 277.2 us)
Async XLA Ops:
  7.2 131.1 %all-gather.24.cloned.1.call-start = ((), (), s32[]{:S(2)}) async-start(), calls=%async_computation.16 | async-start | bytes 6127616 | tf_op jit(solution)/shard_map/all_gather | solution.py:1036
  46.3 37.3 %all-to-all-start.4 = ((bf16[16,64,512]{2,1,0:T(8,128)(2,1)}), bf16[16,64,512]{2,1,0:T(8,128)(2,1)}, u32[]{:S(2)}, u32[]{:S(2)}) async-start(bf16[16,64,512]{2,1,0:T(8,128)(2,1)} %bitcast.826), calls=%async_computation.4 | async-start | bytes 2097152 | tf_op jit(solution)/shard_map/all_to_all | solution.py:419
  58.8 42.6 %collective-permute-start.3 = (bf16[3,2,512,512]{3,2,1,0:T(8,128)(2,1)S(1)}, bf16[3,2,512,512]{3,2,1,0:T(8,128)(2,1)}, u32[]{:S(2)}, u32[]{:S(2)}) collective-permute-start(bf16[3,2,512,512]{3,2,1,0:T(8,128)(2,1)S(1)} %pad_maximum_fusion.4.wi_own), channel_id=1, source_target_pairs={{0,1},{1,0},{2,3},{3,2},{4,5},{5,4},{6,7},{7,6},{8,9},{9,8},{10,11... | collective-permute-start | bytes 9437192 | tf_op jit(solution)/shard_map/ppermute | solution.py:415
  76.3 25.1 %collective-permute-start.4 = (bf16[3,2,512,512]{3,2,1,0:T(8,128)(2,1)}, bf16[3,2,512,512]{3,2,1,0:T(8,128)(2,1)}, u32[]{:S(2)}, u32[]{:S(2)}) collective-permute-start(bf16[3,2,512,512]{3,2,1,0:T(8,128)(2,1)} %pad_maximum_fusion.5.wr_own), channel_id=1, source_target_pairs={{0,1},{1,0},{2,3},{3,2},{4,5},{5,4},{6,7},{7,6},{8,9},{9,8},{10,11... | collective-permute-start | bytes 9437192 | tf_op jit(solution)/shard_map/ppermute | solution.py:415
  87.5 45.6 %all-to-all-start.5 = ((bf16[16,64,512]{2,1,0:T(8,128)(2,1)}), bf16[16,64,512]{2,1,0:T(8,128)(2,1)}, u32[]{:S(2)}, u32[]{:S(2)}) async-start(bf16[16,64,512]{2,1,0:T(8,128)(2,1)} %bitcast.827), calls=%async_computation.5 | async-start | bytes 2097152 | tf_op jit(solution)/shard_map/all_to_all | solution.py:419
  138.3 22.4 %collective-permute-start.8 = (bf16[5632,512]{1,0:T(8,128)(2,1)}, bf16[5632,512]{1,0:T(8,128)(2,1)}, u32[]{:S(2)}, u32[]{:S(2)}) collective-permute-start(bf16[5632,512]{1,0:T(8,128)(2,1)} %all-gather.24.cloned.1.call-done), channel_id=1, source_target_pairs={{0,1},{1,0},{2,3},{3,2},{4,5},{5,4},{6,7},{7,6},{8,9},{9,8},{10,11... | collective-permute-start | bytes 17301512 | tf_op jit(solution)/shard_map/ppermute | solution.py:415
  180.2 40.5 %collective-permute-start.9 = (bf16[256,3328]{1,0:T(8,128)(2,1)}, bf16[256,3328]{1,0:T(8,128)(2,1)S(1)}, u32[]{:S(2)}, u32[]{:S(2)}) collective-permute-start(bf16[256,3328]{1,0:T(8,128)(2,1)} %get-tuple-element.950), channel_id=1, source_target_pairs={{0,1},{1,0},{2,3},{3,2},{4,5},{5,4},{6,7},{7,6},{8,9},{9,8},{10,11... | collective-permute-start | bytes 5111816 | tf_op jit(solution)/shard_map/ppermute | solution.py:415
  227.5 46.2 %collective-permute-start.15 = (bf16[2,2,2,2,80,512]{5,4,2,1,0,3:T(8,128)(2,1)}, bf16[2,2,2,2,80,512]{5,4,2,1,0,3:T(8,128)(2,1)}, u32[]{:S(2)}, u32[]{:S(2)}) collective-permute-start(bf16[2,2,2,2,80,512]{5,4,2,1,0,3:T(8,128)(2,1)} %dynamic-slice_bitcast_fusion.7), channel_id=1, source_target_pairs={{0,4},{2,6},{4,0},{6,2},{8,12},{10,14},{12,8},{14,10},{16,20},{18,... | collective-permute-start | bytes 3932168 | tf_op jit(solution)/shard_map/ppermute | solution.py:909
  229.5 47.6 %collective-permute-start.14 = (bf16[2,2,2,2,96,512]{5,4,2,1,0,3:T(8,128)(2,1)}, bf16[2,2,2,2,96,512]{5,4,2,1,0,3:T(8,128)(2,1)}, u32[]{:S(2)}, u32[]{:S(2)}) collective-permute-start(bf16[2,2,2,2,96,512]{5,4,2,1,0,3:T(8,128)(2,1)} %dynamic-slice_bitcast_fusion.6), channel_id=1, source_target_pairs={{0,2},{2,0},{4,6},{6,4},{8,10},{10,8},{12,14},{14,12},{16,18},{18,... | collective-permute-start | bytes 4718600 | tf_op jit(solution)/shard_map/ppermute | solution.py:909
  256.9 63.8 %collective-permute-start.17 = (bf16[4,8,32,512]{3,2,1,0:T(8,128)(2,1)}, bf16[4,8,32,512]{3,2,1,0:T(8,128)(2,1)}, u32[]{:S(2)}, u32[]{:S(2)}) collective-permute-start(bf16[4,8,32,512]{3,2,1,0:T(8,128)(2,1)} %get-tuple-element.966), channel_id=1, source_target_pairs={{0,1},{1,0},{2,3},{3,2},{4,5},{5,4},{6,7},{7,6},{8,9},{9,8},{10,11... | collective-permute-start | bytes 3145736 | tf_op jit(solution)/shard_map/ppermute | solution.py:415
  268.5 56.3 %all-to-all-start.8 = ((bf16[16,64,512]{2,1,0:T(8,128)(2,1)}), bf16[16,64,512]{2,1,0:T(8,128)(2,1)}, u32[]{:S(2)}, u32[]{:S(2)}) async-start(bf16[16,64,512]{2,1,0:T(8,128)(2,1)} %bitcast.825), calls=%async_computation.8 | async-start | bytes 2097152 | tf_op jit(solution)/shard_map/all_to_all | solution.py:419
  315.9 26.6 %collective-permute-start.22 = (bf16[2,2,2,80,512]{4,3,1,0,2:T(8,128)(2,1)}, bf16[2,2,2,80,512]{4,3,1,0,2:T(8,128)(2,1)}, u32[]{:S(2)}, u32[]{:S(2)}) collective-permute-start(bf16[2,2,2,80,512]{4,3,1,0,2:T(8,128)(2,1)} %dynamic-slice_bitcast_fusion.9), channel_id=1, source_target_pairs={{0,2},{2,0},{4,6},{6,4},{8,10},{10,8},{12,14},{14,12},{16,18},{18,... | collective-permute-start | bytes 1966088 | tf_op jit(solution)/shard_map/ppermute | solution.py:909
  317.4 22.5 %collective-permute-start.20 = (bf16[2,2,2,96,512]{4,3,1,0,2:T(8,128)(2,1)}, bf16[2,2,2,96,512]{4,3,1,0,2:T(8,128)(2,1)}, u32[]{:S(2)}, u32[]{:S(2)}) collective-permute-start(bf16[2,2,2,96,512]{4,3,1,0,2:T(8,128)(2,1)} %dynamic-slice_bitcast_fusion.8), channel_id=1, source_target_pairs={{0,4},{2,6},{4,0},{6,2},{8,12},{10,14},{12,8},{14,10},{16,20},{18,... | collective-permute-start | bytes 2359304 | tf_op jit(solution)/shard_map/ppermute | solution.py:909
  331.4 22.3 %collective-permute-start.27 = (bf16[512,512]{1,0:T(8,128)(2,1)S(1)}, bf16[512,512]{1,0:T(8,128)(2,1)S(1)}, u32[]{:S(2)}, u32[]{:S(2)}) collective-permute-start(bf16[512,512]{1,0:T(8,128)(2,1)S(1)} %constant_dynamic-slice_fusion.30), channel_id=1, source_target_pairs={{0,2},{2,0},{4,6},{6,4},{8,10},{10,8},{12,14},{14,12},{16,18},{18,... | collective-permute-start | bytes 1572872 | tf_op jit(solution)/shard_map/ppermute | solution.py:909
  355.2 24.8 %collective-permute-start.21 = (bf16[2,2,96,512]{3,2,0,1:T(8,128)(2,1)S(1)}, bf16[2,2,96,512]{3,2,0,1:T(8,128)(2,1)S(1)}, u32[]{:S(2)}, u32[]{:S(2)}) collective-permute-start(bf16[2,2,96,512]{3,2,0,1:T(8,128)(2,1)S(1)} %dynamic-slice_bitcast_fusion.10), channel_id=1, source_target_pairs={{0,8},{2,10},{4,12},{6,14},{8,0},{10,2},{12,4},{14,6},{16,24},{18,... | collective-permute-start | bytes 1179656 | tf_op jit(solution)/shard_map/ppermute | solution.py:909
  356.5 22.6 %collective-permute-start.23 = (bf16[2,2,80,512]{3,2,0,1:T(8,128)(2,1)S(1)}, bf16[2,2,80,512]{3,2,0,1:T(8,128)(2,1)S(1)}, u32[]{:S(2)}, u32[]{:S(2)}) collective-permute-start(bf16[2,2,80,512]{3,2,0,1:T(8,128)(2,1)S(1)} %dynamic-slice_bitcast_fusion.11), channel_id=1, source_target_pairs={{0,8},{2,10},{4,12},{6,14},{8,0},{10,2},{12,4},{14,6},{16,24},{18,... | collective-permute-start | bytes 983048 | tf_op jit(solution)/shard_map/ppermute | solution.py:909
  361.3 136.8 %collective-permute-start.68 = (f32[32,512]{1,0:T(8,128)}, f32[32,512]{1,0:T(8,128)}, u32[]{:S(2)}, u32[]{:S(2)}) collective-permute-start(f32[32,512]{1,0:T(8,128)} %get-tuple-element.1944), channel_id=1, source_target_pairs={{0,1},{1,0},{2,3},{3,2},{4,5},{5,4},{6,7},{7,6},{8,9},{9,8},{10,11... | collective-permute-start | bytes 196616 | tf_op jit(solution)/shard_map/ppermute | solution.py:415
  450.2 33.7 %collective-permute-start.50 = (bf16[256,1024]{1,0:T(8,128)(2,1)S(1)}, bf16[256,1024]{1,0:T(8,128)(2,1)}, u32[]{:S(2)}, u32[]{:S(2)}) collective-permute-start(bf16[256,1024]{1,0:T(8,128)(2,1)S(1)} %maximum_select_fusion.3), channel_id=1, source_target_pairs={{0,2},{2,0},{4,6},{6,4},{8,10},{10,8},{12,14},{14,12},{16,18},{18,... | collective-permute-start | bytes 1572872 | tf_op jit(solution)/shard_map/ppermute | solution.py:909
  452.8 28.2 %collective-permute-start.62 = (bf16[256,512]{1,0:T(8,128)(2,1)}, bf16[256,512]{1,0:T(8,128)(2,1)}, u32[]{:S(2)}, u32[]{:S(2)}) collective-permute-start(bf16[256,512]{1,0:T(8,128)(2,1)} %maximum_select_fusion.9), channel_id=1, source_target_pairs={{0,2},{2,0},{4,6},{6,4},{8,10},{10,8},{12,14},{14,12},{16,18},{18,... | collective-permute-start | bytes 786440 | tf_op jit(solution)/shard_map/ppermute | solution.py:909
  455.0 39.9 %collective-permute-start.42 = (bf16[256,1024]{1,0:T(8,128)(2,1)S(1)}, bf16[256,1024]{1,0:T(8,128)(2,1)}, u32[]{:S(2)}, u32[]{:S(2)}) collective-permute-start(bf16[256,1024]{1,0:T(8,128)(2,1)S(1)} %maximum_select_fusion.2), channel_id=1, source_target_pairs={{0,4},{2,6},{4,0},{6,2},{8,12},{10,14},{12,8},{14,10},{16,20},{18,... | collective-permute-start | bytes 1572872 | tf_op jit(solution)/shard_map/ppermute | solution.py:909
  457.1 72.8 %all-to-all-start.9 = ((bf16[16,64,512]{2,1,0:T(8,128)(2,1)}), bf16[16,64,512]{2,1,0:T(8,128)(2,1)}, u32[]{:S(2)}, u32[]{:S(2)}) async-start(bf16[16,64,512]{2,1,0:T(8,128)(2,1)} %add_convert_fusion.2), calls=%async_computation.9 | async-start | bytes 2097152 | tf_op jit(solution)/shard_map/all_to_all | solution.py:419
  468.1 31.9 %collective-permute-start.69 = (f32[1176]{0:T(1024)S(1)}, f32[1176]{0:T(1024)S(1)}, u32[]{:S(2)}, u32[]{:S(2)}) collective-permute-start(f32[1176]{0:T(1024)S(1)} %slice_reduce_fusion.2), channel_id=1, source_target_pairs={{0,1},{1,0},{2,3},{3,2},{4,5},{5,4},{6,7},{7,6},{8,9},{9,8},{10,11... | collective-permute-start | bytes 14120 | tf_op jit(solution)/shard_map/ppermute | solution.py:415
  492.2 35.1 %collective-permute-start.51 = (bf16[512,1024]{1,0:T(8,128)(2,1)S(1)}, bf16[512,1024]{1,0:T(8,128)(2,1)S(1)}, u32[]{:S(2)}, u32[]{:S(2)}) collective-permute-start(bf16[512,1024]{1,0:T(8,128)(2,1)S(1)} %maximum_select_fusion.1), channel_id=1, source_target_pairs={{0,4},{2,6},{4,0},{6,2},{8,12},{10,14},{12,8},{14,10},{16,20},{18,... | collective-permute-start | bytes 3145736 | tf_op jit(solution)/shard_map/ppermute | solution.py:909
  498.1 29.9 %collective-permute-start.43 = (bf16[512,1024]{1,0:T(8,128)(2,1)S(1)}, bf16[512,1024]{1,0:T(8,128)(2,1)S(1)}, u32[]{:S(2)}, u32[]{:S(2)}) collective-permute-start(bf16[512,1024]{1,0:T(8,128)(2,1)S(1)} %maximum_select_fusion), channel_id=1, source_target_pairs={{0,2},{2,0},{4,6},{6,4},{8,10},{10,8},{12,14},{14,12},{16,18},{18,... | collective-permute-start | bytes 3145736 | tf_op jit(solution)/shard_map/ppermute | solution.py:909
  (131 other events, 1510.4 us)
Sparse Core Ops, SparseCore 0:
  15.5 122.8 all-gather.23

commit v3 on v2

--- a/solution.py
+++ b/solution.py
@@ -1083,7 +1083,6 @@
     item_hot = one_hot(slots_first, devices * capacity)
     emb_own = dot_f32(item_hot, item_rows).astype(low)
     emb_oth = swap_cores(emb_own)
-    target_rows = exchange(after(target_send, emb_own)).reshape(devices * capacity, width)
     emb_own = emb_own.reshape(2, blocks, events, width)
     emb_oth = emb_oth.reshape(2, blocks, events, width)
     inputs = jnp.concatenate(
@@ -1094,9 +1093,6 @@
         axis=1,
     )
 
-    target_slot_blocks = target_slot.reshape(2, blocks, events).transpose(1, 0, 2)
-    target_hot = one_hot(target_slot_blocks.reshape(blocks * batch), devices * capacity)
-    tgt_own = dot_f32(target_hot, target_rows).astype(low)
     hop = -(-slots // devices)
     saves = []
     outs = []
@@ -1124,7 +1120,6 @@
             flat = jnp.where(lanes == half + 1, 1.0, flat).astype(low)
             put = (jnp.arange(devices * hop)[:, None] == position[None, :]).astype(low)
             sent = dot_f32(put, flat).astype(low).reshape(devices, hop, 2 * width)
-            sent = after(sent, target_rows)
             came = exchange(sent).reshape(devices * hop, 2 * width)
             both = jnp.concatenate([came, swap_cores(came)], axis=0)
             label = jnp.where(both[:, half + 1] > 0.5, both[:, half].astype(f32), -1.0)
@@ -1132,14 +1127,22 @@
             take = (here[:, None] == label[None, :]).astype(low)
             moved = dot_f32(take, both) * lane_real
             state = moved.reshape(slots, 2, width).transpose(1, 0, 2)
-            state = after(state, tgt_own)
-            neg_own = after(neg_own, sent)
-            outs[block] = after(outs[block], state)
+            if block == 0:
+                target_send = after(target_send, state)
+                state = after(state, target_send)
+                target_rows = exchange(target_send)
+                target_rows = target_rows.reshape(devices * capacity, width)
+                neg_own = after(neg_own, state)
             routes.append((label[: devices * hop], put))
 
+    target_slot_blocks = target_slot.reshape(2, blocks, events).transpose(1, 0, 2)
+    target_hot = one_hot(target_slot_blocks.reshape(blocks * batch), devices * capacity)
     neg_oth = swap_cores(neg_own)
+    outs[-1] = after(outs[-1], neg_oth)
+    outs[:-1] = after(outs[:-1], outs[-1])
+    target_rows = after(target_rows, outs[-1])
+    tgt_own = dot_f32(target_hot, target_rows).astype(low)
     tgt_oth = swap_cores(tgt_own).reshape(blocks, batch, width)
-    outs[-1] = after(outs[-1], neg_oth, tgt_oth)
     neg_oth = neg_oth.reshape(devices, blocks, neg_capacity, width)
     neg_own = neg_own.reshape(devices, blocks, neg_capacity, width)
     tgt_own = tgt_own.reshape(blocks, batch, width)

time: 574 us -> 562 us (0.979)
  waiting for transfers between devices: 128 us -> 121 us
  transfers between devices with their start and end apart: 77 -> 77, of which waited for: 39 -> 37; matrix products, arithmetic and copies ran while one was open for 23% -> 23% of each run, Pallas kernels for 18% -> 18%
where the time goes in v3:
time: 562 us; the launch traced here: 553 us
  Pallas kernels  126 us (22%)
  starting transfers between devices  124 us (22%)
  waiting for transfers between devices  121 us (22%)
  matrix products  55.5 us (10%)
  other arithmetic  48.2 us (9%)
  local copies, waits for them, and re-layouts  45.2 us (8%)
  between operations  32.1 us (6%)
    ppermute x48, waiting for transfers between devices, flip(): lax.ppermute(values, 'dp', [(i, i ^ 1 << bit) for i in range(devices)])  96.1 us
    pallas_call x2, Pallas kernels, run_backward(): pl.pallas_call(functools.partial(backward_kernel, half), grid_spec=pltpu....  47.9 us
    all_to_all x7, starting transfers between devices, exchange(): return lax.all_to_all(values, 'dp', split_axis=0, concat_axis=0, tiled=True)  46.1 us
    ppermute x48, starting transfers between devices, flip(): lax.ppermute(values, 'dp', [(i, i ^ 1 << bit) for i in range(devices)])  44.8 us
    pallas_call x2, Pallas kernels, run_forward(): pl.pallas_call(functools.partial(forward_kernel, half), grid_spec=pltpu.P...  36.4 us
    dot_general x18, matrix products, dot_first(): lax.dot_general(left, right, (((0,), (0,)), ((), ())), preferred_element_...  35.1 us
    pallas_call x2, Pallas kernels, run_scores(): pl.pallas_call(functools.partial(score_kernel, half), grid_spec=pltpu.Pre...  34.1 us
    ppermute x21, starting transfers between devices, swap_cores(): return lax.ppermute(values, 'mp', [(0, 1), (1, 0)])  32.6 us
  transfers between devices with their start and end apart: 77, of which 37 were waited for; matrix products, arithmetic and copies ran while one was open for 23% of the time, Pallas kernels for 18%

profile of v3, /device:TPU:1, one launch (start us, length us, event | category | flops | bytes accessed | tf_op | source)
XLA Modules:
  0.0 553.4 jit_solution(13365155120291131826)
XLA Ops:
  28.5 7.4 %all-to-all-start.3 = ((s32[16,1,130]{2,1,0:T(1,128)}), s32[16,1,130]{2,1,0:T(1,128)S(1)}, u32[]{:S(2)}, u32[]{:S(2)}) async-start(s32[16,1,130]{2,1,0:T(1,128)} %copy.310), calls=%async_computation.3 | async-start | bytes 32768 | tf_op jit(solution)/shard_map/all_to_all | solution.py:419
  37.0 5.1 all-to-all-done.3
  46.3 4.5 all-to-all-start.4
  91.8 18.3 %forward.2 = (bf16[8,32,512]{2,1,0:T(8,128)(2,1)}, bf16[8,32,512]{2,1,0:T(8,128)(2,1)}, bf16[8,32,1024]{2,1,0:T(8,128)(2,1)}, f32[2,8,32,512]{3,2,1,0:T(8,128)},...) custom-call(s32[1]{0:T(128)} %bitcast.103.mp_ref, ...), custom_call_target="tpu_custom_call" | custom-call | bytes 64800000 | tf_op jit(solution)/shard_map/forward/pallas_call | solution.py:569
  111.9 6.9 %all-to-all-start.5 = ((bf16[16,2,1024]{2,1,0:T(2,128)(2,1)}), bf16[16,2,1024]{2,1,0:T(2,128)(2,1)S(1)}, u32[]{:S(2)}, u32[]{:S(2)}) async-start(bf16[16,2,1024]{2,1,0:T(2,128)(2,1)} %reshape.1787), calls=%async_computation.5 | async-start | bytes 131072 | tf_op jit(solution)/shard_map/all_to_all | solution.py:419
  134.9 18.1 %forward.3 = (bf16[8,32,512]{2,1,0:T(8,128)(2,1)}, bf16[8,32,512]{2,1,0:T(8,128)(2,1)}, bf16[8,32,1024]{2,1,0:T(8,128)(2,1)}, f32[2,8,32,512]{3,2,1,0:T(8,128)},...) custom-call(s32[1]{0:T(128)} %bitcast.103.mp_ref, ...), custom_call_target="tpu_custom_call" | custom-call | bytes 64800000 | tf_op jit(solution)/shard_map/forward/pallas_call | solution.py:569
  164.8 17.0 %scores.2 = (bf16[256,3328]{1,0:T(8,128)(2,1)}, f32[256,512]{1,0:T(8,128)}, f32[256,512]{1,0:T(8,128)}, f32[2,8,128]{2,1,0:T(8,128)}) custom-call(s32[1]{0:T(128)} %bitcast.103.mp_ref, f32[1]{0:T(128)} %bitcast.139.inv_ref, bf16[256,512]{1,0:T(8,128)(2,1)} %bitcast.828, bf16[256,512]{1,0:T(8,128)(2,1)} %bitcast.853, ...), custom_call_target="tpu_custom_call" | custom-call | bytes 79200000 | tf_op jit(solution)/shard_map/scores/pallas_call | solution.py:817
  182.8 17.1 %scores.3 = (bf16[256,3328]{1,0:T(8,128)(2,1)}, f32[256,512]{1,0:T(8,128)}, f32[256,512]{1,0:T(8,128)}, f32[2,8,128]{2,1,0:T(8,128)}) custom-call(s32[1]{0:T(128)} %bitcast.103.mp_ref, f32[1]{0:T(128)} %bitcast.139.inv_ref, bf16[256,512]{1,0:T(8,128)(2,1)} %bitcast.830, bf16[256,512]{1,0:T(8,128)(2,1)} %bitcast.855, ...), custom_call_target="tpu_custom_call" | custom-call | bytes 79200000 | tf_op jit(solution)/shard_map/scores/pallas_call | solution.py:817
  215.9 23.9 %backward.2 = (bf16[4,8,32,512]{3,2,1,0:T(8,128)(2,1)}, bf16[4,8,32,512]{3,2,1,0:T(8,128)(2,1)}, bf16[256,512]{1,0:T(8,128)(2,1)}, bf16[256,512]{1,0:T(8,128)(2,1)}, f32[2,32,512]{2,1,0:T(8,128)}) custom-call(s32[1]{0:T(128)} %bitcast.103.mp_ref, f32[2,8,32,128]{3,2,1,0:T(8,128)} %broadcast_in_dim.484.code_ref, f32[8,32,512]{2,1,0:T(8,128)} %bitcast.836, ...), custom_call_target="tpu_custom_call" | custom-call | bytes 82800000 | tf_op jit(solution)/shard_map/backward/pallas_call | solution.py:684
  243.3 5.8 %all-to-all-start.7 = ((bf16[16,2,1024]{2,1,0:T(2,128)(2,1)}), bf16[16,2,1024]{2,1,0:T(2,128)(2,1)S(1)}, u32[]{:S(2)}, u32[]{:S(2)}) async-start(bf16[16,2,1024]{2,1,0:T(2,128)(2,1)} %reshape.1812), calls=%async_computation.7 | async-start | bytes 131072 | tf_op jit(solution)/shard_map/all_to_all | solution.py:419
  268.3 24.0 %backward.3 = (bf16[4,8,32,512]{3,2,1,0:T(8,128)(2,1)}, bf16[4,8,32,512]{3,2,1,0:T(8,128)(2,1)}, bf16[256,512]{1,0:T(8,128)(2,1)}, bf16[256,512]{1,0:T(8,128)(2,1)}, f32[2,32,512]{2,1,0:T(8,128)}) custom-call(s32[1]{0:T(128)} %bitcast.103.mp_ref, f32[2,8,32,128]{3,2,1,0:T(8,128)} %broadcast_in_dim.484.code_ref, f32[8,32,512]{2,1,0:T(8,128)} %bitcast.834, ...), custom_call_target="tpu_custom_call" | custom-call | bytes 82800000 | tf_op jit(solution)/shard_map/backward/pallas_call | solution.py:684
  355.7 4.6 collective-permute-done.33
  360.8 5.1 collective-permute-done.28
  390.3 6.6 %collective-permute-done.58 = bf16[128,512]{1,0:T(8,128)(2,1)S(1)} collective-permute-done((bf16[128,512]{1,0:T(8,128)(2,1)S(1)}, bf16[128,512]{1,0:T(8,128)(2,1)S(1)}, u32[]{:S(2)}, u32[]{:S(2)}) %collective-permute-start.58) | collective-permute-done | bytes 131104 | tf_op jit(solution)/shard_map/ppermute | solution.py:909
  406.4 5.7 %collective-permute-done.39 = bf16[64,512]{1,0:T(8,128)(2,1)S(1)} collective-permute-done((bf16[64,512]{1,0:T(8,128)(2,1)S(1)}, bf16[64,512]{1,0:T(8,128)(2,1)S(1)}, u32[]{:S(2)}, u32[]{:S(2)}) %collective-permute-start.39) | collective-permute-done | bytes 65568 | tf_op jit(solution)/shard_map/ppermute | solution.py:909
  421.7 5.9 %collective-permute-done.48 = bf16[64,1024]{1,0:T(8,128)(2,1)S(1)} collective-permute-done((bf16[64,1024]{1,0:T(8,128)(2,1)S(1)}, bf16[64,1024]{1,0:T(8,128)(2,1)S(1)}, u32[]{:S(2)}, u32[]{:S(2)}) %collective-permute-start.48) | collective-permute-done | bytes 131104 | tf_op jit(solution)/shard_map/ppermute | solution.py:909
  444.8 13.0 %all-to-all-start.9 = ((bf16[16,64,512]{2,1,0:T(8,128)(2,1)}), bf16[16,64,512]{2,1,0:T(8,128)(2,1)}, u32[]{:S(2)}, u32[]{:S(2)}) async-start(bf16[16,64,512]{2,1,0:T(8,128)(2,1)} %add_convert_fusion.2), calls=%async_computation.9 | async-start | bytes 2097152 | tf_op jit(solution)/shard_map/all_to_all | solution.py:419
  458.2 8.8 %collective-permute-start.69 = (f32[1176]{0:T(1024)S(1)}, f32[1176]{0:T(1024)S(1)}, u32[]{:S(2)}, u32[]{:S(2)}) collective-permute-start(f32[1176]{0:T(1024)S(1)} %slice_reduce_fusion.2), channel_id=1, source_target_pairs={{0,1},{1,0},{2,3},{3,2},{4,5},{5,4},{6,7},{7,6},{8,9},{9,8},{10,11... | collective-permute-start | bytes 14120 | tf_op jit(solution)/shard_map/ppermute | solution.py:415
  471.8 9.6 %collective-permute-done.56 = bf16[256,512]{1,0:T(8,128)(2,1)S(1)} collective-permute-done((bf16[256,512]{1,0:T(8,128)(2,1)}, bf16[256,512]{1,0:T(8,128)(2,1)S(1)}, u32[]{:S(2)}, u32[]{:S(2)}) %collective-permute-start.56) | collective-permute-done | bytes 262176 | tf_op jit(solution)/shard_map/ppermute | solution.py:909
  488.8 4.6 collective-permute-done.63
  493.7 22.1 %collective-permute-done.51 = bf16[512,1024]{1,0:T(8,128)(2,1)S(1)} collective-permute-done((bf16[512,1024]{1,0:T(8,128)(2,1)S(1)}, bf16[512,1024]{1,0:T(8,128)(2,1)S(1)}, u32[]{:S(2)}, u32[]{:S(2)}) %collective-permute-start.51) | collective-permute-done | bytes 1048608 | tf_op jit(solution)/shard_map/ppermute | solution.py:909
  522.8 4.5 fusion.193
  530.6 9.7 %conditional.1 = (f32[64,500]{1,0:T(8,128)}, f32[64,500]{1,0:T(8,128)}, f32[]{:T(128)}, f32[]{:T(128)}, f32[]{:T(128)}, /*index=5*/f32[]{:T(128)}, f32[1176,500]...) conditional(s32[]{:T(128)} %convert_element_type.991, ...), branch_computations={%region_26.103_spmd, %region_100.104_spmd} | conditional | flops 30975397888 | bytes 1957420800 | solution.py:1339
  532.6 7.8 %unpad.1 = (f32[3,1000,500]{2,1,0:T(8,128)}, f32[3,1000,500]{2,1,0:T(8,128)}) custom-call(s32[6]{0:T(128)} %get-tuple-element.799.sides_ref, bf16[512,1024]{1,0:T(8,128)(2,1)} %get-tuple-element.800.refs_0_, bf16[512,1024]{1,0:T(8,128)(2,1)} %get-tuple-element.801.refs_1_, bf16[512,1024]{1,0:T(8,128)(2,1)} %get-tuple-element.802.refs_2_, ...), custom_call_target="tpu_custom_call" | custom-call | bytes 28800000 | tf_op jit(solution)/shard_map/cond/branch_1_fun/unpad/pallas_call | solution.py:882
  (578 shorter events, 272.9 us)
Async XLA Ops:
  7.2 121.9 %all-gather.24.cloned.1.call-start = ((), (), s32[]{:S(2)}) async-start(), calls=%async_computation.16 | async-start | bytes 6127616 | tf_op jit(solution)/shard_map/all_gather | solution.py:1036
  46.3 37.4 %all-to-all-start.4 = ((bf16[16,64,512]{2,1,0:T(8,128)(2,1)}), bf16[16,64,512]{2,1,0:T(8,128)(2,1)}, u32[]{:S(2)}, u32[]{:S(2)}) async-start(bf16[16,64,512]{2,1,0:T(8,128)(2,1)} %bitcast.824), calls=%async_computation.4 | async-start | bytes 2097152 | tf_op jit(solution)/shard_map/all_to_all | solution.py:419
  57.8 33.2 %collective-permute-start.3 = (bf16[3,2,512,512]{3,2,1,0:T(8,128)(2,1)S(1)}, bf16[3,2,512,512]{3,2,1,0:T(8,128)(2,1)}, u32[]{:S(2)}, u32[]{:S(2)}) collective-permute-start(bf16[3,2,512,512]{3,2,1,0:T(8,128)(2,1)S(1)} %pad_maximum_fusion.4.wi_own), channel_id=1, source_target_pairs={{0,1},{1,0},{2,3},{3,2},{4,5},{5,4},{6,7},{7,6},{8,9},{9,8},{10,11... | collective-permute-start | bytes 9437192 | tf_op jit(solution)/shard_map/ppermute | solution.py:415
  129.1 23.9 %collective-permute-start.7 = (bf16[5632,512]{1,0:T(8,128)(2,1)}, bf16[5632,512]{1,0:T(8,128)(2,1)}, u32[]{:S(2)}, u32[]{:S(2)}) collective-permute-start(bf16[5632,512]{1,0:T(8,128)(2,1)} %all-gather.24.cloned.1.call-done), channel_id=1, source_target_pairs={{0,1},{1,0},{2,3},{3,2},{4,5},{5,4},{6,7},{7,6},{8,9},{9,8},{10,11... | collective-permute-start | bytes 17301512 | tf_op jit(solution)/shard_map/ppermute | solution.py:415
  129.5 26.8 %all-to-all-start.6 = ((bf16[16,64,512]{2,1,0:T(8,128)(2,1)}), bf16[16,64,512]{2,1,0:T(8,128)(2,1)S(1)}, u32[]{:S(2)}, u32[]{:S(2)}) async-start(bf16[16,64,512]{2,1,0:T(8,128)(2,1)} %bitcast.137), calls=%async_computation.6 | async-start | bytes 2097152 | tf_op jit(solution)/shard_map/all_to_all | solution.py:419
  181.7 22.4 %collective-permute-start.9 = (bf16[256,3328]{1,0:T(8,128)(2,1)}, bf16[256,3328]{1,0:T(8,128)(2,1)S(1)}, u32[]{:S(2)}, u32[]{:S(2)}) collective-permute-start(bf16[256,3328]{1,0:T(8,128)(2,1)} %get-tuple-element.950), channel_id=1, source_target_pairs={{0,1},{1,0},{2,3},{3,2},{4,5},{5,4},{6,7},{7,6},{8,9},{9,8},{10,11... | collective-permute-start | bytes 5111816 | tf_op jit(solution)/shard_map/ppermute | solution.py:415
  211.0 49.8 %collective-permute-start.15 = (bf16[2,2,2,2,80,512]{5,4,2,1,0,3:T(8,128)(2,1)}, bf16[2,2,2,2,80,512]{5,4,2,1,0,3:T(8,128)(2,1)}, u32[]{:S(2)}, u32[]{:S(2)}) collective-permute-start(bf16[2,2,2,2,80,512]{5,4,2,1,0,3:T(8,128)(2,1)} %dynamic-slice_bitcast_fusion.7), channel_id=1, source_target_pairs={{0,4},{2,6},{4,0},{6,2},{8,12},{10,14},{12,8},{14,10},{16,20},{18,... | collective-permute-start | bytes 3932168 | tf_op jit(solution)/shard_map/ppermute | solution.py:909
  214.0 50.2 %collective-permute-start.14 = (bf16[2,2,2,2,96,512]{5,4,2,1,0,3:T(8,128)(2,1)}, bf16[2,2,2,2,96,512]{5,4,2,1,0,3:T(8,128)(2,1)}, u32[]{:S(2)}, u32[]{:S(2)}) collective-permute-start(bf16[2,2,2,2,96,512]{5,4,2,1,0,3:T(8,128)(2,1)} %dynamic-slice_bitcast_fusion.6), channel_id=1, source_target_pairs={{0,2},{2,0},{4,6},{6,4},{8,10},{10,8},{12,14},{14,12},{16,18},{18,... | collective-permute-start | bytes 4718600 | tf_op jit(solution)/shard_map/ppermute | solution.py:909
  241.7 65.1 %collective-permute-start.17 = (bf16[4,8,32,512]{3,2,1,0:T(8,128)(2,1)}, bf16[4,8,32,512]{3,2,1,0:T(8,128)(2,1)}, u32[]{:S(2)}, u32[]{:S(2)}) collective-permute-start(bf16[4,8,32,512]{3,2,1,0:T(8,128)(2,1)} %get-tuple-element.966), channel_id=1, source_target_pairs={{0,1},{1,0},{2,3},{3,2},{4,5},{5,4},{6,7},{7,6},{8,9},{9,8},{10,11... | collective-permute-start | bytes 3145736 | tf_op jit(solution)/shard_map/ppermute | solution.py:415
  255.5 55.4 %all-to-all-start.8 = ((bf16[16,64,512]{2,1,0:T(8,128)(2,1)}), bf16[16,64,512]{2,1,0:T(8,128)(2,1)}, u32[]{:S(2)}, u32[]{:S(2)}) async-start(bf16[16,64,512]{2,1,0:T(8,128)(2,1)} %bitcast.823), calls=%async_computation.8 | async-start | bytes 2097152 | tf_op jit(solution)/shard_map/all_to_all | solution.py:419
  294.1 22.4 %collective-permute-start.6 = (bf16[512,1024]{1,0:T(8,128)(2,1)S(1)}, bf16[512,1024]{1,0:T(8,128)(2,1)}, u32[]{:S(2)}, u32[]{:S(2)}) collective-permute-start(bf16[512,1024]{1,0:T(8,128)(2,1)S(1)} %pad_maximum_fusion.10), channel_id=1, source_target_pairs={{0,1},{1,0},{2,3},{3,2},{4,5},{5,4},{6,7},{7,6},{8,9},{9,8},{10,11... | collective-permute-start | bytes 3145736 | tf_op jit(solution)/shard_map/ppermute | solution.py:415
  303.0 28.6 %collective-permute-start.22 = (bf16[2,2,2,80,512]{4,3,1,0,2:T(8,128)(2,1)}, bf16[2,2,2,80,512]{4,3,1,0,2:T(8,128)(2,1)}, u32[]{:S(2)}, u32[]{:S(2)}) collective-permute-start(bf16[2,2,2,80,512]{4,3,1,0,2:T(8,128)(2,1)} %dynamic-slice_bitcast_fusion.9), channel_id=1, source_target_pairs={{0,2},{2,0},{4,6},{6,4},{8,10},{10,8},{12,14},{14,12},{16,18},{18,... | collective-permute-start | bytes 1966088 | tf_op jit(solution)/shard_map/ppermute | solution.py:909
  304.5 24.5 %collective-permute-start.20 = (bf16[2,2,2,96,512]{4,3,1,0,2:T(8,128)(2,1)}, bf16[2,2,2,96,512]{4,3,1,0,2:T(8,128)(2,1)}, u32[]{:S(2)}, u32[]{:S(2)}) collective-permute-start(bf16[2,2,2,96,512]{4,3,1,0,2:T(8,128)(2,1)} %dynamic-slice_bitcast_fusion.8), channel_id=1, source_target_pairs={{0,4},{2,6},{4,0},{6,2},{8,12},{10,14},{12,8},{14,10},{16,20},{18,... | collective-permute-start | bytes 2359304 | tf_op jit(solution)/shard_map/ppermute | solution.py:909
  319.1 23.7 %collective-permute-start.27 = (bf16[512,512]{1,0:T(8,128)(2,1)S(1)}, bf16[512,512]{1,0:T(8,128)(2,1)S(1)}, u32[]{:S(2)}, u32[]{:S(2)}) collective-permute-start(bf16[512,512]{1,0:T(8,128)(2,1)S(1)} %constant_dynamic-slice_fusion.30), channel_id=1, source_target_pairs={{0,2},{2,0},{4,6},{6,4},{8,10},{10,8},{12,14},{14,12},{16,18},{18,... | collective-permute-start | bytes 1572872 | tf_op jit(solution)/shard_map/ppermute | solution.py:909
  343.2 24.5 %collective-permute-start.21 = (bf16[2,2,96,512]{3,2,0,1:T(8,128)(2,1)S(1)}, bf16[2,2,96,512]{3,2,0,1:T(8,128)(2,1)S(1)}, u32[]{:S(2)}, u32[]{:S(2)}) collective-permute-start(bf16[2,2,96,512]{3,2,0,1:T(8,128)(2,1)S(1)} %dynamic-slice_bitcast_fusion.10), channel_id=1, source_target_pairs={{0,8},{2,10},{4,12},{6,14},{8,0},{10,2},{12,4},{14,6},{16,24},{18,... | collective-permute-start | bytes 1179656 | tf_op jit(solution)/shard_map/ppermute | solution.py:909
  349.0 137.2 %collective-permute-start.68 = (f32[32,512]{1,0:T(8,128)}, f32[32,512]{1,0:T(8,128)}, u32[]{:S(2)}, u32[]{:S(2)}) collective-permute-start(f32[32,512]{1,0:T(8,128)} %get-tuple-element.1944), channel_id=1, source_target_pairs={{0,1},{1,0},{2,3},{3,2},{4,5},{5,4},{6,7},{7,6},{8,9},{9,8},{10,11... | collective-permute-start | bytes 196616 | tf_op jit(solution)/shard_map/ppermute | solution.py:415
  437.9 32.1 %collective-permute-start.50 = (bf16[256,1024]{1,0:T(8,128)(2,1)S(1)}, bf16[256,1024]{1,0:T(8,128)(2,1)}, u32[]{:S(2)}, u32[]{:S(2)}) collective-permute-start(bf16[256,1024]{1,0:T(8,128)(2,1)S(1)} %maximum_select_fusion.3), channel_id=1, source_target_pairs={{0,2},{2,0},{4,6},{6,4},{8,10},{10,8},{12,14},{14,12},{16,18},{18,... | collective-permute-start | bytes 1572872 | tf_op jit(solution)/shard_map/ppermute | solution.py:909
  440.5 26.5 %collective-permute-start.62 = (bf16[256,512]{1,0:T(8,128)(2,1)}, bf16[256,512]{1,0:T(8,128)(2,1)}, u32[]{:S(2)}, u32[]{:S(2)}) collective-permute-start(bf16[256,512]{1,0:T(8,128)(2,1)} %maximum_select_fusion.9), channel_id=1, source_target_pairs={{0,2},{2,0},{4,6},{6,4},{8,10},{10,8},{12,14},{14,12},{16,18},{18,... | collective-permute-start | bytes 786440 | tf_op jit(solution)/shard_map/ppermute | solution.py:909
  442.7 40.6 %collective-permute-start.42 = (bf16[256,1024]{1,0:T(8,128)(2,1)S(1)}, bf16[256,1024]{1,0:T(8,128)(2,1)}, u32[]{:S(2)}, u32[]{:S(2)}) collective-permute-start(bf16[256,1024]{1,0:T(8,128)(2,1)S(1)} %maximum_select_fusion.2), channel_id=1, source_target_pairs={{0,4},{2,6},{4,0},{6,2},{8,12},{10,14},{12,8},{14,10},{16,20},{18,... | collective-permute-start | bytes 1572872 | tf_op jit(solution)/shard_map/ppermute | solution.py:909
  444.8 73.6 %all-to-all-start.9 = ((bf16[16,64,512]{2,1,0:T(8,128)(2,1)}), bf16[16,64,512]{2,1,0:T(8,128)(2,1)}, u32[]{:S(2)}, u32[]{:S(2)}) async-start(bf16[16,64,512]{2,1,0:T(8,128)(2,1)} %add_convert_fusion.2), calls=%async_computation.9 | async-start | bytes 2097152 | tf_op jit(solution)/shard_map/all_to_all | solution.py:419
  458.2 30.0 %collective-permute-start.69 = (f32[1176]{0:T(1024)S(1)}, f32[1176]{0:T(1024)S(1)}, u32[]{:S(2)}, u32[]{:S(2)}) collective-permute-start(f32[1176]{0:T(1024)S(1)} %slice_reduce_fusion.2), channel_id=1, source_target_pairs={{0,1},{1,0},{2,3},{3,2},{4,5},{5,4},{6,7},{7,6},{8,9},{9,8},{10,11... | collective-permute-start | bytes 14120 | tf_op jit(solution)/shard_map/ppermute | solution.py:415
  470.0 23.3 %collective-permute-start.63 = (bf16[512,512]{1,0:T(8,128)(2,1)S(1)}, bf16[512,512]{1,0:T(8,128)(2,1)S(1)}, u32[]{:S(2)}, u32[]{:S(2)}) collective-permute-start(bf16[512,512]{1,0:T(8,128)(2,1)S(1)} %maximum_select_fusion.5), channel_id=1, source_target_pairs={{0,4},{2,6},{4,0},{6,2},{8,12},{10,14},{12,8},{14,10},{16,20},{18,... | collective-permute-start | bytes 1572872 | tf_op jit(solution)/shard_map/ppermute | solution.py:909
  481.4 34.4 %collective-permute-start.51 = (bf16[512,1024]{1,0:T(8,128)(2,1)S(1)}, bf16[512,1024]{1,0:T(8,128)(2,1)S(1)}, u32[]{:S(2)}, u32[]{:S(2)}) collective-permute-start(bf16[512,1024]{1,0:T(8,128)(2,1)S(1)} %maximum_select_fusion.1), channel_id=1, source_target_pairs={{0,4},{2,6},{4,0},{6,2},{8,12},{10,14},{12,8},{14,10},{16,20},{18,... | collective-permute-start | bytes 3145736 | tf_op jit(solution)/shard_map/ppermute | solution.py:909
  486.3 30.3 %collective-permute-start.43 = (bf16[512,1024]{1,0:T(8,128)(2,1)S(1)}, bf16[512,1024]{1,0:T(8,128)(2,1)S(1)}, u32[]{:S(2)}, u32[]{:S(2)}) collective-permute-start(bf16[512,1024]{1,0:T(8,128)(2,1)S(1)} %maximum_select_fusion), channel_id=1, source_target_pairs={{0,2},{2,0},{4,6},{6,4},{8,10},{10,8},{12,14},{14,12},{16,18},{18,... | collective-permute-start | bytes 3145736 | tf_op jit(solution)/shard_map/ppermute | solution.py:909
  (130 other events, 1517.7 us)
Sparse Core Ops, SparseCore 0:
  15.5 104.3 all-gather.23

commit v4 on v3

--- a/solution.py
+++ b/solution.py
@@ -499,9 +499,8 @@
     own = own_ref[...]
     oth = oth_ref[...]
     state[...] = start_ref[...]
-    copies[0].wait()
-    copies[1].wait()
-    for side in range(2):
+    for side, copy in ((me, copies[0]), (other, copies[1])):
+        copy.wait()
         for gate in range(3):
             value = dot_f32(own, wi[side, gate, me]) + dot_f32(oth, wi[side, gate, other])
             pre[side, gate] = value.reshape(steps, slots, width)
@@ -743,7 +742,7 @@
     ids = scores[events : events + 1, :]
     usable = jnp.concatenate([use_ref[:1, :], scores[events + 1 : events + 2, batch:]], axis=1)
     ids = jnp.where(usable > 0.5, ids, -1.0)
-    group = 16
+    group = 64
     inv = inv_ref[0]
     base = me * events
 
@@ -790,8 +789,8 @@
 
     zero = jnp.zeros((group, 1), jnp.float32)
     loss_sum, square_sum = lax.fori_loop(0, events // group, rows_step, (zero, zero))
-    stat_ref[0] = jnp.broadcast_to(loss_sum[:8] + loss_sum[8:], (8, 128))
-    stat_ref[1] = jnp.broadcast_to(square_sum[:8] + square_sum[8:], (8, 128))
+    stat_ref[0] = jnp.broadcast_to(sum(loss_sum[i : i + 8] for i in range(0, group, 8)), (8, 128))
+    stat_ref[1] = jnp.broadcast_to(sum(square_sum[i : i + 8] for i in range(0, group, 8)), (8, 128))
     grad_tgt = grad_ref[:, :batch]
     grad_neg = grad_ref[:, batch:]
     real = lax.broadcasted_iota(jnp.int32, (events, width), 1) < half
@@ -924,7 +923,7 @@
 def scatter_sum(chunks, orders, owner_sums):
     parts = list(chunks)
     for level in range(len(orders[0])):
-        if level >= 2:
+        if level == 2:
             arrived = [value.came for value in owner_sums]
             parts = [after(part, arrived) for part in parts]
         sends = []

time: 562 us -> 546 us (0.972)
  starting transfers between devices: 124 us -> 114 us
    all_to_all x7, starting transfers between devices: 46.1 us -> 37.4 us  [exchange(): return lax.all_to_all(values, 'dp', split_axis=0, concat_axis=0, tiled=True)]
  transfers between devices with their start and end apart: 77 -> 77, of which waited for: 37 -> 35; matrix products, arithmetic and copies ran while one was open for 23% -> 24% of each run, Pallas kernels for 18% -> 18%
where the time goes in v4:
time: 546 us; the launch traced here: 538 us
  Pallas kernels  122 us (22%)
  waiting for transfers between devices  118 us (22%)
  starting transfers between devices  114 us (21%)
  matrix products  55.6 us (10%)
  other arithmetic  48.2 us (9%)
  local copies, waits for them, and re-layouts  45.2 us (8%)
  between operations  32.2 us (6%)
    ppermute x48, waiting for transfers between devices, flip(): lax.ppermute(values, 'dp', [(i, i ^ 1 << bit) for i in range(devices)])  93.7 us
    pallas_call x2, Pallas kernels, run_backward(): pl.pallas_call(functools.partial(backward_kernel, half), grid_spec=pltpu....  47.9 us
    ppermute x48, starting transfers between devices, flip(): lax.ppermute(values, 'dp', [(i, i ^ 1 << bit) for i in range(devices)])  43.3 us
    all_to_all x7, starting transfers between devices, exchange(): return lax.all_to_all(values, 'dp', split_axis=0, concat_axis=0, tiled=True)  37.4 us
    pallas_call x2, Pallas kernels, run_forward(): pl.pallas_call(functools.partial(forward_kernel, half), grid_spec=pltpu.P...  36.4 us
    dot_general x18, matrix products, dot_first(): lax.dot_general(left, right, (((0,), (0,)), ((), ())), preferred_element_...  35.1 us
    ppermute x21, starting transfers between devices, swap_cores(): return lax.ppermute(values, 'mp', [(0, 1), (1, 0)])  33.7 us
    pallas_call x2, Pallas kernels, run_scores(): pl.pallas_call(functools.partial(score_kernel, half), grid_spec=pltpu.Pre...  30 us
  transfers between devices with their start and end apart: 77, of which 35 were waited for; matrix products, arithmetic and copies ran while one was open for 24% of the time, Pallas kernels for 18%

profile of v4, /device:TPU:1, one launch (start us, length us, event | category | flops | bytes accessed | tf_op | source)
XLA Modules:
  0.0 537.8 jit_solution(353588917111902989)
XLA Ops:
  28.5 7.4 %all-to-all-start.3 = ((s32[16,1,130]{2,1,0:T(1,128)}), s32[16,1,130]{2,1,0:T(1,128)S(1)}, u32[]{:S(2)}, u32[]{:S(2)}) async-start(s32[16,1,130]{2,1,0:T(1,128)} %copy.310), calls=%async_computation.3 | async-start | bytes 32768 | tf_op jit(solution)/shard_map/all_to_all | solution.py:419
  37.0 5.1 all-to-all-done.3
  46.3 4.5 all-to-all-start.4
  91.8 18.3 %forward.2 = (bf16[8,32,512]{2,1,0:T(8,128)(2,1)}, bf16[8,32,512]{2,1,0:T(8,128)(2,1)}, bf16[8,32,1024]{2,1,0:T(8,128)(2,1)}, f32[2,8,32,512]{3,2,1,0:T(8,128)},...) custom-call(s32[1]{0:T(128)} %bitcast.103.mp_ref, ...), custom_call_target="tpu_custom_call" | custom-call | bytes 64800000 | tf_op jit(solution)/shard_map/forward/pallas_call | solution.py:568
  111.9 6.9 %all-to-all-start.5 = ((bf16[16,2,1024]{2,1,0:T(2,128)(2,1)}), bf16[16,2,1024]{2,1,0:T(2,128)(2,1)S(1)}, u32[]{:S(2)}, u32[]{:S(2)}) async-start(bf16[16,2,1024]{2,1,0:T(2,128)(2,1)} %reshape.1787), calls=%async_computation.5 | async-start | bytes 131072 | tf_op jit(solution)/shard_map/all_to_all | solution.py:419
  134.9 18.1 %forward.3 = (bf16[8,32,512]{2,1,0:T(8,128)(2,1)}, bf16[8,32,512]{2,1,0:T(8,128)(2,1)}, bf16[8,32,1024]{2,1,0:T(8,128)(2,1)}, f32[2,8,32,512]{3,2,1,0:T(8,128)},...) custom-call(s32[1]{0:T(128)} %bitcast.103.mp_ref, ...), custom_call_target="tpu_custom_call" | custom-call | bytes 64800000 | tf_op jit(solution)/shard_map/forward/pallas_call | solution.py:568
  164.8 14.9 %scores.2 = (bf16[256,3328]{1,0:T(8,128)(2,1)}, f32[256,512]{1,0:T(8,128)}, f32[256,512]{1,0:T(8,128)}, f32[2,8,128]{2,1,0:T(8,128)}) custom-call(s32[1]{0:T(128)} %bitcast.103.mp_ref, f32[1]{0:T(128)} %bitcast.139.inv_ref, bf16[256,512]{1,0:T(8,128)(2,1)} %bitcast.828, bf16[256,512]{1,0:T(8,128)(2,1)} %bitcast.853, ...), custom_call_target="tpu_custom_call" | custom-call | bytes 79200000 | tf_op jit(solution)/shard_map/scores/pallas_call | solution.py:816
  180.7 15.1 %scores.3 = (bf16[256,3328]{1,0:T(8,128)(2,1)}, f32[256,512]{1,0:T(8,128)}, f32[256,512]{1,0:T(8,128)}, f32[2,8,128]{2,1,0:T(8,128)}) custom-call(s32[1]{0:T(128)} %bitcast.103.mp_ref, f32[1]{0:T(128)} %bitcast.139.inv_ref, bf16[256,512]{1,0:T(8,128)(2,1)} %bitcast.830, bf16[256,512]{1,0:T(8,128)(2,1)} %bitcast.855, ...), custom_call_target="tpu_custom_call" | custom-call | bytes 79200000 | tf_op jit(solution)/shard_map/scores/pallas_call | solution.py:816
  211.8 23.9 %backward.2 = (bf16[4,8,32,512]{3,2,1,0:T(8,128)(2,1)}, bf16[4,8,32,512]{3,2,1,0:T(8,128)(2,1)}, bf16[256,512]{1,0:T(8,128)(2,1)}, bf16[256,512]{1,0:T(8,128)(2,1)}, f32[2,32,512]{2,1,0:T(8,128)}) custom-call(s32[1]{0:T(128)} %bitcast.103.mp_ref, f32[2,8,32,128]{3,2,1,0:T(8,128)} %broadcast_in_dim.484.code_ref, f32[8,32,512]{2,1,0:T(8,128)} %bitcast.836, ...), custom_call_target="tpu_custom_call" | custom-call | bytes 82800000 | tf_op jit(solution)/shard_map/backward/pallas_call | solution.py:683
  239.2 5.8 %all-to-all-start.7 = ((bf16[16,2,1024]{2,1,0:T(2,128)(2,1)}), bf16[16,2,1024]{2,1,0:T(2,128)(2,1)S(1)}, u32[]{:S(2)}, u32[]{:S(2)}) async-start(bf16[16,2,1024]{2,1,0:T(2,128)(2,1)} %reshape.1812), calls=%async_computation.7 | async-start | bytes 131072 | tf_op jit(solution)/shard_map/all_to_all | solution.py:419
  264.2 24.0 %backward.3 = (bf16[4,8,32,512]{3,2,1,0:T(8,128)(2,1)}, bf16[4,8,32,512]{3,2,1,0:T(8,128)(2,1)}, bf16[256,512]{1,0:T(8,128)(2,1)}, bf16[256,512]{1,0:T(8,128)(2,1)}, f32[2,32,512]{2,1,0:T(8,128)}) custom-call(s32[1]{0:T(128)} %bitcast.103.mp_ref, f32[2,8,32,128]{3,2,1,0:T(8,128)} %broadcast_in_dim.484.code_ref, f32[8,32,512]{2,1,0:T(8,128)} %bitcast.834, ...), custom_call_target="tpu_custom_call" | custom-call | bytes 82800000 | tf_op jit(solution)/shard_map/backward/pallas_call | solution.py:683
  342.4 4.4 collective-permute-start.66
  354.2 5.4 %collective-permute-done.27 = bf16[256,512]{1,0:T(8,128)(2,1)S(1)} collective-permute-done((bf16[256,512]{1,0:T(8,128)(2,1)S(1)}, bf16[256,512]{1,0:T(8,128)(2,1)S(1)}, u32[]{:S(2)}, u32[]{:S(2)}) %collective-permute-start.27) | collective-permute-done | bytes 262176 | tf_op jit(solution)/shard_map/ppermute | solution.py:908
  383.7 5.2 collective-permute-done.56
  396.3 7.7 %collective-permute-done.41 = bf16[64,512]{1,0:T(8,128)(2,1)S(1)} collective-permute-done((bf16[64,512]{1,0:T(8,128)(2,1)S(1)}, bf16[64,512]{1,0:T(8,128)(2,1)S(1)}, u32[]{:S(2)}, u32[]{:S(2)}) %collective-permute-start.41) | collective-permute-done | bytes 65568 | tf_op jit(solution)/shard_map/ppermute | solution.py:908
  412.7 6.9 %collective-permute-done.42 = bf16[64,1024]{1,0:T(8,128)(2,1)S(1)} collective-permute-done((bf16[64,1024]{1,0:T(8,128)(2,1)S(1)}, bf16[64,1024]{1,0:T(8,128)(2,1)S(1)}, u32[]{:S(2)}, u32[]{:S(2)}) %collective-permute-start.42) | collective-permute-done | bytes 131104 | tf_op jit(solution)/shard_map/ppermute | solution.py:908
  430.4 4.7 collective-permute-done.31
  442.4 9.1 %collective-permute-start.69 = (f32[1176]{0:T(1024)S(1)}, f32[1176]{0:T(1024)S(1)}, u32[]{:S(2)}, u32[]{:S(2)}) collective-permute-start(f32[1176]{0:T(1024)S(1)} %slice_reduce_fusion.2), channel_id=1, source_target_pairs={{0,1},{1,0},{2,3},{3,2},{4,5},{5,4},{6,7},{7,6},{8,9},{9,8},{10,11... | collective-permute-start | bytes 14120 | tf_op jit(solution)/shard_map/ppermute | solution.py:415
  456.2 8.3 %collective-permute-done.52 = bf16[256,512]{1,0:T(8,128)(2,1)S(1)} collective-permute-done((bf16[256,512]{1,0:T(8,128)(2,1)}, bf16[256,512]{1,0:T(8,128)(2,1)S(1)}, u32[]{:S(2)}, u32[]{:S(2)}) %collective-permute-start.52) | collective-permute-done | bytes 262176 | tf_op jit(solution)/shard_map/ppermute | solution.py:908
  477.0 22.4 %collective-permute-done.45 = bf16[512,1024]{1,0:T(8,128)(2,1)S(1)} collective-permute-done((bf16[512,1024]{1,0:T(8,128)(2,1)S(1)}, bf16[512,1024]{1,0:T(8,128)(2,1)S(1)}, u32[]{:S(2)}, u32[]{:S(2)}) %collective-permute-start.45) | collective-permute-done | bytes 1048608 | tf_op jit(solution)/shard_map/ppermute | solution.py:908
  502.7 4.4 collective-permute-start.64
  507.1 4.5 fusion.193
  515.0 9.7 %conditional.1 = (f32[64,500]{1,0:T(8,128)}, f32[64,500]{1,0:T(8,128)}, f32[]{:T(128)}, f32[]{:T(128)}, f32[]{:T(128)}, /*index=5*/f32[]{:T(128)}, f32[1176,500]...) conditional(s32[]{:T(128)} %convert_element_type.991, ...), branch_computations={%region_26.103_spmd, %region_100.104_spmd} | conditional | flops 30975397888 | bytes 1957420800 | solution.py:1338
  516.9 7.8 %unpad.1 = (f32[3,1000,500]{2,1,0:T(8,128)}, f32[3,1000,500]{2,1,0:T(8,128)}) custom-call(s32[6]{0:T(128)} %get-tuple-element.799.sides_ref, bf16[512,1024]{1,0:T(8,128)(2,1)} %get-tuple-element.800.refs_0_, bf16[512,1024]{1,0:T(8,128)(2,1)} %get-tuple-element.801.refs_1_, bf16[512,1024]{1,0:T(8,128)(2,1)} %get-tuple-element.802.refs_2_, ...), custom_call_target="tpu_custom_call" | custom-call | bytes 28800000 | tf_op jit(solution)/shard_map/cond/branch_1_fun/unpad/pallas_call | solution.py:881
  (578 shorter events, 269.0 us)
Async XLA Ops:
  7.2 121.9 %all-gather.24.cloned.1.call-start = ((), (), s32[]{:S(2)}) async-start(), calls=%async_computation.16 | async-start | bytes 6127616 | tf_op jit(solution)/shard_map/all_gather | solution.py:1035
  46.3 37.4 %all-to-all-start.4 = ((bf16[16,64,512]{2,1,0:T(8,128)(2,1)}), bf16[16,64,512]{2,1,0:T(8,128)(2,1)}, u32[]{:S(2)}, u32[]{:S(2)}) async-start(bf16[16,64,512]{2,1,0:T(8,128)(2,1)} %bitcast.824), calls=%async_computation.4 | async-start | bytes 2097152 | tf_op jit(solution)/shard_map/all_to_all | solution.py:419
  57.8 33.2 %collective-permute-start.3 = (bf16[3,2,512,512]{3,2,1,0:T(8,128)(2,1)S(1)}, bf16[3,2,512,512]{3,2,1,0:T(8,128)(2,1)}, u32[]{:S(2)}, u32[]{:S(2)}) collective-permute-start(bf16[3,2,512,512]{3,2,1,0:T(8,128)(2,1)S(1)} %pad_maximum_fusion.4.wi_own), channel_id=1, source_target_pairs={{0,1},{1,0},{2,3},{3,2},{4,5},{5,4},{6,7},{7,6},{8,9},{9,8},{10,11... | collective-permute-start | bytes 9437192 | tf_op jit(solution)/shard_map/ppermute | solution.py:415
  129.1 23.9 %collective-permute-start.7 = (bf16[5632,512]{1,0:T(8,128)(2,1)}, bf16[5632,512]{1,0:T(8,128)(2,1)}, u32[]{:S(2)}, u32[]{:S(2)}) collective-permute-start(bf16[5632,512]{1,0:T(8,128)(2,1)} %all-gather.24.cloned.1.call-done), channel_id=1, source_target_pairs={{0,1},{1,0},{2,3},{3,2},{4,5},{5,4},{6,7},{7,6},{8,9},{9,8},{10,11... | collective-permute-start | bytes 17301512 | tf_op jit(solution)/shard_map/ppermute | solution.py:415
  129.5 26.8 %all-to-all-start.6 = ((bf16[16,64,512]{2,1,0:T(8,128)(2,1)}), bf16[16,64,512]{2,1,0:T(8,128)(2,1)S(1)}, u32[]{:S(2)}, u32[]{:S(2)}) async-start(bf16[16,64,512]{2,1,0:T(8,128)(2,1)} %bitcast.137), calls=%async_computation.6 | async-start | bytes 2097152 | tf_op jit(solution)/shard_map/all_to_all | solution.py:419
  206.9 49.8 %collective-permute-start.15 = (bf16[2,2,2,2,80,512]{5,4,2,1,0,3:T(8,128)(2,1)}, bf16[2,2,2,2,80,512]{5,4,2,1,0,3:T(8,128)(2,1)}, u32[]{:S(2)}, u32[]{:S(2)}) collective-permute-start(bf16[2,2,2,2,80,512]{5,4,2,1,0,3:T(8,128)(2,1)} %dynamic-slice_bitcast_fusion.7), channel_id=1, source_target_pairs={{0,4},{2,6},{4,0},{6,2},{8,12},{10,14},{12,8},{14,10},{16,20},{18,... | collective-permute-start | bytes 3932168 | tf_op jit(solution)/shard_map/ppermute | solution.py:908
  209.9 50.3 %collective-permute-start.14 = (bf16[2,2,2,2,96,512]{5,4,2,1,0,3:T(8,128)(2,1)}, bf16[2,2,2,2,96,512]{5,4,2,1,0,3:T(8,128)(2,1)}, u32[]{:S(2)}, u32[]{:S(2)}) collective-permute-start(bf16[2,2,2,2,96,512]{5,4,2,1,0,3:T(8,128)(2,1)} %dynamic-slice_bitcast_fusion.6), channel_id=1, source_target_pairs={{0,2},{2,0},{4,6},{6,4},{8,10},{10,8},{12,14},{14,12},{16,18},{18,... | collective-permute-start | bytes 4718600 | tf_op jit(solution)/shard_map/ppermute | solution.py:908
  237.6 65.1 %collective-permute-start.17 = (bf16[4,8,32,512]{3,2,1,0:T(8,128)(2,1)}, bf16[4,8,32,512]{3,2,1,0:T(8,128)(2,1)}, u32[]{:S(2)}, u32[]{:S(2)}) collective-permute-start(bf16[4,8,32,512]{3,2,1,0:T(8,128)(2,1)} %get-tuple-element.960), channel_id=1, source_target_pairs={{0,1},{1,0},{2,3},{3,2},{4,5},{5,4},{6,7},{7,6},{8,9},{9,8},{10,11... | collective-permute-start | bytes 3145736 | tf_op jit(solution)/shard_map/ppermute | solution.py:415
  251.4 55.4 %all-to-all-start.8 = ((bf16[16,64,512]{2,1,0:T(8,128)(2,1)}), bf16[16,64,512]{2,1,0:T(8,128)(2,1)}, u32[]{:S(2)}, u32[]{:S(2)}) async-start(bf16[16,64,512]{2,1,0:T(8,128)(2,1)} %bitcast.823), calls=%async_computation.8 | async-start | bytes 2097152 | tf_op jit(solution)/shard_map/all_to_all | solution.py:419
  290.1 22.4 %collective-permute-start.6 = (bf16[512,1024]{1,0:T(8,128)(2,1)S(1)}, bf16[512,1024]{1,0:T(8,128)(2,1)}, u32[]{:S(2)}, u32[]{:S(2)}) collective-permute-start(bf16[512,1024]{1,0:T(8,128)(2,1)S(1)} %pad_maximum_fusion.10), channel_id=1, source_target_pairs={{0,1},{1,0},{2,3},{3,2},{4,5},{5,4},{6,7},{7,6},{8,9},{9,8},{10,11... | collective-permute-start | bytes 3145736 | tf_op jit(solution)/shard_map/ppermute | solution.py:415
  298.9 28.6 %collective-permute-start.22 = (bf16[2,2,2,80,512]{4,3,1,0,2:T(8,128)(2,1)}, bf16[2,2,2,80,512]{4,3,1,0,2:T(8,128)(2,1)}, u32[]{:S(2)}, u32[]{:S(2)}) collective-permute-start(bf16[2,2,2,80,512]{4,3,1,0,2:T(8,128)(2,1)} %dynamic-slice_bitcast_fusion.9), channel_id=1, source_target_pairs={{0,2},{2,0},{4,6},{6,4},{8,10},{10,8},{12,14},{14,12},{16,18},{18,... | collective-permute-start | bytes 1966088 | tf_op jit(solution)/shard_map/ppermute | solution.py:908
  300.4 24.5 %collective-permute-start.20 = (bf16[2,2,2,96,512]{4,3,1,0,2:T(8,128)(2,1)}, bf16[2,2,2,96,512]{4,3,1,0,2:T(8,128)(2,1)}, u32[]{:S(2)}, u32[]{:S(2)}) collective-permute-start(bf16[2,2,2,96,512]{4,3,1,0,2:T(8,128)(2,1)} %dynamic-slice_bitcast_fusion.8), channel_id=1, source_target_pairs={{0,4},{2,6},{4,0},{6,2},{8,12},{10,14},{12,8},{14,10},{16,20},{18,... | collective-permute-start | bytes 2359304 | tf_op jit(solution)/shard_map/ppermute | solution.py:908
  315.0 23.7 %collective-permute-start.26 = (bf16[512,512]{1,0:T(8,128)(2,1)S(1)}, bf16[512,512]{1,0:T(8,128)(2,1)S(1)}, u32[]{:S(2)}, u32[]{:S(2)}) collective-permute-start(bf16[512,512]{1,0:T(8,128)(2,1)S(1)} %constant_dynamic-slice_fusion.30), channel_id=1, source_target_pairs={{0,2},{2,0},{4,6},{6,4},{8,10},{10,8},{12,14},{14,12},{16,18},{18,... | collective-permute-start | bytes 1572872 | tf_op jit(solution)/shard_map/ppermute | solution.py:908
  339.1 22.3 %collective-permute-start.21 = (bf16[2,2,96,512]{3,2,0,1:T(8,128)(2,1)S(1)}, bf16[2,2,96,512]{3,2,0,1:T(8,128)(2,1)S(1)}, u32[]{:S(2)}, u32[]{:S(2)}) collective-permute-start(bf16[2,2,96,512]{3,2,0,1:T(8,128)(2,1)S(1)} %dynamic-slice_bitcast_fusion.10), channel_id=1, source_target_pairs={{0,8},{2,10},{4,12},{6,14},{8,0},{10,2},{12,4},{14,6},{16,24},{18,... | collective-permute-start | bytes 1179656 | tf_op jit(solution)/shard_map/ppermute | solution.py:908
  342.4 128.2 %collective-permute-start.66 = (f32[32,512]{1,0:T(8,128)}, f32[32,512]{1,0:T(8,128)}, u32[]{:S(2)}, u32[]{:S(2)}) collective-permute-start(f32[32,512]{1,0:T(8,128)} %get-tuple-element.1932), channel_id=1, source_target_pairs={{0,1},{1,0},{2,3},{3,2},{4,5},{5,4},{6,7},{7,6},{8,9},{9,8},{10,11... | collective-permute-start | bytes 196616 | tf_op jit(solution)/shard_map/ppermute | solution.py:415
  380.5 29.5 %collective-permute-start.67 = (bf16[2,96,512]{2,1,0:T(8,128)(2,1)S(1)}, bf16[2,96,512]{2,1,0:T(8,128)(2,1)S(1)}, u32[]{:S(2)}, u32[]{:S(2)}) collective-permute-start(bf16[2,96,512]{2,1,0:T(8,128)(2,1)S(1)} %dynamic-slice_bitcast_fusion.12), channel_id=1, source_target_pairs={{0,16},{2,18},{4,20},{6,22},{8,24},{10,26},{12,28},{14,30},{16,0},... | collective-permute-start | bytes 589832 | tf_op jit(solution)/shard_map/ppermute | solution.py:908
  426.7 27.6 %collective-permute-start.44 = (bf16[256,1024]{1,0:T(8,128)(2,1)S(1)}, bf16[256,1024]{1,0:T(8,128)(2,1)}, u32[]{:S(2)}, u32[]{:S(2)}) collective-permute-start(bf16[256,1024]{1,0:T(8,128)(2,1)S(1)} %maximum_select_fusion.3), channel_id=1, source_target_pairs={{0,2},{2,0},{4,6},{6,4},{8,10},{10,8},{12,14},{14,12},{16,18},{18,... | collective-permute-start | bytes 1572872 | tf_op jit(solution)/shard_map/ppermute | solution.py:908
  430.2 21.4 %collective-permute-start.60 = (bf16[256,512]{1,0:T(8,128)(2,1)}, bf16[256,512]{1,0:T(8,128)(2,1)}, u32[]{:S(2)}, u32[]{:S(2)}) collective-permute-start(bf16[256,512]{1,0:T(8,128)(2,1)} %maximum_select_fusion.9), channel_id=1, source_target_pairs={{0,2},{2,0},{4,6},{6,4},{8,10},{10,8},{12,14},{14,12},{16,18},{18,... | collective-permute-start | bytes 786440 | tf_op jit(solution)/shard_map/ppermute | solution.py:908
  435.2 32.5 %collective-permute-start.32 = (bf16[256,1024]{1,0:T(8,128)(2,1)S(1)}, bf16[256,1024]{1,0:T(8,128)(2,1)}, u32[]{:S(2)}, u32[]{:S(2)}) collective-permute-start(bf16[256,1024]{1,0:T(8,128)(2,1)S(1)} %maximum_select_fusion.2), channel_id=1, source_target_pairs={{0,4},{2,6},{4,0},{6,2},{8,12},{10,14},{12,8},{14,10},{16,20},{18,... | collective-permute-start | bytes 1572872 | tf_op jit(solution)/shard_map/ppermute | solution.py:908
  437.7 64.2 %all-to-all-start.9 = ((bf16[16,64,512]{2,1,0:T(8,128)(2,1)}), bf16[16,64,512]{2,1,0:T(8,128)(2,1)}, u32[]{:S(2)}, u32[]{:S(2)}) async-start(bf16[16,64,512]{2,1,0:T(8,128)(2,1)} %add_convert_fusion.2), calls=%async_computation.9 | async-start | bytes 2097152 | tf_op jit(solution)/shard_map/all_to_all | solution.py:419
  442.4 30.1 %collective-permute-start.69 = (f32[1176]{0:T(1024)S(1)}, f32[1176]{0:T(1024)S(1)}, u32[]{:S(2)}, u32[]{:S(2)}) collective-permute-start(f32[1176]{0:T(1024)S(1)} %slice_reduce_fusion.2), channel_id=1, source_target_pairs={{0,1},{1,0},{2,3},{3,2},{4,5},{5,4},{6,7},{7,6},{8,9},{9,8},{10,11... | collective-permute-start | bytes 14120 | tf_op jit(solution)/shard_map/ppermute | solution.py:415
  454.4 22.6 %collective-permute-start.61 = (bf16[512,512]{1,0:T(8,128)(2,1)S(1)}, bf16[512,512]{1,0:T(8,128)(2,1)S(1)}, u32[]{:S(2)}, u32[]{:S(2)}) collective-permute-start(bf16[512,512]{1,0:T(8,128)(2,1)S(1)} %maximum_select_fusion.5), channel_id=1, source_target_pairs={{0,4},{2,6},{4,0},{6,2},{8,12},{10,14},{12,8},{14,10},{16,20},{18,... | collective-permute-start | bytes 1572872 | tf_op jit(solution)/shard_map/ppermute | solution.py:908
  464.4 35.0 %collective-permute-start.45 = (bf16[512,1024]{1,0:T(8,128)(2,1)S(1)}, bf16[512,1024]{1,0:T(8,128)(2,1)S(1)}, u32[]{:S(2)}, u32[]{:S(2)}) collective-permute-start(bf16[512,1024]{1,0:T(8,128)(2,1)S(1)} %maximum_select_fusion.1), channel_id=1, source_target_pairs={{0,4},{2,6},{4,0},{6,2},{8,12},{10,14},{12,8},{14,10},{16,20},{18,... | collective-permute-start | bytes 3145736 | tf_op jit(solution)/shard_map/ppermute | solution.py:908
  470.6 29.5 %collective-permute-start.33 = (bf16[512,1024]{1,0:T(8,128)(2,1)S(1)}, bf16[512,1024]{1,0:T(8,128)(2,1)S(1)}, u32[]{:S(2)}, u32[]{:S(2)}) collective-permute-start(bf16[512,1024]{1,0:T(8,128)(2,1)S(1)} %maximum_select_fusion), channel_id=1, source_target_pairs={{0,2},{2,0},{4,6},{6,4},{8,10},{10,8},{12,14},{14,12},{16,18},{18,... | collective-permute-start | bytes 3145736 | tf_op jit(solution)/shard_map/ppermute | solution.py:908
  (130 other events, 1531.6 us)
Sparse Core Ops, SparseCore 0:
  15.5 104.3 all-gather.23
